TPU v7x, 32 devices: a whole 2x2x4 slice. The times are simulated.
32 devices in a mesh: pipe: 2 (over y), expert: 16 (over z, x, core).
Axes of the slice: x: 2, y: 2, z: 4, core: 2. Of those that a mesh axis runs over, the one named last changes fastest.
Arguments:
- tokens: bfloat16 [2, 2048, 2048], P('pipe', 'expert'), may hold values from -6 to 6
- routes: int32 [2, 2048, 6], P('pipe', 'expert'), may hold values from 0 to 15, all different within a row; in each aligned block of 128 rows (0 to 127, 128 to 255, ..., all dimensions but the last counted through in order) at most 72 rows name the same one
- norm_gain: float32 [2, 2048], P('pipe'), may hold values from 0.1 to 1.9
- router_weight: bfloat16 [2, 2048, 16], P('pipe'), may hold values from -0.125 to 0.125
- w_gate: bfloat16 [2, 16, 2048, 768], P('pipe', 'expert'), may hold values from -0.125 to 0.125
- w_up: bfloat16 [2, 16, 2048, 768], P('pipe', 'expert'), may hold values from -0.125 to 0.125
- w_down: bfloat16 [2, 16, 768, 2048], P('pipe', 'expert'), may hold values from -0.21875 to 0.21875
Outputs:
- received: bfloat16 [2, 2048, 2048], P('pipe', 'expert')
Inputs may be any that keep to these rules, and one draw needn't show every extreme that they name: Within each aligned block of 128 tokens of a section (the tokens of one device), the 6 routes of a token name different experts and no expert is named by more than 72 routes; some expert is named by exactly 72 routes in some block; every expert is named somewhere.
All inputs are finite; a program needn't handle non-finite values.
Results may differ from a plain program's by a relative error of at most 0.0039.
Values may be sent and summed in bfloat16 or wider, within the bound.
No kernel may reach another device: no remote copies, remote signals or barrier semaphores. Data moves between devices by JAX's collectives and lax.ppermute only.
A program may use at most 128 MiB of HBM per device.

v0:
```python
import jax
import jax.numpy as jnp
from jax import lax
from jax.sharding import PartitionSpec as P


def shifted(shard, axis, by):
    devices = lax.axis_size(axis)
    return lax.ppermute(shard, axis, [(i, (i + by) % devices) for i in range(devices)])


def earlier_matrix(count):
    positions = jnp.arange(count, dtype=jnp.int32)
    return (positions[None, :] < positions[:, None]).astype(jnp.bfloat16)


def slot_ranks(route_block, experts):
    flat_routes = route_block.reshape(-1)
    hits = (flat_routes[:, None] == jnp.arange(experts, dtype=jnp.int32)[None, :]).astype(
        jnp.bfloat16
    )
    before = jnp.dot(earlier_matrix(flat_routes.shape[0]), hits, preferred_element_type=jnp.float32)
    ranks = jnp.sum(before * hits.astype(jnp.float32), axis=1).astype(jnp.int32)
    return ranks.reshape(route_block.shape)


def expert_ffn(slot_block, gate_matrix, up_matrix, down_matrix):
    gate_part = jnp.dot(slot_block, gate_matrix, preferred_element_type=jnp.float32)
    up_part = jnp.dot(slot_block, up_matrix, preferred_element_type=jnp.float32)
    hidden = (jax.nn.silu(gate_part) * up_part).astype(jnp.bfloat16)
    return jnp.dot(hidden, down_matrix, preferred_element_type=jnp.float32).astype(jnp.bfloat16)


def local(tokens, routes, norm_gain, router_weight, w_gate, w_up, w_down):
    local_rows = tokens[0]
    route_local = routes[0]
    gate_matrix = w_gate[0, 0]
    up_matrix = w_up[0, 0]
    down_matrix = w_down[0, 0]
    experts = lax.axis_size("expert")
    tok_dev, top_count = route_local.shape
    model_width = local_rows.shape[1]
    capacity = 3 * tok_dev * top_count // (2 * experts)
    wide_rows = local_rows.astype(jnp.float32)
    mean_square = jnp.mean(wide_rows * wide_rows, axis=-1, keepdims=True)
    normed = (wide_rows * lax.rsqrt(mean_square + 1e-06) * norm_gain[0]).astype(jnp.bfloat16)
    score = jax.nn.sigmoid(jnp.dot(normed, router_weight[0], preferred_element_type=jnp.float32))
    expert_ids = jnp.arange(experts, dtype=jnp.int32)
    chosen = route_local[..., None] == expert_ids[None, None, :]
    picked = jnp.sum(jnp.where(chosen, score[:, None, :], 0.0), axis=-1)
    gate_values = (picked / jnp.sum(picked, axis=1, keepdims=True)).astype(jnp.bfloat16)
    ranks = slot_ranks(route_local, experts)
    slots = route_local * capacity + ranks
    slot_hits = slots[..., None] == jnp.arange(experts * capacity, dtype=jnp.int32)[None, None, :]
    weights_map = jnp.sum(
        jnp.where(slot_hits, gate_values.astype(jnp.float32)[..., None], 0.0), axis=1
    ).astype(jnp.bfloat16)
    table = lax.all_gather(route_local, "expert", axis=0, tiled=True)
    gathered = lax.all_gather(normed, "expert", axis=0, tiled=True)
    own_index = lax.axis_index("expert")
    flat_count = tok_dev * top_count
    blocks = table.reshape(experts, flat_count)
    mine = blocks == own_index
    mine_values = mine.astype(jnp.bfloat16)
    own_ranks = jnp.dot(
        mine_values, earlier_matrix(flat_count).T, preferred_element_type=jnp.float32
    ).astype(jnp.int32)
    matches = mine[..., None] & (
        own_ranks[..., None] == jnp.arange(capacity, dtype=jnp.int32)[None, None, :]
    )
    selector = jnp.any(matches.reshape(experts, tok_dev, top_count, capacity), axis=2).astype(
        jnp.bfloat16
    )
    buffer = jnp.einsum(
        "btc,btd->bcd",
        selector,
        gathered.reshape(experts, tok_dev, model_width),
        preferred_element_type=jnp.float32,
    ).astype(jnp.bfloat16)
    owner_out = expert_ffn(buffer.reshape(-1, model_width), gate_matrix, up_matrix, down_matrix)
    returned = lax.all_to_all(
        owner_out.reshape(experts, capacity, model_width),
        "expert",
        split_axis=0,
        concat_axis=0,
        tiled=True,
    )
    moe = jnp.dot(
        weights_map,
        returned.reshape(experts * capacity, model_width),
        preferred_element_type=jnp.float32,
    )
    layer_out = (wide_rows + moe).astype(jnp.bfloat16)[None]
    received = shifted(layer_out, "pipe", 1)
    return received


def solution(mesh):
    return jax.shard_map(
        local,
        mesh=mesh,
        in_specs=(
            P("pipe", "expert", None),
            P("pipe", "expert", None),
            P("pipe", None),
            P("pipe", None, None),
            P("pipe", "expert", None, None),
            P("pipe", "expert", None, None),
            P("pipe", "expert", None, None),
        ),
        out_specs=P("pipe", "expert", None),
        check_vma=False,
    )
```

profile of v0, /device:TPU:10, one launch (start us, length us, event | category | flops | bytes accessed | tf_op | source)
XLA Modules:
  0.0 239.3 jit_solution(10218874851888454683)
XLA Ops:
  6.5 0.0 copy-start
  6.5 0.0 all-gather.3.cloned.1.call-start
  6.5 1.4 fusion.19
  7.9 0.0 copy-start.3
  7.9 0.6 copy-done.3
  8.5 2.1 fusion.21
  10.6 0.0 all-gather.3.cloned.1.call-update
  10.6 15.6 %all-gather = s32[1,2048,6]{1,0,2:T(1,128)S(1)} all-gather(s32[1,128,6]{1,0,2:T(1,128)} %param.8), channel_id=2, replica_groups=mesh['pipe'=2,'expert'=16] {'expert'}, dimensions={1}, use_global_device_ids=true | all-gather | bytes 52224 | tf_op jit(solution)/shard_map/all_gather | solution.py:58
  26.2 0.2 fusion.34
  26.4 0.5 copy.24
  26.9 0.7 eq.86
  27.5 1.0 fusion.14
  28.5 1.0 copy.25
  29.5 0.8 eq.87
  30.3 1.2 copy.26
  31.5 0.8 fusion.1
  32.3 53.0 %all-gather.3.cloned.1.call-done = bf16[2048,2048]{1,0:T(8,128)(2,1)} async-done(((bf16[128,2048]{1,0:T(8,128)(2,1)}), bf16[2048,2048]{1,0:T(8,128)(2,1)}) %all-gather.3.cloned.1.call-update) | async-done | bytes 8388624 | tf_op jit(solution)/shard_map/all_gather | solution.py:59
  85.4 0.0 copy-start.5
  85.4 4.9 %convolution_convert_fusion.1 = bf16[16,72,2048]{2,1,0:T(8,128)(2,1)S(1)} fusion(pred[16,128,72]{1,2,0:T(8,128)(4,1)S(1)} %fusion.1, bf16[16,128,2048]{2,1,0:T(8,128)(2,1)} %bitcast.54), kind=kOutput, calls=%fused_computation.2 | convolution fusion | flops 606339072 | bytes 13254656 | tf_op jit(solution)/shard_map/btc,btd->bcd/dot_general | solution.py:74
  90.3 0.0 copy-done.5
  90.3 0.0 copy-start.6
  90.3 3.9 %fusion.5 = f32[1152,768]{1,0:T(8,128)S(1)} fusion(bf16[1152,2048]{1,0:T(8,128)(2,1)S(1)} %bitcast.55, bf16[1,1,2048,768]{3,2,1,0:T(8,128)(2,1)S(1)} %copy-done.5), kind=kOutput, calls=%fused_computation.11 | convolution fusion | flops 3623878656 | bytes 11403264 | tf_op jit(solution)/shard_map/dot_general | solution.py:28
  94.2 0.0 copy-done.6
  94.2 4.2 %fusion.2 = bf16[1152,768]{1,0:T(8,128)(2,1)S(1)} fusion(bf16[1152,2048]{1,0:T(8,128)(2,1)S(1)} %bitcast.56, f32[1152,768]{1,0:T(8,128)S(1)} %fusion.5, bf16[1,1,2048,768]{3,2,1,0:T(8,128)(2,1)S(1)} %copy-done.6), kind=kOutput, calls=%fused_computation.8 | convolution fusion | flops 3629187072 | bytes 13172736 | tf_op jit(solution)/shard_map/dot_general | solution.py:29
  98.4 0.0 copy-done
  98.4 5.6 %convolution_convert_fusion = bf16[1152,2048]{1,0:T(8,128)(2,1)} fusion(bf16[1152,768]{1,0:T(8,128)(2,1)S(1)} %fusion.2, bf16[1,1,768,2048]{3,2,1,0:T(8,128)(2,1)S(1)} %copy-done), kind=kOutput, calls=%fused_computation | convolution fusion | flops 3626237952 | bytes 9633792 | tf_op jit(solution)/shard_map/dot_general | solution.py:31
  104.0 0.0 copy-start.1
  104.0 0.0 copy-start.2
  104.0 0.0 copy-start.4
  104.0 0.0 copy-start.7
  104.0 6.5 %all-to-all-start = ((bf16[16,72,2048]{2,1,0:T(8,128)(2,1)}), bf16[16,72,2048]{2,1,0:T(8,128)(2,1)}, u32[]{:S(2)}, u32[]{:S(2)}) async-start(bf16[16,72,2048]{2,1,0:T(8,128)(2,1)} %bitcast.57), calls=%async_computation | async-start | bytes 9437184 | tf_op jit(solution)/shard_map/all_to_all | solution.py:81
  110.6 0.0 copy-done.1
  110.6 0.1 copy.19
  110.7 0.1 eq.73
  110.8 0.3 fusion.15
  111.2 0.1 convert_element_type.75
  111.3 0.1 copy.21
  111.4 0.0 copy-done.2
  111.4 0.0 copy-done.4
  111.4 0.0 copy-done.7
  111.4 1.4 fusion.18
  112.8 0.1 select_reduce_fusion.1
  112.9 0.5 select_reduce_fusion
  113.4 100.8 %all-to-all-done = bf16[16,72,2048]{2,1,0:T(8,128)(2,1)} async-done(((bf16[16,72,2048]{2,1,0:T(8,128)(2,1)}), bf16[16,72,2048]{2,1,0:T(8,128)(2,1)}, u32[]{:S(2)}, u32[]{:S(2)}) %all-to-all-start) | async-done | bytes 4718624 | tf_op jit(solution)/shard_map/all_to_all | solution.py:81
  214.1 3.3 %fusion.10 = bf16[1,128,2048]{2,1,0:T(8,128)(2,1)S(1)} fusion(bf16[1152,2048]{1,0:T(8,128)(2,1)} %bitcast.12, bf16[1,128,2048]{2,1,0:T(8,128)(2,1)} %param.7, bf16[128,1152]{1,0:T(8,128)(2,1)S(1)} %select_reduce_fusion), kind=kOutput, calls=%fused_computation.18 | convolution fusion | flops 604766208 | bytes 6062080 | tf_op jit(solution)/shard_map/dot_general | solution.py:88
  217.4 1.5 collective-permute-start
  219.0 12.7 %collective-permute-done = bf16[1,128,2048]{2,1,0:T(8,128)(2,1)S(1)} collective-permute-done((bf16[1,128,2048]{2,1,0:T(8,128)(2,1)S(1)}, bf16[1,128,2048]{2,1,0:T(8,128)(2,1)S(1)}, u32[]{:S(2)}, u32[]{:S(2)}) %collective-permute-start) | collective-permute-done | bytes 524320 | tf_op jit(solution)/shard_map/ppermute | solution.py:9
  231.6 0.8 copy.31
  (5 shorter events, 0.0 us)
Async XLA Ops:
  6.5 91.9 %copy-start = (bf16[1,1,768,2048]{3,2,1,0:T(8,128)(2,1)S(1)}, bf16[1,1,768,2048]{3,2,1,0:T(8,128)(2,1)}, u32[]{:S(2)}) copy-start(bf16[1,1,768,2048]{3,2,1,0:T(8,128)(2,1)} %param.13) | copy-start | bytes 9437188
  6.5 78.8 %all-gather.3.cloned.1.call-start = ((), (), s32[]{:S(2)}) async-start(), calls=%async_computation.1 | async-start | bytes 8912896 | tf_op jit(solution)/shard_map/all_gather | solution.py:59
  7.9 0.6 copy-start.3
  85.4 4.9 %copy-start.5 = (bf16[1,1,2048,768]{3,2,1,0:T(8,128)(2,1)S(1)}, bf16[1,1,2048,768]{3,2,1,0:T(8,128)(2,1)}, u32[]{:S(2)}) copy-start(bf16[1,1,2048,768]{3,2,1,0:T(8,128)(2,1)} %param.11) | copy-start | bytes 9437188
  90.3 3.9 %copy-start.6 = (bf16[1,1,2048,768]{3,2,1,0:T(8,128)(2,1)S(1)}, bf16[1,1,2048,768]{3,2,1,0:T(8,128)(2,1)}, u32[]{:S(2)}) copy-start(bf16[1,1,2048,768]{3,2,1,0:T(8,128)(2,1)} %param.12) | copy-start | bytes 9437188
  104.0 6.5 %copy-start.1 = (s32[1,128,6]{1,0,2:T(1,128)S(1)}, s32[1,128,6]{1,0,2:T(1,128)}, u32[]{:S(2)}) copy-start(s32[1,128,6]{1,0,2:T(1,128)} %param.8) | copy-start | bytes 9220
  104.0 7.4 %copy-start.2 = (f32[1,2048]{1,0:T(1,128)S(1)}, f32[1,2048]{1,0:T(1,128)}, u32[]{:S(2)}) copy-start(f32[1,2048]{1,0:T(1,128)} %param.9) | copy-start | bytes 24580
  104.0 7.4 %copy-start.4 = (f32[128]{0:T(128)S(1)}, f32[128]{0:T(128)}, u32[]{:S(2)}) copy-start(f32[128]{0:T(128)} %copy-done.3) | copy-start | bytes 1540
  104.0 7.4 %copy-start.7 = (bf16[1,2048,16]{1,2,0:T(8,128)(2,1)S(1)}, bf16[1,2048,16]{1,2,0:T(8,128)(2,1)}, u32[]{:S(2)}) copy-start(bf16[1,2048,16]{1,2,0:T(8,128)(2,1)} %param.10) | copy-start | bytes 196612
  104.0 110.1 %all-to-all-start = ((bf16[16,72,2048]{2,1,0:T(8,128)(2,1)}), bf16[16,72,2048]{2,1,0:T(8,128)(2,1)}, u32[]{:S(2)}, u32[]{:S(2)}) async-start(bf16[16,72,2048]{2,1,0:T(8,128)(2,1)} %bitcast.57), calls=%async_computation | async-start | bytes 9437184 | tf_op jit(solution)/shard_map/all_to_all | solution.py:81
  217.4 14.2 %collective-permute-start = (bf16[1,128,2048]{2,1,0:T(8,128)(2,1)S(1)}, bf16[1,128,2048]{2,1,0:T(8,128)(2,1)S(1)}, u32[]{:S(2)}, u32[]{:S(2)}) collective-permute-start(bf16[1,128,2048]{2,1,0:T(8,128)(2,1)S(1)} %fusion.10), channel_id=1, source_target_pairs={{0,16},{16,0},{1,17},{17,1},{2,18},{18,2},{3,19},{19,3},{4,20},{20... | collective-permute-start | bytes 1572872 | tf_op jit(solution)/shard_map/ppermute | solution.py:9
Sparse Core Ops, SparseCore 0:
  10.7 74.6 all-gather.2
where the time goes:
time: 240 us; the launch traced here: 239 us
  waiting for transfers between devices  166 us (69%)
  matrix products  24.6 us (10%)
  blocking collectives  15.6 us (6%)
  between operations  13.6 us (6%)
  starting transfers between devices  8.04 us (3%)
  local copies, waits for them, and re-layouts  5.99 us (2%)
  other arithmetic  5.01 us (2%)
    all_to_all x1, waiting for transfers between devices, local(): lax.all_to_all(owner_out.reshape(experts, capacity, model_width), 'expert...  101 us
    all_gather x1, waiting for transfers between devices, local(): gathered = lax.all_gather(normed, 'expert', axis=0, tiled=True)  53 us
    all_gather x1, blocking collectives, local(): table = lax.all_gather(route_local, 'expert', axis=0, tiled=True)  15.6 us
    ppermute x1, waiting for transfers between devices, shifted(): lax.ppermute(shard, axis, [(i, (i + by) % devices) for i in range(devices)])  12.7 us
    all_to_all x1, starting transfers between devices, local(): lax.all_to_all(owner_out.reshape(experts, capacity, model_width), 'expert...  6.51 us
    dot_general x1, matrix products, expert_ffn(): jnp.dot(hidden, down_matrix, preferred_element_type=jnp.float32)  5.58 us
    dot_general x1, matrix products, local(): jnp.einsum('btc,btd->bcd', selector, gathered.reshape(experts, tok_dev, m...  4.9 us
  transfers between devices with their start and end apart: 3, of which 3 were waited for; matrix products, arithmetic and copies ran while one was open for 4% of the time, Pallas kernels for 0%

commit v1 on v0

v1 whole, which is shorter than its diff:
```python
import jax
import jax.numpy as jnp
from jax import lax
from jax.sharding import PartitionSpec as P


def ring_chips(devices):
    depth = devices // 4
    return [2 * z for z in range(depth)] + [2 * z + 1 for z in reversed(range(depth))]


def ring_pairs(devices, by):
    chips = ring_chips(devices)
    count = len(chips)
    return [
        (2 * chip + core, 2 * chips[(place + by) % count] + core)
        for place, chip in enumerate(chips)
        for core in range(2)
    ]


def round_ring(shard, by):
    return lax.ppermute(shard, "expert", ring_pairs(lax.axis_size("expert"), by))


def across_cores(shard):
    devices = lax.axis_size("expert")
    return lax.ppermute(shard, "expert", [(i, i ^ 1) for i in range(devices)])


def next_section(shard):
    sections = lax.axis_size("pipe")
    return lax.ppermute(shard, "pipe", [(i, (i + 1) % sections) for i in range(sections)])


def gate_table(normed, router, route_local, experts):
    score = jax.nn.sigmoid(jnp.dot(normed, router, preferred_element_type=jnp.float32))
    expert_ids = jnp.arange(experts, dtype=jnp.int32)
    chosen = route_local[..., None] == expert_ids
    picked = jnp.sum(jnp.where(chosen, score[:, None, :], 0.0), axis=-1)
    gate_values = (picked / jnp.sum(picked, axis=1, keepdims=True)).astype(jnp.bfloat16)
    named = jnp.any(chosen, axis=1)
    table = jnp.sum(jnp.where(chosen, gate_values.astype(jnp.float32)[..., None], 0.0), axis=1)
    return jnp.where(named, table, -1.0).astype(jnp.bfloat16).T


def gather_tables(table, chips):
    tables = table[None]
    while tables.shape[0] < chips:
        have = tables.shape[0]
        more = min(have, chips - have)
        tables = jnp.concatenate([tables, round_ring(tables[:more], have)], axis=0)
    return tables


def local(tokens, routes, norm_gain, router_weight, w_gate, w_up, w_down):
    rows = tokens[0]
    route_local = routes[0]
    devices = lax.axis_size("expert")
    chips = devices // 2
    half = chips // 2
    tok_dev, top_count = route_local.shape
    cut = tok_dev // 2
    capacity = 3 * tok_dev * top_count // (2 * devices)
    pair_slots = -(-2 * capacity // 16) * 16
    device = lax.axis_index("expert")
    core = device % 2

    wide_rows = rows.astype(jnp.float32)
    mean_square = jnp.mean(wide_rows * wide_rows, axis=-1, keepdims=True)
    normed = (wide_rows * lax.rsqrt(mean_square + 1e-06) * norm_gain[0]).astype(jnp.bfloat16)
    own = [normed[:cut], normed[cut:]]

    ahead, behind = {0: own}, {0: own}
    for step in range(1, half):
        ahead[step] = [round_ring(part, 1) for part in ahead[step - 1]]
        behind[step] = [round_ring(part, -1) for part in behind[step - 1]]
    far = [round_ring(ahead[half - 1][0], 1), round_ring(behind[half - 1][1], -1)]

    table = gate_table(normed, router_weight[0], route_local, devices)
    tables = gather_tables(table, chips)
    first = lax.dynamic_slice_in_dim(tables, device, 1, axis=1)[:, 0]
    second = lax.dynamic_slice_in_dim(tables, device + 1 - 2 * core, 1, axis=1)[:, 0]
    gates = jnp.stack([first, second], axis=1).astype(jnp.float32)
    named = gates >= 0
    positions = jnp.arange(tok_dev, dtype=jnp.int32)
    earlier = (positions[:, None] < positions[None, :]).astype(jnp.bfloat16)
    ranks = jnp.dot(
        named.astype(jnp.bfloat16).reshape(-1, tok_dev), earlier, preferred_element_type=jnp.float32
    ).astype(jnp.int32).reshape(named.shape)
    order = [[0, half]] + [[k, chips - k] for k in range(1, half)]
    pick = lambda values: jnp.stack(
        [jnp.concatenate([values[a], values[b]], axis=-1) for a, b in order]
    )
    offset = jnp.concatenate(
        [jnp.zeros((tok_dev,), jnp.int32), jnp.full((tok_dev,), capacity, jnp.int32)]
    )
    pair_named, pair_ranks, pair_gates = pick(named), pick(ranks) + offset, pick(gates)
    hits = pair_named[:, :, None, :] & (
        pair_ranks[:, :, None, :] == jnp.arange(pair_slots, dtype=jnp.int32)[:, None]
    )
    selector = hits.astype(jnp.bfloat16)
    weighted = jnp.where(hits, pair_gates[:, :, None, :], 0.0).astype(jnp.bfloat16)

    def pair_rows(k):
        if k == 0:
            return jnp.concatenate(own + far, axis=0)
        return jnp.concatenate(ahead[k] + behind[k], axis=0)

    def experts_out(k):
        block = pair_rows(k)
        taken = jnp.einsum("est,td->esd", selector[k], block, preferred_element_type=jnp.float32)
        taken = taken.astype(jnp.bfloat16)
        slot_rows = jnp.concatenate([taken[0], across_cores(taken[1])], axis=0)
        gate_part = jnp.dot(slot_rows, w_gate[0, 0], preferred_element_type=jnp.float32)
        up_part = jnp.dot(slot_rows, w_up[0, 0], preferred_element_type=jnp.float32)
        hidden = (jax.nn.silu(gate_part) * up_part).astype(jnp.bfloat16)
        out = jnp.dot(hidden, w_down[0, 0], preferred_element_type=jnp.float32).astype(jnp.bfloat16)
        return jnp.stack([out[:pair_slots], across_cores(out[pair_slots:])])

    outs = {k: experts_out(k) for k in list(range(1, half)) + [0]}

    def share(k, begin, count):
        return jnp.einsum(
            "est,esd->td",
            weighted[k][:, :, begin : begin + count],
            outs[k],
            preferred_element_type=jnp.float32,
        )

    bf16 = jnp.bfloat16
    up_low = round_ring(share(0, tok_dev, cut).astype(bf16), 1)
    down_high = round_ring(share(0, tok_dev + cut, cut).astype(bf16), -1)
    up_high = down_low = None
    for k in reversed(range(1, half)):
        before, after = share(k, 0, tok_dev), share(k, tok_dev, tok_dev)
        new_up_high = after[cut:] + (0.0 if up_high is None else up_high.astype(jnp.float32))
        new_down_low = before[:cut] + (0.0 if down_low is None else down_low.astype(jnp.float32))
        new_up_low = after[:cut] + up_low.astype(jnp.float32)
        new_down_high = before[cut:] + down_high.astype(jnp.float32)
        up_high = round_ring(new_up_high.astype(bf16), 1)
        down_low = round_ring(new_down_low.astype(bf16), -1)
        up_low = round_ring(new_up_low.astype(bf16), 1)
        down_high = round_ring(new_down_high.astype(bf16), -1)
    mine = wide_rows + share(0, 0, tok_dev)
    low = mine[:cut] + down_low.astype(jnp.float32) + up_low.astype(jnp.float32)
    high = mine[cut:] + up_high.astype(jnp.float32) + down_high.astype(jnp.float32)
    received = [next_section(low.astype(bf16)), next_section(high.astype(bf16))]
    return jnp.concatenate(received, axis=0)[None]


def solution(mesh):
    return jax.shard_map(
        local,
        mesh=mesh,
        in_specs=(
            P("pipe", "expert", None),
            P("pipe", "expert", None),
            P("pipe", None),
            P("pipe", None, None),
            P("pipe", "expert", None, None),
            P("pipe", "expert", None, None),
            P("pipe", "expert", None, None),
        ),
        out_specs=P("pipe", "expert", None),
        check_vma=False,
    )
```

time: 240 us -> 178 us (0.74)
  waiting for transfers between devices: 166 us -> 61.6 us
  matrix products: 24.6 us -> 54.8 us
  starting transfers between devices: 8.04 us -> 37.4 us
  blocking collectives: 15.6 us -> 0 us
  between operations: 13.6 us -> 0.52 us
  local copies, waits for them, and re-layouts: 5.99 us -> 16 us
    all_to_all x1 -> x0, waiting for transfers between devices: 101 us -> none  [local(): lax.all_to_all(owner_out.reshape(experts, capacity, model_width), 'expert...]
    all_gather x1 -> x0, waiting for transfers between devices: 53 us -> none  [local(): gathered = lax.all_gather(normed, 'expert', axis=0, tiled=True)]
    ppermute x1 -> x41, waiting for transfers between devices: 12.7 us -> 61.6 us  [the longest x31 53.4 us: round_ring(): lax.ppermute(shard, 'expert', ring_pairs(lax.axis_size('expert'), by))]
    ppermute x1 -> x41, starting transfers between devices: 1.52 us -> 37.4 us  [the longest x31 33.9 us: round_ring(): lax.ppermute(shard, 'expert', ring_pairs(lax.axis_size('expert'), by))]
    dot_general x8 -> x23, matrix products: 24.6 us -> 54.8 us  [the longest x4 23.8 us: experts_out(): jnp.dot(hidden, w_down[0, 0], preferred_element_type=jnp.float32)]
    all_gather x1 -> x0, blocking collectives: 15.6 us -> none  [local(): table = lax.all_gather(route_local, 'expert', axis=0, tiled=True)]
    another operation x0 -> x4, local copies, waits for them, and re-layouts: none -> 8.92 us  [experts_out(): return jnp.stack([out[:pair_slots], across_cores(out[pair_slots:])])]
    all_to_all x1 -> x0, starting transfers between devices: 6.51 us -> none  [local(): lax.all_to_all(owner_out.reshape(experts, capacity, model_width), 'expert...]
  transfers between devices with their start and end apart: 3 -> 41, of which waited for: 3 -> 22; matrix products, arithmetic and copies ran while one was open for 4% -> 40% of each run, Pallas kernels for 0% -> 0%
where the time goes in v1:
time: 178 us; the launch traced here: 175 us
  waiting for transfers between devices  61.6 us (35%)
  matrix products  54.8 us (31%)
  starting transfers between devices  37.4 us (21%)
  local copies, waits for them, and re-layouts  16 us (9%)
  other arithmetic  4.89 us (3%)
    ppermute x31, waiting for transfers between devices, round_ring(): lax.ppermute(shard, 'expert', ring_pairs(lax.axis_size('expert'), by))  53.4 us
    ppermute x31, starting transfers between devices, round_ring(): lax.ppermute(shard, 'expert', ring_pairs(lax.axis_size('expert'), by))  33.9 us
    dot_general x4, matrix products, experts_out(): jnp.dot(hidden, w_down[0, 0], preferred_element_type=jnp.float32)  23.8 us
    dot_general x4, matrix products, experts_out(): jnp.dot(slot_rows, w_gate[0, 0], preferred_element_type=jnp.float32)  12.3 us
    dot_general x9, matrix products, share(): jnp.einsum('est,esd->td', weighted[k][:, :, begin:begin + count], outs[k]...  11.7 us
    another operation x4, local copies, waits for them, and re-layouts, experts_out(): return jnp.stack([out[:pair_slots], across_cores(out[pair_slots:])])  8.92 us
    ppermute x2, waiting for transfers between devices, next_section(): lax.ppermute(shard, 'pipe', [(i, (i + 1) % sections) for i in range(secti...  8.12 us
    dot_general x4, matrix products, experts_out(): jnp.einsum('est,td->esd', selector[k], block, preferred_element_type=jnp....  5.5 us
  transfers between devices with their start and end apart: 41, of which 22 were waited for; matrix products, arithmetic and copies ran while one was open for 40% of the time, Pallas kernels for 0%

profile of v1, /device:TPU:10, one launch (start us, length us, event | category | flops | bytes accessed | tf_op | source)
XLA Modules:
  0.0 175.1 jit_solution(1914299010260035633)
XLA Ops:
  4.1 3.2 %collective-permute-done = bf16[1,16,128]{2,1,0:T(8,128)(2,1)S(1)} collective-permute-done((bf16[1,16,128]{2,1,0:T(8,128)(2,1)S(1)}, bf16[1,16,128]{2,1,0:T(8,128)(2,1)S(1)}, u32[]{:S(2)}, u32[]{:S(2)}) %collective-permute-start) | collective-permute-done | bytes 4128 | tf_op jit(solution)/shard_map/ppermute | solution.py:23
  8.5 3.3 %collective-permute-done.1 = bf16[2,16,128]{2,1,0:T(8,128)(2,1)S(1)} collective-permute-done((bf16[2,16,128]{2,1,0:T(8,128)(2,1)S(1)}, bf16[2,16,128]{2,1,0:T(8,128)(2,1)S(1)}, u32[]{:S(2)}, u32[]{:S(2)}) %collective-permute-start.1) | collective-permute-done | bytes 8224 | tf_op jit(solution)/shard_map/ppermute | solution.py:23
  11.8 1.5 collective-permute-start.2
  14.7 2.0 %collective-permute-start.3 = (bf16[64,2048]{1,0:T(8,128)(2,1)}, bf16[64,2048]{1,0:T(8,128)(2,1)}, u32[]{:S(2)}, u32[]{:S(2)}) collective-permute-start(bf16[64,2048]{1,0:T(8,128)(2,1)} %get-tuple-element.37), channel_id=1, source_target_pairs={{0,4},{1,5},{4,8},{5,9},{8,12},{9,13},{12,14},{13,15},{14,10},{15,... | collective-permute-start | bytes 786440 | tf_op jit(solution)/shard_map/ppermute | solution.py:23
  16.7 2.0 %collective-permute-start.13 = (bf16[64,2048]{1,0:T(8,128)(2,1)}, bf16[64,2048]{1,0:T(8,128)(2,1)}, u32[]{:S(2)}, u32[]{:S(2)}) collective-permute-start(bf16[64,2048]{1,0:T(8,128)(2,1)} %get-tuple-element.38), channel_id=1, source_target_pairs={{0,4},{1,5},{4,8},{5,9},{8,12},{9,13},{12,14},{13,15},{14,10},{15,... | collective-permute-start | bytes 786440 | tf_op jit(solution)/shard_map/ppermute | solution.py:23
  20.5 3.7 %collective-permute-done.14 = bf16[64,2048]{1,0:T(8,128)(2,1)} collective-permute-done((bf16[64,2048]{1,0:T(8,128)(2,1)}, bf16[64,2048]{1,0:T(8,128)(2,1)}, u32[]{:S(2)}, u32[]{:S(2)}) %collective-permute-start.14) | collective-permute-done | bytes 262176 | tf_op jit(solution)/shard_map/ppermute | solution.py:23
  24.3 1.9 %collective-permute-start.4 = (bf16[64,2048]{1,0:T(8,128)(2,1)}, bf16[64,2048]{1,0:T(8,128)(2,1)S(1)}, u32[]{:S(2)}, u32[]{:S(2)}) collective-permute-start(bf16[64,2048]{1,0:T(8,128)(2,1)} %collective-permute-done.3), channel_id=1, source_target_pairs={{0,4},{1,5},{4,8},{5,9},{8,12},{9,13},{12,14},{13,15},{14,10},{15,... | collective-permute-start | bytes 786440 | tf_op jit(solution)/shard_map/ppermute | solution.py:23
  26.3 3.6 %collective-permute-done.13 = bf16[64,2048]{1,0:T(8,128)(2,1)} collective-permute-done((bf16[64,2048]{1,0:T(8,128)(2,1)}, bf16[64,2048]{1,0:T(8,128)(2,1)}, u32[]{:S(2)}, u32[]{:S(2)}) %collective-permute-start.13) | collective-permute-done | bytes 262176 | tf_op jit(solution)/shard_map/ppermute | solution.py:23
  29.9 2.0 %collective-permute-start.17 = (bf16[64,2048]{1,0:T(8,128)(2,1)}, bf16[64,2048]{1,0:T(8,128)(2,1)S(1)}, u32[]{:S(2)}, u32[]{:S(2)}) collective-permute-start(bf16[64,2048]{1,0:T(8,128)(2,1)} %collective-permute-done.13), channel_id=1, source_target_pairs={{0,4},{1,5},{4,8},{5,9},{8,12},{9,13},{12,14},{13,15},{14,10},{15,... | collective-permute-start | bytes 786440 | tf_op jit(solution)/shard_map/ppermute | solution.py:23
  31.9 1.7 convolution_convert_fusion.2
  35.3 1.6 collective-permute-start.5
  37.5 2.3 %collective-permute-start.21 = (bf16[64,2048]{1,0:T(8,128)(2,1)S(1)}, bf16[64,2048]{1,0:T(8,128)(2,1)S(1)}, u32[]{:S(2)}, u32[]{:S(2)}) collective-permute-start(bf16[64,2048]{1,0:T(8,128)(2,1)S(1)} %collective-permute-done.17), channel_id=1, source_target_pairs={{0,4},{1,5},{4,8},{5,9},{8,12},{9,13},{12,14},{13,15},{14,10},{15,... | collective-permute-start | bytes 786440 | tf_op jit(solution)/shard_map/ppermute | solution.py:23
  41.5 3.9 %collective-permute-done.22 = bf16[64,2048]{1,0:T(8,128)(2,1)S(1)} collective-permute-done((bf16[64,2048]{1,0:T(8,128)(2,1)S(1)}, bf16[64,2048]{1,0:T(8,128)(2,1)S(1)}, u32[]{:S(2)}, u32[]{:S(2)}) %collective-permute-start.22) | collective-permute-done | bytes 262176 | tf_op jit(solution)/shard_map/ppermute | solution.py:23
  45.3 3.8 %collective-permute-done.21 = bf16[64,2048]{1,0:T(8,128)(2,1)S(1)} collective-permute-done((bf16[64,2048]{1,0:T(8,128)(2,1)S(1)}, bf16[64,2048]{1,0:T(8,128)(2,1)S(1)}, u32[]{:S(2)}, u32[]{:S(2)}) %collective-permute-start.21) | collective-permute-done | bytes 262176 | tf_op jit(solution)/shard_map/ppermute | solution.py:23
  49.8 1.7 convolution_convert_fusion
  52.6 2.0 %collective-permute-start.6 = (bf16[64,2048]{1,0:T(8,128)(2,1)}, bf16[64,2048]{1,0:T(8,128)(2,1)}, u32[]{:S(2)}, u32[]{:S(2)}) collective-permute-start(bf16[64,2048]{1,0:T(8,128)(2,1)} %collective-permute-done.5), channel_id=1, source_target_pairs={{0,4},{1,5},{4,8},{5,9},{8,12},{9,13},{12,14},{13,15},{14,10},{15,... | collective-permute-start | bytes 786440 | tf_op jit(solution)/shard_map/ppermute | solution.py:23
  55.5 2.0 %fusion.20 = f32[288,768]{1,0:T(8,128)} fusion(bf16[1,1,2048,768]{3,2,1,0:T(8,128)(2,1)S(1)} %copy-done.18, bf16[144,2048]{1,0:T(8,128)(2,1)S(1)} %collective-permute-done.15, bf16[144,2048]{1,0:T(8,128)(2,1)S(1)} %get-tuple-element.17), kind=kOutput, calls=%fused_computation.20 | convolution fusion | flops 908328960 | bytes 5210112 | tf_op jit(solution)/shard_map/dot_general | solution.py:115
  57.6 5.9 %fusion.27 = bf16[288,2048]{1,0:T(8,128)(2,1)} fusion(bf16[1,1,768,2048]{3,2,1,0:T(8,128)(2,1)S(1)} %copy-done, f32[288,768]{1,0:T(8,128)} %fusion.20, bf16[1,1,2048,768]{3,2,1,0:T(8,128)(2,1)} %param.12, bf16[144,2048]{1,0:T(8,128)(2,1)} %copy-done.21, bf16[144,2048]{1,0:T(8,128)(2,1)} %copy-done.11), kind=kOutput, calls=%fused_computation.25 | convolution fusion | flops 1816215552 | bytes 9535488 | tf_op jit(solution)/shard_map/dot_general | solution.py:118
  63.4 2.5 %slice_bitcast_fusion.6 = (bf16[1,144,2048]{2,1,0:T(8,128)(2,1)}, bf16[144,2048]{1,0:T(8,128)(2,1)}) fusion(bf16[288,2048]{1,0:T(8,128)(2,1)} %fusion.27), kind=kLoop, calls=%fused_computation.105 | loop fusion | bytes 2359296 | tf_op jit(solution)/shard_map/stack | solution.py:119
  66.2 1.7 convolution_convert_fusion.3
  69.3 3.1 %fusion.18 = f32[288,768]{1,0:T(8,128)} fusion(bf16[1,1,2048,768]{3,2,1,0:T(8,128)(2,1)S(1)} %copy-done.19, bf16[144,2048]{1,0:T(8,128)(2,1)} %collective-permute-done.19, bf16[144,2048]{1,0:T(8,128)(2,1)S(1)} %copy-done.12), kind=kOutput, calls=%fused_computation.18 | convolution fusion | flops 908328960 | bytes 5210112 | tf_op jit(solution)/shard_map/dot_general | solution.py:115
  72.4 5.9 %fusion.30 = bf16[288,2048]{1,0:T(8,128)(2,1)} fusion(bf16[1,1,768,2048]{3,2,1,0:T(8,128)(2,1)S(1)} %copy-done, f32[288,768]{1,0:T(8,128)} %fusion.18, bf16[1,1,2048,768]{3,2,1,0:T(8,128)(2,1)} %param.12, bf16[144,2048]{1,0:T(8,128)(2,1)} %collective-permute-done.19, bf16[144,2048]{1,0:T(8,128)(2,1)} %get-tuple-element.13), kind=kOutput, calls=%fused_computation.26 | convolution fusion | flops 1816215552 | bytes 9535488 | tf_op jit(solution)/shard_map/dot_general | solution.py:118
  78.3 2.5 %slice_bitcast_fusion.3 = (bf16[1,144,2048]{2,1,0:T(8,128)(2,1)}, bf16[144,2048]{1,0:T(8,128)(2,1)}) fusion(bf16[288,2048]{1,0:T(8,128)(2,1)} %fusion.30), kind=kLoop, calls=%fused_computation.102 | loop fusion | bytes 2359296 | tf_op jit(solution)/shard_map/stack | solution.py:119
  81.0 4.1 %fusion.16 = f32[288,768]{1,0:T(8,128)} fusion(bf16[1,1,2048,768]{3,2,1,0:T(8,128)(2,1)} %param.11, bf16[144,2048]{1,0:T(8,128)(2,1)} %collective-permute-done.23, bf16[144,2048]{1,0:T(8,128)(2,1)S(1)} %copy-done.13), kind=kOutput, calls=%fused_computation.16 | convolution fusion | flops 908328960 | bytes 5210112 | tf_op jit(solution)/shard_map/dot_general | solution.py:115
  85.1 5.9 %fusion.33 = bf16[288,2048]{1,0:T(8,128)(2,1)} fusion(bf16[1,1,768,2048]{3,2,1,0:T(8,128)(2,1)S(1)} %copy-done, f32[288,768]{1,0:T(8,128)} %fusion.16, bf16[1,1,2048,768]{3,2,1,0:T(8,128)(2,1)} %param.12, bf16[144,2048]{1,0:T(8,128)(2,1)} %collective-permute-done.23, bf16[144,2048]{1,0:T(8,128)(2,1)} %get-tuple-element.9), kind=kOutput, calls=%fused_computation.27 | convolution fusion | flops 1816215552 | bytes 9535488 | tf_op jit(solution)/shard_map/dot_general | solution.py:118
  91.0 2.6 %slice_bitcast_fusion = (bf16[1,144,2048]{2,1,0:T(8,128)(2,1)}, bf16[144,2048]{1,0:T(8,128)(2,1)}) fusion(bf16[288,2048]{1,0:T(8,128)(2,1)} %fusion.33), kind=kLoop, calls=%fused_computation.99 | loop fusion | bytes 2359296 | tf_op jit(solution)/shard_map/stack | solution.py:119
  93.8 2.5 %convolution_bitcast_fusion.2 = f32[128,2048]{1,0:T(8,128)} fusion(bf16[1,144,2048]{2,1,0:T(8,128)(2,1)} %bitcast.52, bf16[1,144,2048]{2,1,0:T(8,128)(2,1)S(1)} %copy-done.1, bf16[2,144,256]{2,1,0:T(8,128)(2,1)S(1)} %copy-done.9), kind=kOutput, calls=%fused_computation.34 | convolution fusion | flops 151584768 | bytes 2301952 | tf_op jit(solution)/shard_map/est,esd->td/dot_general | solution.py:124
  96.4 3.1 %fusion.22 = f32[288,768]{1,0:T(8,128)} fusion(bf16[1,1,2048,768]{3,2,1,0:T(8,128)(2,1)S(1)} %copy-done.20, bf16[144,2048]{1,0:T(8,128)(2,1)} %collective-permute-done.11, bf16[144,2048]{1,0:T(8,128)(2,1)S(1)} %copy-done.14), kind=kOutput, calls=%fused_computation.22 | convolution fusion | flops 908328960 | bytes 5210112 | tf_op jit(solution)/shard_map/dot_general | solution.py:115
  99.5 6.1 %fusion.24 = bf16[288,2048]{1,0:T(8,128)(2,1)} fusion(bf16[1,1,768,2048]{3,2,1,0:T(8,128)(2,1)S(1)} %copy-done, f32[288,768]{1,0:T(8,128)} %fusion.22, bf16[1,1,2048,768]{3,2,1,0:T(8,128)(2,1)} %param.12, bf16[144,2048]{1,0:T(8,128)(2,1)} %collective-permute-done.11, bf16[144,2048]{1,0:T(8,128)(2,1)} %get-tuple-element.21), kind=kOutput, calls=%fused_computation.24 | convolution fusion | flops 1816215552 | bytes 9535488 | tf_op jit(solution)/shard_map/dot_general | solution.py:118
  108.9 1.6 convolution_bitcast_fusion.1
  110.5 1.6 convolution_bitcast_fusion.4
  112.1 1.5 convolution_bitcast_fusion
  114.1 2.0 %collective-permute-start.28 = (bf16[64,2048]{1,0:T(8,128)(2,1)S(1)}, bf16[64,2048]{1,0:T(8,128)(2,1)S(1)}, u32[]{:S(2)}, u32[]{:S(2)}) collective-permute-start(bf16[64,2048]{1,0:T(8,128)(2,1)S(1)} %fusion.37), channel_id=1, source_target_pairs={{0,4},{1,5},{4,8},{5,9},{8,12},{9,13},{12,14},{13,15},{14,10},{15,... | collective-permute-start | bytes 786440 | tf_op jit(solution)/shard_map/ppermute | solution.py:23
  117.8 1.6 collective-permute-start.33
  120.4 2.9 %collective-permute-done.28 = bf16[64,2048]{1,0:T(8,128)(2,1)S(1)} collective-permute-done((bf16[64,2048]{1,0:T(8,128)(2,1)S(1)}, bf16[64,2048]{1,0:T(8,128)(2,1)S(1)}, u32[]{:S(2)}, u32[]{:S(2)}) %collective-permute-start.28) | collective-permute-done | bytes 262176 | tf_op jit(solution)/shard_map/ppermute | solution.py:23
  123.3 2.0 %collective-permute-start.29 = (bf16[64,2048]{1,0:T(8,128)(2,1)S(1)}, bf16[64,2048]{1,0:T(8,128)(2,1)S(1)}, u32[]{:S(2)}, u32[]{:S(2)}) collective-permute-start(bf16[64,2048]{1,0:T(8,128)(2,1)S(1)} %fusion.97), channel_id=1, source_target_pairs={{0,4},{1,5},{4,8},{5,9},{8,12},{9,13},{12,14},{13,15},{14,10},{15,... | collective-permute-start | bytes 786440 | tf_op jit(solution)/shard_map/ppermute | solution.py:23
  125.3 7.7 %collective-permute-done.36 = bf16[64,2048]{1,0:T(8,128)(2,1)S(1)} collective-permute-done((bf16[64,2048]{1,0:T(8,128)(2,1)S(1)}, bf16[64,2048]{1,0:T(8,128)(2,1)S(1)}, u32[]{:S(2)}, u32[]{:S(2)}) %collective-permute-start.36) | collective-permute-done | bytes 262176 | tf_op jit(solution)/shard_map/ppermute | solution.py:23
  134.0 2.2 %collective-permute-start.30 = (bf16[64,2048]{1,0:T(8,128)(2,1)S(1)}, bf16[64,2048]{1,0:T(8,128)(2,1)S(1)}, u32[]{:S(2)}, u32[]{:S(2)}) collective-permute-start(bf16[64,2048]{1,0:T(8,128)(2,1)S(1)} %get-tuple-element.31), channel_id=1, source_target_pairs={{0,4},{1,5},{4,8},{5,9},{8,12},{9,13},{12,14},{13,15},{14,10},{15,... | collective-permute-start | bytes 786440 | tf_op jit(solution)/shard_map/ppermute | solution.py:23
  137.7 2.7 %collective-permute-done.37 = bf16[64,2048]{1,0:T(8,128)(2,1)S(1)} collective-permute-done((bf16[64,2048]{1,0:T(8,128)(2,1)S(1)}, bf16[64,2048]{1,0:T(8,128)(2,1)S(1)}, u32[]{:S(2)}, u32[]{:S(2)}) %collective-permute-start.37) | collective-permute-done | bytes 262176 | tf_op jit(solution)/shard_map/ppermute | solution.py:23
  141.7 1.6 collective-permute-done.30
  143.3 4.1 %collective-permute-done.34 = bf16[64,2048]{1,0:T(8,128)(2,1)S(1)} collective-permute-done((bf16[64,2048]{1,0:T(8,128)(2,1)S(1)}, bf16[64,2048]{1,0:T(8,128)(2,1)S(1)}, u32[]{:S(2)}, u32[]{:S(2)}) %collective-permute-start.34) | collective-permute-done | bytes 262176 | tf_op jit(solution)/shard_map/ppermute | solution.py:23
  147.5 2.4 %collective-permute-start.31 = (bf16[64,2048]{1,0:T(8,128)(2,1)S(1)}, bf16[64,2048]{1,0:T(8,128)(2,1)S(1)}, u32[]{:S(2)}, u32[]{:S(2)}) collective-permute-start(bf16[64,2048]{1,0:T(8,128)(2,1)S(1)} %get-tuple-element.29), channel_id=1, source_target_pairs={{0,4},{1,5},{4,8},{5,9},{8,12},{9,13},{12,14},{13,15},{14,10},{15,... | collective-permute-start | bytes 786440 | tf_op jit(solution)/shard_map/ppermute | solution.py:23
  154.6 2.2 %collective-permute-done.31 = bf16[64,2048]{1,0:T(8,128)(2,1)S(1)} collective-permute-done((bf16[64,2048]{1,0:T(8,128)(2,1)S(1)}, bf16[64,2048]{1,0:T(8,128)(2,1)S(1)}, u32[]{:S(2)}, u32[]{:S(2)}) %collective-permute-start.31) | collective-permute-done | bytes 262176 | tf_op jit(solution)/shard_map/ppermute | solution.py:23
  156.8 3.3 %collective-permute-done.35 = bf16[64,2048]{1,0:T(8,128)(2,1)S(1)} collective-permute-done((bf16[64,2048]{1,0:T(8,128)(2,1)S(1)}, bf16[64,2048]{1,0:T(8,128)(2,1)S(1)}, u32[]{:S(2)}, u32[]{:S(2)}) %collective-permute-start.35) | collective-permute-done | bytes 262176 | tf_op jit(solution)/shard_map/ppermute | solution.py:23
  161.0 2.8 %collective-permute-done.39 = bf16[64,2048]{1,0:T(8,128)(2,1)S(1)} collective-permute-done((bf16[64,2048]{1,0:T(8,128)(2,1)S(1)}, bf16[64,2048]{1,0:T(8,128)(2,1)S(1)}, u32[]{:S(2)}, u32[]{:S(2)}) %collective-permute-start.39) | collective-permute-done | bytes 262176 | tf_op jit(solution)/shard_map/ppermute | solution.py:23
  164.0 1.6 collective-permute-start.32
  166.1 5.3 %collective-permute-done.32 = bf16[64,2048]{1,0:T(8,128)(2,1)S(1)} collective-permute-done((bf16[64,2048]{1,0:T(8,128)(2,1)S(1)}, bf16[64,2048]{1,0:T(8,128)(2,1)S(1)}, u32[]{:S(2)}, u32[]{:S(2)}) %collective-permute-start.32) | collective-permute-done | bytes 262176 | tf_op jit(solution)/shard_map/ppermute | solution.py:33
  171.4 2.8 %collective-permute-done.40 = bf16[64,2048]{1,0:T(8,128)(2,1)S(1)} collective-permute-done((bf16[64,2048]{1,0:T(8,128)(2,1)S(1)}, bf16[64,2048]{1,0:T(8,128)(2,1)S(1)}, u32[]{:S(2)}, u32[]{:S(2)}) %collective-permute-start.40) | collective-permute-done | bytes 262176 | tf_op jit(solution)/shard_map/ppermute | solution.py:33
  (151 shorter events, 34.7 us)
Async XLA Ops:
  0.0 57.5 %copy-start = (bf16[1,1,768,2048]{3,2,1,0:T(8,128)(2,1)S(1)}, bf16[1,1,768,2048]{3,2,1,0:T(8,128)(2,1)}, u32[]{:S(2)}) copy-start(bf16[1,1,768,2048]{3,2,1,0:T(8,128)(2,1)} %param.13) | copy-start | bytes 9437188
  0.0 19.1 %copy-start.17 = (s32[256]{0:T(256)S(1)}, s32[256]{0:T(256)}, u32[]{:S(2)}) copy-start(s32[256]{0:T(256)} %constant.42.clone.1) | copy-start | bytes 3076
  3.6 3.7 %collective-permute-start = (bf16[1,16,128]{2,1,0:T(8,128)(2,1)S(1)}, bf16[1,16,128]{2,1,0:T(8,128)(2,1)S(1)}, u32[]{:S(2)}, u32[]{:S(2)}) collective-permute-start(bf16[1,16,128]{2,1,0:T(8,128)(2,1)S(1)} %fusion.121), channel_id=1, source_target_pairs={{0,4},{1,5},{4,8},{5,9},{8,12},{9,13},{12,14},{13,15},{14,10},{15,... | collective-permute-start | bytes 12296 | tf_op jit(solution)/shard_map/ppermute | solution.py:23
  7.2 4.5 %collective-permute-start.1 = (bf16[2,16,128]{2,1,0:T(8,128)(2,1)S(1)}, bf16[2,16,128]{2,1,0:T(8,128)(2,1)S(1)}, u32[]{:S(2)}, u32[]{:S(2)}) collective-permute-start(bf16[2,16,128]{2,1,0:T(8,128)(2,1)S(1)} %pad_maximum_fusion.43), channel_id=1, source_target_pairs={{0,8},{1,9},{4,12},{5,13},{8,14},{9,15},{12,10},{13,11},{14,6},{15... | collective-permute-start | bytes 24584 | tf_op jit(solution)/shard_map/ppermute | solution.py:23
  11.8 6.9 %collective-permute-start.2 = (bf16[4,16,128]{2,1,0:T(8,128)(2,1)S(1)}, bf16[4,16,128]{2,1,0:T(8,128)(2,1)S(1)}, u32[]{:S(2)}, u32[]{:S(2)}) collective-permute-start(bf16[4,16,128]{2,1,0:T(8,128)(2,1)S(1)} %pad_maximum_fusion.42), channel_id=1, source_target_pairs={{0,14},{1,15},{4,10},{5,11},{8,6},{9,7},{12,2},{13,3},{14,0},{15,1... | collective-permute-start | bytes 49160 | tf_op jit(solution)/shard_map/ppermute | solution.py:23
  14.2 10.0 %collective-permute-start.14 = (bf16[64,2048]{1,0:T(8,128)(2,1)}, bf16[64,2048]{1,0:T(8,128)(2,1)}, u32[]{:S(2)}, u32[]{:S(2)}) collective-permute-start(bf16[64,2048]{1,0:T(8,128)(2,1)} %get-tuple-element.37), channel_id=1, source_target_pairs={{0,2},{1,3},{4,0},{5,1},{8,4},{9,5},{12,8},{13,9},{14,12},{15,13},... | collective-permute-start | bytes 786440 | tf_op jit(solution)/shard_map/ppermute | solution.py:23
  14.7 9.7 %collective-permute-start.3 = (bf16[64,2048]{1,0:T(8,128)(2,1)}, bf16[64,2048]{1,0:T(8,128)(2,1)}, u32[]{:S(2)}, u32[]{:S(2)}) collective-permute-start(bf16[64,2048]{1,0:T(8,128)(2,1)} %get-tuple-element.37), channel_id=1, source_target_pairs={{0,4},{1,5},{4,8},{5,9},{8,12},{9,13},{12,14},{13,15},{14,10},{15,... | collective-permute-start | bytes 786440 | tf_op jit(solution)/shard_map/ppermute | solution.py:23
  16.7 13.1 %collective-permute-start.13 = (bf16[64,2048]{1,0:T(8,128)(2,1)}, bf16[64,2048]{1,0:T(8,128)(2,1)}, u32[]{:S(2)}, u32[]{:S(2)}) collective-permute-start(bf16[64,2048]{1,0:T(8,128)(2,1)} %get-tuple-element.38), channel_id=1, source_target_pairs={{0,4},{1,5},{4,8},{5,9},{8,12},{9,13},{12,14},{13,15},{14,10},{15,... | collective-permute-start | bytes 786440 | tf_op jit(solution)/shard_map/ppermute | solution.py:23
  18.7 13.2 %collective-permute-start.7 = (bf16[64,2048]{1,0:T(8,128)(2,1)}, bf16[64,2048]{1,0:T(8,128)(2,1)}, u32[]{:S(2)}, u32[]{:S(2)}) collective-permute-start(bf16[64,2048]{1,0:T(8,128)(2,1)} %get-tuple-element.38), channel_id=1, source_target_pairs={{0,2},{1,3},{4,0},{5,1},{8,4},{9,5},{12,8},{13,9},{14,12},{15,13},... | collective-permute-start | bytes 786440 | tf_op jit(solution)/shard_map/ppermute | solution.py:23
  19.7 30.1 %copy-start.16 = (pred[4,2,144,256]{3,2,1,0:T(8,128)(4,1)}, pred[4,2,144,256]{3,2,1,0:T(8,128)(4,1)S(1)}, u32[]{:S(2)}) copy-start(pred[4,2,144,256]{3,2,1,0:T(8,128)(4,1)S(1)} %fusion.41) | copy-start | bytes 884740
  24.2 10.6 %collective-permute-start.18 = (bf16[64,2048]{1,0:T(8,128)(2,1)}, bf16[64,2048]{1,0:T(8,128)(2,1)S(1)}, u32[]{:S(2)}, u32[]{:S(2)}) collective-permute-start(bf16[64,2048]{1,0:T(8,128)(2,1)} %collective-permute-done.14), channel_id=1, source_target_pairs={{0,2},{1,3},{4,0},{5,1},{8,4},{9,5},{12,8},{13,9},{14,12},{15,13},... | collective-permute-start | bytes 786440 | tf_op jit(solution)/shard_map/ppermute | solution.py:23
  24.3 10.9 %collective-permute-start.4 = (bf16[64,2048]{1,0:T(8,128)(2,1)}, bf16[64,2048]{1,0:T(8,128)(2,1)S(1)}, u32[]{:S(2)}, u32[]{:S(2)}) collective-permute-start(bf16[64,2048]{1,0:T(8,128)(2,1)} %collective-permute-done.3), channel_id=1, source_target_pairs={{0,4},{1,5},{4,8},{5,9},{8,12},{9,13},{12,14},{13,15},{14,10},{15,... | collective-permute-start | bytes 786440 | tf_op jit(solution)/shard_map/ppermute | solution.py:23
  29.9 7.7 %collective-permute-start.17 = (bf16[64,2048]{1,0:T(8,128)(2,1)}, bf16[64,2048]{1,0:T(8,128)(2,1)S(1)}, u32[]{:S(2)}, u32[]{:S(2)}) collective-permute-start(bf16[64,2048]{1,0:T(8,128)(2,1)} %collective-permute-done.13), channel_id=1, source_target_pairs={{0,4},{1,5},{4,8},{5,9},{8,12},{9,13},{12,14},{13,15},{14,10},{15,... | collective-permute-start | bytes 786440 | tf_op jit(solution)/shard_map/ppermute | solution.py:23
  31.9 7.9 %collective-permute-start.8 = (bf16[64,2048]{1,0:T(8,128)(2,1)}, bf16[64,2048]{1,0:T(8,128)(2,1)S(1)}, u32[]{:S(2)}, u32[]{:S(2)}) collective-permute-start(bf16[64,2048]{1,0:T(8,128)(2,1)} %collective-permute-done.7), channel_id=1, source_target_pairs={{0,2},{1,3},{4,0},{5,1},{8,4},{9,5},{12,8},{13,9},{14,12},{15,13},... | collective-permute-start | bytes 786440 | tf_op jit(solution)/shard_map/ppermute | solution.py:23
  33.7 21.0 %copy-start.11 = (bf16[144,2048]{1,0:T(8,128)(2,1)}, bf16[144,2048]{1,0:T(8,128)(2,1)S(1)}, u32[]{:S(2)}) copy-start(bf16[144,2048]{1,0:T(8,128)(2,1)S(1)} %get-tuple-element.17) | copy-start | bytes 1769476
  33.7 21.0 %collective-permute-start.15 = (bf16[144,2048]{1,0:T(8,128)(2,1)S(1)}, bf16[144,2048]{1,0:T(8,128)(2,1)S(1)}, u32[]{:S(2)}, u32[]{:S(2)}) collective-permute-start(bf16[144,2048]{1,0:T(8,128)(2,1)S(1)} %get-tuple-element.18), channel_id=1, source_target_pairs={{0,1},{1,0},{2,3},{3,2},{4,5},{5,4},{6,7},{7,6},{8,9},{9,8},{10,11... | collective-permute-start | bytes 1769480 | tf_op jit(solution)/shard_map/ppermute | solution.py:28
  34.9 10.5 %collective-permute-start.22 = (bf16[64,2048]{1,0:T(8,128)(2,1)S(1)}, bf16[64,2048]{1,0:T(8,128)(2,1)S(1)}, u32[]{:S(2)}, u32[]{:S(2)}) collective-permute-start(bf16[64,2048]{1,0:T(8,128)(2,1)S(1)} %collective-permute-done.18), channel_id=1, source_target_pairs={{0,2},{1,3},{4,0},{5,1},{8,4},{9,5},{12,8},{13,9},{14,12},{15,13},... | collective-permute-start | bytes 786440 | tf_op jit(solution)/shard_map/ppermute | solution.py:23
  35.3 10.0 %collective-permute-start.5 = (bf16[64,2048]{1,0:T(8,128)(2,1)S(1)}, bf16[64,2048]{1,0:T(8,128)(2,1)}, u32[]{:S(2)}, u32[]{:S(2)}) collective-permute-start(bf16[64,2048]{1,0:T(8,128)(2,1)S(1)} %collective-permute-done.4), channel_id=1, source_target_pairs={{0,4},{1,5},{4,8},{5,9},{8,12},{9,13},{12,14},{13,15},{14,10},{15,... | collective-permute-start | bytes 786440 | tf_op jit(solution)/shard_map/ppermute | solution.py:23
  37.5 11.6 %collective-permute-start.21 = (bf16[64,2048]{1,0:T(8,128)(2,1)S(1)}, bf16[64,2048]{1,0:T(8,128)(2,1)S(1)}, u32[]{:S(2)}, u32[]{:S(2)}) collective-permute-start(bf16[64,2048]{1,0:T(8,128)(2,1)S(1)} %collective-permute-done.17), channel_id=1, source_target_pairs={{0,4},{1,5},{4,8},{5,9},{8,12},{9,13},{12,14},{13,15},{14,10},{15,... | collective-permute-start | bytes 786440 | tf_op jit(solution)/shard_map/ppermute | solution.py:23
  39.8 10.0 %collective-permute-start.9 = (bf16[64,2048]{1,0:T(8,128)(2,1)S(1)}, bf16[64,2048]{1,0:T(8,128)(2,1)}, u32[]{:S(2)}, u32[]{:S(2)}) collective-permute-start(bf16[64,2048]{1,0:T(8,128)(2,1)S(1)} %collective-permute-done.8), channel_id=1, source_target_pairs={{0,2},{1,3},{4,0},{5,1},{8,4},{9,5},{12,8},{13,9},{14,12},{15,13},... | collective-permute-start | bytes 786440 | tf_op jit(solution)/shard_map/ppermute | solution.py:23
  45.3 24.0 %collective-permute-start.19 = (bf16[144,2048]{1,0:T(8,128)(2,1)}, bf16[144,2048]{1,0:T(8,128)(2,1)}, u32[]{:S(2)}, u32[]{:S(2)}) collective-permute-start(bf16[144,2048]{1,0:T(8,128)(2,1)} %get-tuple-element.14), channel_id=1, source_target_pairs={{0,1},{1,0},{2,3},{3,2},{4,5},{5,4},{6,7},{7,6},{8,9},{9,8},{10,11... | collective-permute-start | bytes 1769480 | tf_op jit(solution)/shard_map/ppermute | solution.py:28
  49.8 5.7 %copy-start.18 = (bf16[1,1,2048,768]{3,2,1,0:T(8,128)(2,1)S(1)}, bf16[1,1,2048,768]{3,2,1,0:T(8,128)(2,1)}, u32[]{:S(2)}) copy-start(bf16[1,1,2048,768]{3,2,1,0:T(8,128)(2,1)} %param.11) | copy-start | bytes 9437188
  52.6 28.4 %collective-permute-start.23 = (bf16[144,2048]{1,0:T(8,128)(2,1)}, bf16[144,2048]{1,0:T(8,128)(2,1)}, u32[]{:S(2)}, u32[]{:S(2)}) collective-permute-start(bf16[144,2048]{1,0:T(8,128)(2,1)} %get-tuple-element.10), channel_id=1, source_target_pairs={{0,1},{1,0},{2,3},{3,2},{4,5},{5,4},{6,7},{7,6},{8,9},{9,8},{10,11... | collective-permute-start | bytes 1769480 | tf_op jit(solution)/shard_map/ppermute | solution.py:28
  52.6 13.5 %collective-permute-start.6 = (bf16[64,2048]{1,0:T(8,128)(2,1)}, bf16[64,2048]{1,0:T(8,128)(2,1)}, u32[]{:S(2)}, u32[]{:S(2)}) collective-permute-start(bf16[64,2048]{1,0:T(8,128)(2,1)} %collective-permute-done.5), channel_id=1, source_target_pairs={{0,4},{1,5},{4,8},{5,9},{8,12},{9,13},{12,14},{13,15},{14,10},{15,... | collective-permute-start | bytes 786440 | tf_op jit(solution)/shard_map/ppermute | solution.py:23
  54.7 11.5 %collective-permute-start.10 = (bf16[64,2048]{1,0:T(8,128)(2,1)}, bf16[64,2048]{1,0:T(8,128)(2,1)}, u32[]{:S(2)}, u32[]{:S(2)}) collective-permute-start(bf16[64,2048]{1,0:T(8,128)(2,1)} %collective-permute-done.9), channel_id=1, source_target_pairs={{0,2},{1,3},{4,0},{5,1},{8,4},{9,5},{12,8},{13,9},{14,12},{15,13},... | collective-permute-start | bytes 786440 | tf_op jit(solution)/shard_map/ppermute | solution.py:23
  65.9 27.9 %collective-permute-start.16 = (bf16[144,2048]{1,0:T(8,128)(2,1)}, bf16[144,2048]{1,0:T(8,128)(2,1)}, u32[]{:S(2)}, u32[]{:S(2)}) collective-permute-start(bf16[144,2048]{1,0:T(8,128)(2,1)} %get-tuple-element.16), channel_id=1, source_target_pairs={{0,1},{1,0},{2,3},{3,2},{4,5},{5,4},{6,7},{7,6},{8,9},{9,8},{10,11... | collective-permute-start | bytes 1769480 | tf_op jit(solution)/shard_map/ppermute | solution.py:28
  69.0 27.3 %collective-permute-start.11 = (bf16[144,2048]{1,0:T(8,128)(2,1)}, bf16[144,2048]{1,0:T(8,128)(2,1)}, u32[]{:S(2)}, u32[]{:S(2)}) collective-permute-start(bf16[144,2048]{1,0:T(8,128)(2,1)} %get-tuple-element.22), channel_id=1, source_target_pairs={{0,1},{1,0},{2,3},{3,2},{4,5},{5,4},{6,7},{7,6},{8,9},{9,8},{10,11... | collective-permute-start | bytes 1769480 | tf_op jit(solution)/shard_map/ppermute | solution.py:28
  80.8 28.1 %collective-permute-start.20 = (bf16[144,2048]{1,0:T(8,128)(2,1)}, bf16[144,2048]{1,0:T(8,128)(2,1)}, u32[]{:S(2)}, u32[]{:S(2)}) collective-permute-start(bf16[144,2048]{1,0:T(8,128)(2,1)} %get-tuple-element.12), channel_id=1, source_target_pairs={{0,1},{1,0},{2,3},{3,2},{4,5},{5,4},{6,7},{7,6},{8,9},{9,8},{10,11... | collective-permute-start | bytes 1769480 | tf_op jit(solution)/shard_map/ppermute | solution.py:28
  93.5 18.6 %collective-permute-start.24 = (bf16[144,2048]{1,0:T(8,128)(2,1)}, bf16[144,2048]{1,0:T(8,128)(2,1)}, u32[]{:S(2)}, u32[]{:S(2)}) collective-permute-start(bf16[144,2048]{1,0:T(8,128)(2,1)} %get-tuple-element.8), channel_id=1, source_target_pairs={{0,1},{1,0},{2,3},{3,2},{4,5},{5,4},{6,7},{7,6},{8,9},{9,8},{10,11... | collective-permute-start | bytes 1769480 | tf_op jit(solution)/shard_map/ppermute | solution.py:28
  107.0 6.7 %collective-permute-start.12 = (bf16[144,2048]{1,0:T(8,128)(2,1)S(1)}, bf16[144,2048]{1,0:T(8,128)(2,1)S(1)}, u32[]{:S(2)}, u32[]{:S(2)}) collective-permute-start(bf16[144,2048]{1,0:T(8,128)(2,1)S(1)} %get-tuple-element.20), channel_id=1, source_target_pairs={{0,1},{1,0},{2,3},{3,2},{4,5},{5,4},{6,7},{7,6},{8,9},{9,8},{10,11... | collective-permute-start | bytes 1769480 | tf_op jit(solution)/shard_map/ppermute | solution.py:28
  114.1 9.2 %collective-permute-start.28 = (bf16[64,2048]{1,0:T(8,128)(2,1)S(1)}, bf16[64,2048]{1,0:T(8,128)(2,1)S(1)}, u32[]{:S(2)}, u32[]{:S(2)}) collective-permute-start(bf16[64,2048]{1,0:T(8,128)(2,1)S(1)} %fusion.37), channel_id=1, source_target_pairs={{0,4},{1,5},{4,8},{5,9},{8,12},{9,13},{12,14},{13,15},{14,10},{15,... | collective-permute-start | bytes 786440 | tf_op jit(solution)/shard_map/ppermute | solution.py:23
  117.8 16.0 %collective-permute-start.33 = (bf16[64,2048]{1,0:T(8,128)(2,1)S(1)}, bf16[64,2048]{1,0:T(8,128)(2,1)S(1)}, u32[]{:S(2)}, u32[]{:S(2)}) collective-permute-start(bf16[64,2048]{1,0:T(8,128)(2,1)S(1)} %slice.481), channel_id=1, source_target_pairs={{0,4},{1,5},{4,8},{5,9},{8,12},{9,13},{12,14},{13,15},{14,10},{15,... | collective-permute-start | bytes 786440 | tf_op jit(solution)/shard_map/ppermute | solution.py:23
  119.3 18.4 %collective-permute-start.25 = (bf16[64,2048]{1,0:T(8,128)(2,1)S(1)}, bf16[64,2048]{1,0:T(8,128)(2,1)S(1)}, u32[]{:S(2)}, u32[]{:S(2)}) collective-permute-start(bf16[64,2048]{1,0:T(8,128)(2,1)S(1)} %slice.482), channel_id=1, source_target_pairs={{0,2},{1,3},{4,0},{5,1},{8,4},{9,5},{12,8},{13,9},{14,12},{15,13},... | collective-permute-start | bytes 786440 | tf_op jit(solution)/shard_map/ppermute | solution.py:23
  120.3 12.8 %collective-permute-start.36 = (bf16[64,2048]{1,0:T(8,128)(2,1)S(1)}, bf16[64,2048]{1,0:T(8,128)(2,1)S(1)}, u32[]{:S(2)}, u32[]{:S(2)}) collective-permute-start(bf16[64,2048]{1,0:T(8,128)(2,1)S(1)} %fusion.38), channel_id=1, source_target_pairs={{0,2},{1,3},{4,0},{5,1},{8,4},{9,5},{12,8},{13,9},{14,12},{15,13},... | collective-permute-start | bytes 786440 | tf_op jit(solution)/shard_map/ppermute | solution.py:23
  123.3 10.5 %collective-permute-start.29 = (bf16[64,2048]{1,0:T(8,128)(2,1)S(1)}, bf16[64,2048]{1,0:T(8,128)(2,1)S(1)}, u32[]{:S(2)}, u32[]{:S(2)}) collective-permute-start(bf16[64,2048]{1,0:T(8,128)(2,1)S(1)} %fusion.97), channel_id=1, source_target_pairs={{0,4},{1,5},{4,8},{5,9},{8,12},{9,13},{12,14},{13,15},{14,10},{15,... | collective-permute-start | bytes 786440 | tf_op jit(solution)/shard_map/ppermute | solution.py:23
  133.1 14.2 %copy-start.6 = (f32[128,2048]{1,0:T(8,128)S(1)}, f32[128,2048]{1,0:T(8,128)}, u32[]{:S(2)}) copy-start(f32[128,2048]{1,0:T(8,128)} %convolution_bitcast_fusion.2) | copy-start | bytes 3145732
  133.2 7.3 %collective-permute-start.37 = (bf16[64,2048]{1,0:T(8,128)(2,1)S(1)}, bf16[64,2048]{1,0:T(8,128)(2,1)S(1)}, u32[]{:S(2)}, u32[]{:S(2)}) collective-permute-start(bf16[64,2048]{1,0:T(8,128)(2,1)S(1)} %fusion.90), channel_id=1, source_target_pairs={{0,2},{1,3},{4,0},{5,1},{8,4},{9,5},{12,8},{13,9},{14,12},{15,13},... | collective-permute-start | bytes 786440 | tf_op jit(solution)/shard_map/ppermute | solution.py:23
  134.0 9.3 %collective-permute-start.30 = (bf16[64,2048]{1,0:T(8,128)(2,1)S(1)}, bf16[64,2048]{1,0:T(8,128)(2,1)S(1)}, u32[]{:S(2)}, u32[]{:S(2)}) collective-permute-start(bf16[64,2048]{1,0:T(8,128)(2,1)S(1)} %get-tuple-element.31), channel_id=1, source_target_pairs={{0,4},{1,5},{4,8},{5,9},{8,12},{9,13},{12,14},{13,15},{14,10},{15,... | collective-permute-start | bytes 786440 | tf_op jit(solution)/shard_map/ppermute | solution.py:23
  136.2 11.1 %collective-permute-start.34 = (bf16[64,2048]{1,0:T(8,128)(2,1)S(1)}, bf16[64,2048]{1,0:T(8,128)(2,1)S(1)}, u32[]{:S(2)}, u32[]{:S(2)}) collective-permute-start(bf16[64,2048]{1,0:T(8,128)(2,1)S(1)} %get-tuple-element.32), channel_id=1, source_target_pairs={{0,4},{1,5},{4,8},{5,9},{8,12},{9,13},{12,14},{13,15},{14,10},{15,... | collective-permute-start | bytes 786440 | tf_op jit(solution)/shard_map/ppermute | solution.py:23
  140.6 10.8 %collective-permute-start.26 = (bf16[64,2048]{1,0:T(8,128)(2,1)S(1)}, bf16[64,2048]{1,0:T(8,128)(2,1)S(1)}, u32[]{:S(2)}, u32[]{:S(2)}) collective-permute-start(bf16[64,2048]{1,0:T(8,128)(2,1)S(1)} %get-tuple-element.27), channel_id=1, source_target_pairs={{0,2},{1,3},{4,0},{5,1},{8,4},{9,5},{12,8},{13,9},{14,12},{15,13},... | collective-permute-start | bytes 786440 | tf_op jit(solution)/shard_map/ppermute | solution.py:23
  141.1 12.9 %copy-start.5 = (bf16[1,128,2048]{2,1,0:T(8,128)(2,1)S(1)}, bf16[1,128,2048]{2,1,0:T(8,128)(2,1)}, u32[]{:S(2)}) copy-start(bf16[1,128,2048]{2,1,0:T(8,128)(2,1)} %param.7) | copy-start | bytes 1572868
  141.1 11.5 %collective-permute-start.38 = (bf16[64,2048]{1,0:T(8,128)(2,1)S(1)}, bf16[64,2048]{1,0:T(8,128)(2,1)S(1)}, u32[]{:S(2)}, u32[]{:S(2)}) collective-permute-start(bf16[64,2048]{1,0:T(8,128)(2,1)S(1)} %get-tuple-element.28), channel_id=1, source_target_pairs={{0,2},{1,3},{4,0},{5,1},{8,4},{9,5},{12,8},{13,9},{14,12},{15,13},... | collective-permute-start | bytes 786440 | tf_op jit(solution)/shard_map/ppermute | solution.py:23
  147.5 9.3 %collective-permute-start.31 = (bf16[64,2048]{1,0:T(8,128)(2,1)S(1)}, bf16[64,2048]{1,0:T(8,128)(2,1)S(1)}, u32[]{:S(2)}, u32[]{:S(2)}) collective-permute-start(bf16[64,2048]{1,0:T(8,128)(2,1)S(1)} %get-tuple-element.29), channel_id=1, source_target_pairs={{0,4},{1,5},{4,8},{5,9},{8,12},{9,13},{12,14},{13,15},{14,10},{15,... | collective-permute-start | bytes 786440 | tf_op jit(solution)/shard_map/ppermute | solution.py:23
  149.9 10.1 %collective-permute-start.35 = (bf16[64,2048]{1,0:T(8,128)(2,1)S(1)}, bf16[64,2048]{1,0:T(8,128)(2,1)S(1)}, u32[]{:S(2)}, u32[]{:S(2)}) collective-permute-start(bf16[64,2048]{1,0:T(8,128)(2,1)S(1)} %get-tuple-element.30), channel_id=1, source_target_pairs={{0,4},{1,5},{4,8},{5,9},{8,12},{9,13},{12,14},{13,15},{14,10},{15,... | collective-permute-start | bytes 786440 | tf_op jit(solution)/shard_map/ppermute | solution.py:23
  152.7 8.3 %collective-permute-start.27 = (bf16[64,2048]{1,0:T(8,128)(2,1)S(1)}, bf16[64,2048]{1,0:T(8,128)(2,1)S(1)}, u32[]{:S(2)}, u32[]{:S(2)}) collective-permute-start(bf16[64,2048]{1,0:T(8,128)(2,1)S(1)} %get-tuple-element.25), channel_id=1, source_target_pairs={{0,2},{1,3},{4,0},{5,1},{8,4},{9,5},{12,8},{13,9},{14,12},{15,13},... | collective-permute-start | bytes 786440 | tf_op jit(solution)/shard_map/ppermute | solution.py:23
  153.3 10.6 %collective-permute-start.39 = (bf16[64,2048]{1,0:T(8,128)(2,1)S(1)}, bf16[64,2048]{1,0:T(8,128)(2,1)S(1)}, u32[]{:S(2)}, u32[]{:S(2)}) collective-permute-start(bf16[64,2048]{1,0:T(8,128)(2,1)S(1)} %get-tuple-element.26), channel_id=1, source_target_pairs={{0,2},{1,3},{4,0},{5,1},{8,4},{9,5},{12,8},{13,9},{14,12},{15,13},... | collective-permute-start | bytes 786440 | tf_op jit(solution)/shard_map/ppermute | solution.py:23
  164.0 7.4 %collective-permute-start.32 = (bf16[64,2048]{1,0:T(8,128)(2,1)S(1)}, bf16[64,2048]{1,0:T(8,128)(2,1)S(1)}, u32[]{:S(2)}, u32[]{:S(2)}) collective-permute-start(bf16[64,2048]{1,0:T(8,128)(2,1)S(1)} %get-tuple-element.23), channel_id=1, source_target_pairs={{0,16},{16,0},{1,17},{17,1},{2,18},{18,2},{3,19},{19,3},{4,20},{20... | collective-permute-start | bytes 786440 | tf_op jit(solution)/shard_map/ppermute | solution.py:33
  165.6 8.6 %collective-permute-start.40 = (bf16[64,2048]{1,0:T(8,128)(2,1)S(1)}, bf16[64,2048]{1,0:T(8,128)(2,1)S(1)}, u32[]{:S(2)}, u32[]{:S(2)}) collective-permute-start(bf16[64,2048]{1,0:T(8,128)(2,1)S(1)} %get-tuple-element.24), channel_id=1, source_target_pairs={{0,16},{16,0},{1,17},{17,1},{2,18},{18,2},{3,19},{19,3},{4,20},{20... | collective-permute-start | bytes 786440 | tf_op jit(solution)/shard_map/ppermute | solution.py:33
  (15 other events, 47.6 us)

commit v2 on v1

v2 whole, which is shorter than its diff:
```python
import functools

import jax
import jax.numpy as jnp
from jax import lax
from jax.experimental import pallas as pl
from jax.experimental.pallas import tpu as pltpu
from jax.sharding import PartitionSpec as P

F32, BF16 = jnp.float32, jnp.bfloat16
SWAPS = 1
ROWS_LAST = (((1,), (1,)), ((), ()))


def ring_chips(devices):
    depth = devices // 4
    return [2 * z for z in range(depth)] + [2 * z + 1 for z in reversed(range(depth))]


def ring_pairs(devices, by):
    chips = ring_chips(devices)
    count = len(chips)
    return [
        (2 * chip + core, 2 * chips[(place + by) % count] + core)
        for place, chip in enumerate(chips)
        for core in range(2)
    ]


def round_ring(shard, by):
    return lax.ppermute(shard, "expert", ring_pairs(lax.axis_size("expert"), by))


def across_cores(shards):
    devices = lax.axis_size("expert")
    return [lax.ppermute(s, "expert", [(i, i ^ 1) for i in range(devices)]) for s in shards]


def next_section(shard):
    sections = lax.axis_size("pipe")
    return lax.ppermute(shard, "pipe", [(i, (i + 1) % sections) for i in range(sections)])


def call(kernel, out_shapes, operands, after=(), grid=None, in_specs=None, out_specs=None,
         scratch=(), megabytes=16, flops=0):
    count = len(operands)

    def body(*refs):
        kernel(*refs[:count], *refs[count + len(after):])

    if in_specs is None:
        in_specs = [pl.BlockSpec(memory_space=pltpu.VMEM)] * count
    if out_specs is None:
        out_specs = [pl.BlockSpec(memory_space=pltpu.VMEM)] * len(out_shapes)
    return pl.pallas_call(
        body,
        out_shape=out_shapes,
        grid=grid or (),
        in_specs=list(in_specs) + [pl.BlockSpec(memory_space=pl.ANY)] * len(after),
        out_specs=out_specs,
        scratch_shapes=list(scratch),
        compiler_params=pltpu.CompilerParams(vmem_limit_bytes=megabytes * 2**20),
        cost_estimate=pl.CostEstimate(flops=int(flops), bytes_accessed=0, transcendentals=0),
    )(*operands, *after)


def prepare_kernel(*refs):
    sources, (low, high), held, arrived = refs[:4], refs[4:6], refs[6:10], refs[10]
    copies = [
        pltpu.make_async_copy(source, target, arrived.at[index])
        for index, (source, target) in enumerate(zip(sources, held))
    ]
    for copy in copies:
        copy.start()
    for copy in copies:
        copy.wait()
    tokens, gain, router, routes = held
    cut, width = high.shape
    experts = router.shape[0]
    wide = tokens[...].astype(F32)
    mean_square = jnp.mean(wide * wide, axis=-1, keepdims=True)
    normed = (wide * lax.rsqrt(mean_square + 1e-06) * gain[...]).astype(BF16)
    low[:, :width] = normed[:cut]
    high[...] = normed[cut:]
    logits = lax.dot_general(router[...], normed, ROWS_LAST, preferred_element_type=F32)
    score = jax.nn.sigmoid(logits)
    ids = lax.broadcasted_iota(jnp.int32, logits.shape, 0)
    named = ids == routes[0]
    for k in range(1, routes.shape[0]):
        named = named | (ids == routes[k])
    total = jnp.sum(jnp.where(named, score, 0.0), axis=0, keepdims=True)
    table = jnp.where(named, (score / total).astype(BF16).astype(F32), -1.0)
    rest = jnp.zeros((cut - experts, logits.shape[1]), F32)
    low[:, width:] = jnp.concatenate([table, rest], axis=0).astype(BF16)


def select_kernel(capacity, blocks, count, names, *refs):
    parts = refs[:count]
    own, info, others = refs[-2 - SWAPS], refs[-1 - SWAPS], refs[-SWAPS:]
    slots, width = own.shape
    tok_dev = parts[0].shape[1] - width
    both = tok_dev * blocks
    firsts = parts[:: len(parts) // blocks]
    table = jnp.concatenate([part[:, width:] for part in firsts], axis=1).astype(F32)
    ids = lax.broadcasted_iota(jnp.int32, table.shape, 0)
    first = jnp.sum(jnp.where(ids == names[0], table, 0.0), axis=0, keepdims=True)
    second = jnp.sum(jnp.where(ids == names[1], table, 0.0), axis=0, keepdims=True)
    line = lax.broadcasted_iota(jnp.int32, (8, both), 0)
    gates = jnp.where(line == 0, first, jnp.where(line == 1, second, -1.0))
    named = gates >= 0
    row = lax.broadcasted_iota(jnp.int32, (both, both), 0)
    column = lax.broadcasted_iota(jnp.int32, (both, both), 1)
    same = (row >= tok_dev) == (column >= tok_dev)
    earlier = jnp.where((row < column) & same, 1.0, 0.0).astype(BF16)
    ranks = jnp.dot(jnp.where(named, 1.0, 0.0).astype(BF16), earlier, preferred_element_type=F32)
    place = lax.broadcasted_iota(jnp.int32, (8, both), 1)
    ranks = jnp.where(place >= tok_dev, ranks + capacity, ranks)
    ranks = jnp.where(named, ranks, -1.0)
    slot = lax.broadcasted_iota(jnp.int32, (slots, both), 0).astype(F32)
    rows = jnp.concatenate([part[:, :width] for part in parts], axis=0)
    hits = jnp.where(slot == ranks[1:2], 1.0, 0.0).astype(BF16)
    span = width // SWAPS
    for index, other in enumerate(others):
        part = rows[:, index * span : (index + 1) * span]
        other[...] = jnp.dot(hits, part, preferred_element_type=F32).astype(BF16)
    hits = jnp.where(slot == ranks[0:1], 1.0, 0.0).astype(BF16)
    own[...] = jnp.dot(hits, rows, preferred_element_type=F32).astype(BF16)
    lines = jnp.where(line < 2, gates, pltpu.roll(ranks, 2, 0))
    spare = jnp.zeros((128 - 8, both), F32)
    info[...] = jnp.concatenate([lines, spare], axis=0).T


def ffn_kernel(tile, own, *refs):
    swapped, (gate, up, down), refs = refs[:SWAPS], refs[SWAPS : SWAPS + 3], refs[SWAPS + 3 :]
    own_out, swapped_outs, (rows, total) = refs[0], refs[1 : 1 + SWAPS], refs[1 + SWAPS :]
    slots, span = swapped[0].shape
    rows[:slots] = own[...]
    for index, part in enumerate(swapped):
        rows[slots:, index * span : (index + 1) * span] = part[...]

    def terms(step):
        columns = pl.ds(pl.multiple_of(step * tile, tile), tile)
        gate_part = jnp.dot(rows[...], gate[:, columns], preferred_element_type=F32)
        up_part = jnp.dot(rows[...], up[:, columns], preferred_element_type=F32)
        hidden = (gate_part / (1.0 + jnp.exp(-gate_part)) * up_part).astype(BF16)
        return jnp.dot(hidden, down[columns, :], preferred_element_type=F32)

    steps = gate.shape[1] // tile
    total[...] = terms(0)

    @pl.loop(1, steps - 1)
    def _(step):
        total[...] += terms(step)

    result = total[...] + terms(steps - 1)
    own_out[...] = result[:slots].astype(BF16)
    for index, target in enumerate(swapped_outs):
        target[...] = result[slots:, index * span : (index + 1) * span].astype(BF16)


def weights_of(info, begin, count, slots):
    block = info[begin : begin + count, :]
    slot = lax.broadcasted_iota(jnp.int32, (count, slots), 1).astype(F32)
    return [
        jnp.where(slot == block[:, 2 + e : 3 + e], block[:, e : e + 1], 0.0).astype(BF16)
        for e in range(2)
    ]


def expert_sum(begins, count, info, own_out, *other_out):
    slots = own_out.shape[0]
    weights = [weights_of(info, begin, count, slots) for begin in begins]
    own_weights = jnp.concatenate([w[0] for w in weights], axis=0)
    other_weights = jnp.concatenate([w[1] for w in weights], axis=0)
    return jnp.dot(own_weights, own_out[...], preferred_element_type=F32) + jnp.concatenate(
        [jnp.dot(other_weights, o[...], preferred_element_type=F32) for o in other_out], axis=1
    )


def own_kernel(*refs):
    outs, (tokens, low, high) = refs[:-3], refs[-3:]
    cut = low.shape[0]
    value = expert_sum((0,), 2 * cut, *outs) + tokens[...].astype(F32)
    low[...] = value[:cut]
    high[...] = value[cut:]


def final_kernel(mine, up, up_last, down, down_last, target):
    quarter = up_last.shape[0]
    for here, first, second in ((0, up_last, down), (quarter, up, down_last)):
        begin = quarter if first is up else 0
        value = mine[here : here + quarter, :] + first[begin : begin + quarter, :].astype(F32)
        begin = quarter if second is down else 0
        value += second[begin : begin + quarter, :].astype(F32)
        target[here : here + quarter, :] = value.astype(BF16)


def hop_kernel(begins, sums, *refs):
    size = 2 + SWAPS
    count = refs[-1].shape[0] // len(begins)
    came, targets = refs[size * len(begins) : -2], refs[-2:]
    for place, pair in enumerate(begins):
        part = expert_sum(pair, count, *refs[size * place : size * (place + 1)])
        for index, target in enumerate(targets):
            value = part[index * count : (index + 1) * count]
            here = pl.ds(place * count, count)
            if sums:
                value += came[index][here, :].astype(F32)
            target[here, :] = value.astype(target.dtype)


def shape(rows, columns, dtype=BF16):
    return jax.ShapeDtypeStruct((rows, columns), dtype)


def local(tokens, routes, norm_gain, router_weight, w_gate, w_up, w_down):
    rows = tokens[0]
    devices = lax.axis_size("expert")
    chips = devices // 2
    half = chips // 2
    tok_dev, top_count = routes.shape[1:]
    width = rows.shape[1]
    cut, quarter = tok_dev // 2, tok_dev // 4
    capacity = 3 * tok_dev * top_count // (2 * devices)
    device = lax.axis_index("expert")
    names = jnp.stack([device, device ^ 1]).astype(jnp.int32)
    gate, up, down = w_gate[0, 0], w_up[0, 0], w_down[0, 0]
    hidden = gate.shape[1]
    tile = 256 if hidden % 256 == 0 else hidden

    sources = [rows, norm_gain, router_weight[0].T, jnp.transpose(routes, (2, 0, 1))]
    own = call(
        prepare_kernel,
        [shape(cut, width + tok_dev), shape(cut, width)],
        sources,
        in_specs=[pl.BlockSpec(memory_space=pltpu.HBM)] * len(sources),
        scratch=[pltpu.VMEM(a.shape, a.dtype) for a in sources]
        + [pltpu.SemaphoreType.DMA((len(sources),))],
    )

    def select(parts, blocks, after, held=()):
        slots = -(-blocks * capacity // 16) * 16
        return call(
            functools.partial(select_kernel, capacity, blocks, len(parts)),
            [shape(slots, width), shape(blocks * tok_dev, 128, F32)]
            + [shape(slots, width // SWAPS)] * SWAPS,
            [names, *parts, *held],
            after,
            in_specs=[pl.BlockSpec(memory_space=pltpu.SMEM)]
            + [pl.BlockSpec(memory_space=pltpu.VMEM)] * (len(parts) + len(held)),
            flops=2e8 * blocks,
        )

    def ffn(own_rows, swapped_rows, after):
        slots = own_rows.shape[0]
        return call(
            functools.partial(ffn_kernel, tile),
            [shape(slots, width)] + [shape(slots, width // SWAPS)] * SWAPS,
            [own_rows, *swapped_rows, gate, up, down],
            after,
            scratch=[pltpu.VMEM((2 * slots, width), BF16), pltpu.VMEM((2 * slots, width), F32)],
            megabytes=24,
            flops=6e7 * slots,
        )

    def hop(number, high, came, after):
        far_group, near_group = half + 1 - number, half - number
        base = cut if high else 0

        def begins(group, first):
            offset = 0 if group == half else tok_dev
            return (base + first + offset, base + quarter - first)

        groups = [(far_group, begins(far_group, 0))]
        if near_group:
            groups.append((near_group, begins(near_group, quarter)))
        return call(
            functools.partial(hop_kernel, tuple(b for _, b in groups), bool(came)),
            [shape(quarter * len(groups), width)] * 2,
            [array for group, _ in groups for array in outs[group]] + list(came),
            after,
        )

    def send(pair):
        return [round_ring(pair[0], 1), round_ring(pair[1], -1)]

    ahead, behind = {0: own}, {0: own}
    for step in range(1, half):
        ahead[step] = [round_ring(part, 1) for part in ahead[step - 1]]
        behind[step] = [round_ring(part, -1) for part in behind[step - 1]]
    far = []
    for index in range(2):
        far.append(round_ring(ahead[half - 1][index][:quarter], 1))
        far.append(round_ring(behind[half - 1][index][quarter:], -1))

    parts = {k: ahead[k] + behind[k] for k in range(1, half)}
    parts[0], parts[half] = own, far
    picked, outs = {}, {}

    def run_select(k, *after):
        own_rows, info, *other_rows = select(
            parts[k], 1 if k in (0, half) else 2, after, [gate, up, down] if k == 0 else []
        )
        picked[k] = (own_rows, across_cores(other_rows), info)

    def run_ffn(k, *after):
        own_rows, swapped_rows, info = picked[k]
        own_out, *swapped_out = ffn(own_rows, swapped_rows, after)
        outs[k] = (info, own_out, *across_cores(swapped_out))

    def selected(k):
        return picked[k][2]

    def worked(k):
        return outs[k][1]

    run_select(0)
    run_ffn(0)
    for k in range(1, half):
        run_select(k)
    for k in range(1, half - 1):
        run_ffn(k, worked(k - 1))
    run_select(half, worked(half - 2))
    run_ffn(half - 1, selected(half))
    run_ffn(half, worked(half - 1))

    low_sums, high_sums, mine, last, kept = (), (), None, (), {}
    for number in range(1, half + 1):
        sums = hop(number, False, low_sums, last)
        last = (sums[0],)
        low_sums = send(sums)
        sums = hop(number, True, high_sums, last)
        last = (sums[0],)
        high_sums = send(sums)
        kept[number] = (low_sums, high_sums)
        if mine is None:
            mine = call(own_kernel, [shape(cut, width, F32)] * 2, [*outs[0], rows], last)
            last = (mine[0],)
    received = []
    for index in range(2):
        (up_last, down_last), (up, down) = kept[half][index], kept[half - 1][index]
        total = call(
            final_kernel, [shape(cut, width)], [mine[index], up, up_last, down, down_last]
        )
        received.append(next_section(total[0]))
    return jnp.concatenate(received, axis=0)[None]


def solution(mesh):
    return jax.shard_map(
        local,
        mesh=mesh,
        in_specs=(
            P("pipe", "expert", None),
            P("pipe", "expert", None),
            P("pipe", None),
            P("pipe", None, None),
            P("pipe", "expert", None, None),
            P("pipe", "expert", None, None),
            P("pipe", "expert", None, None),
        ),
        out_specs=P("pipe", "expert", None),
        check_vma=False,
    )
```

time: 178 us -> 121 us (0.68)
  matrix products: 54.8 us -> 0 us
  Pallas kernels: 0 us -> 24.4 us
  waiting for transfers between devices: 61.6 us -> 46.7 us
  local copies, waits for them, and re-layouts: 16 us -> 8.98 us
  other arithmetic: 4.89 us -> 0.92 us
    dot_general x23 -> x0, matrix products: 54.8 us -> none  [the longest x4 23.8 us: experts_out(): jnp.dot(hidden, w_down[0, 0], preferred_element_type=jnp.float32)]
    pallas_call x0 -> x22, Pallas kernels: none -> 24.4 us  [call(): pl.pallas_call(body, out_shape=out_shapes, grid=grid or (), in_specs=list...]
    ppermute x31 -> x32, waiting for transfers between devices: 53.4 us -> 38.4 us  [round_ring(): lax.ppermute(shard, 'expert', ring_pairs(lax.axis_size('expert'), by))]
    another operation x4 -> x0, local copies, waits for them, and re-layouts: 8.92 us -> none  [experts_out(): return jnp.stack([out[:pair_slots], across_cores(out[pair_slots:])])]
    unnamed x45 -> x22, local copies, waits for them, and re-layouts: 1.63 us -> 8.94 us
    squeeze x7 -> x0, local copies, waits for them, and re-layouts: 4.46 us -> none  [the longest x4 3.62 us: experts_out(): slot_rows = jnp.concatenate([taken[0], across_cores(taken[1])], axis=0)]
    convert_element_type x11 -> x0, other arithmetic: 2.26 us -> none  [the longest x1 1.23 us: local(): (wide_rows * lax.rsqrt(mean_square + 1e-06) * norm_gain[0]).astype(jnp.bf...]
    ppermute x31 -> x32, starting transfers between devices: 33.9 us -> 33.1 us  [round_ring(): lax.ppermute(shard, 'expert', ring_pairs(lax.axis_size('expert'), by))]
  transfers between devices with their start and end apart: 41 -> 44, of which waited for: 22 -> 22; matrix products, arithmetic and copies ran while one was open for 40% -> 0% of each run, Pallas kernels for 0% -> 20%
where the time goes in v2:
time: 121 us; the launch traced here: 119 us
  waiting for transfers between devices  46.7 us (39%)
  starting transfers between devices  38.2 us (32%)
  Pallas kernels  24.4 us (20%)
  local copies, waits for them, and re-layouts  8.98 us (7%)
    ppermute x32, waiting for transfers between devices, round_ring(): lax.ppermute(shard, 'expert', ring_pairs(lax.axis_size('expert'), by))  38.4 us
    ppermute x32, starting transfers between devices, round_ring(): lax.ppermute(shard, 'expert', ring_pairs(lax.axis_size('expert'), by))  33.1 us
    pallas_call x22, Pallas kernels, call(): pl.pallas_call(body, out_shape=out_shapes, grid=grid or (), in_specs=list...  24.4 us
    unnamed x22, local copies, waits for them, and re-layouts  8.94 us
    ppermute x2, waiting for transfers between devices, next_section(): lax.ppermute(shard, 'pipe', [(i, (i + 1) % sections) for i in range(secti...  7.26 us
    ppermute x2, starting transfers between devices, next_section(): lax.ppermute(shard, 'pipe', [(i, (i + 1) % sections) for i in range(secti...  3.18 us
  transfers between devices with their start and end apart: 44, of which 22 were waited for; matrix products, arithmetic and copies ran while one was open for 0% of the time, Pallas kernels for 20%

profile of v2, /device:TPU:10, one launch (start us, length us, event | category | flops | bytes accessed | tf_op | source)
XLA Modules:
  0.0 119.5 jit_solution(15673790512050122710)
XLA Ops:
  0.0 1.0 copy-done.6
  1.0 0.8 copy-done.8
  4.4 1.6 %collective-permute-start.6 = (bf16[64,2176]{1,0:T(8,128)(2,1)S(1)}, bf16[64,2176]{1,0:T(8,128)(2,1)S(1)}, u32[]{:S(2)}, u32[]{:S(2)}) collective-permute-start(bf16[64,2176]{1,0:T(8,128)(2,1)S(1)} %get-tuple-element.50.refs_1_), channel_id=1, source_target_pairs={{0,2},{1,3},{4,0},{5,1},{8,4},{9,5},{12,8},{13,9},{14,12},{15,13},... | collective-permute-start | bytes 835592 | tf_op jit(solution)/shard_map/ppermute | solution.py:31
  6.4 1.6 %collective-permute-start.14 = (bf16[64,2048]{1,0:T(8,128)(2,1)S(1)}, bf16[64,2048]{1,0:T(8,128)(2,1)S(1)}, u32[]{:S(2)}, u32[]{:S(2)}) collective-permute-start(bf16[64,2048]{1,0:T(8,128)(2,1)S(1)} %get-tuple-element.51.refs_2_), channel_id=1, source_target_pairs={{0,2},{1,3},{4,0},{5,1},{8,4},{9,5},{12,8},{13,9},{14,12},{15,13},... | collective-permute-start | bytes 786440 | tf_op jit(solution)/shard_map/ppermute | solution.py:31
  8.1 1.9 %copy-done = bf16[1,1,2048,768]{3,2,1,0:T(8,128)(2,1)S(1)} copy-done((bf16[1,1,2048,768]{3,2,1,0:T(8,128)(2,1)S(1)}, bf16[1,1,2048,768]{3,2,1,0:T(8,128)(2,1)}, u32[]{:S(2)}) %copy-start) | copy-done | bytes 3145752
  10.0 1.9 %copy-done.2 = bf16[1,1,2048,768]{3,2,1,0:T(8,128)(2,1)S(1)} copy-done((bf16[1,1,2048,768]{3,2,1,0:T(8,128)(2,1)S(1)}, bf16[1,1,2048,768]{3,2,1,0:T(8,128)(2,1)}, u32[]{:S(2)}) %copy-start.2) | copy-done | bytes 3145752
  11.8 1.9 %copy-done.4 = bf16[1,1,768,2048]{3,2,1,0:T(8,128)(2,1)S(1)} copy-done((bf16[1,1,768,2048]{3,2,1,0:T(8,128)(2,1)S(1)}, bf16[1,1,768,2048]{3,2,1,0:T(8,128)(2,1)}, u32[]{:S(2)}) %copy-start.4) | copy-done | bytes 3145752
  13.7 1.0 shard_map.74
  15.3 1.6 %collective-permute-start.7 = (bf16[64,2176]{1,0:T(8,128)(2,1)S(1)}, bf16[64,2176]{1,0:T(8,128)(2,1)S(1)}, u32[]{:S(2)}, u32[]{:S(2)}) collective-permute-start(bf16[64,2176]{1,0:T(8,128)(2,1)S(1)} %collective-permute-done.6.refs_3_), channel_id=1, source_target_pairs={{0,2},{1,3},{4,0},{5,1},{8,4},{9,5},{12,8},{13,9},{14,12},{15,13},... | collective-permute-start | bytes 835592 | tf_op jit(solution)/shard_map/ppermute | solution.py:31
  16.9 1.0 collective-permute-done.10.refs_2_
  18.4 1.6 %collective-permute-start.15 = (bf16[64,2048]{1,0:T(8,128)(2,1)S(1)}, bf16[64,2048]{1,0:T(8,128)(2,1)S(1)}, u32[]{:S(2)}, u32[]{:S(2)}) collective-permute-start(bf16[64,2048]{1,0:T(8,128)(2,1)S(1)} %collective-permute-done.14.refs_4_), channel_id=1, source_target_pairs={{0,2},{1,3},{4,0},{5,1},{8,4},{9,5},{12,8},{13,9},{14,12},{15,13},... | collective-permute-start | bytes 786440 | tf_op jit(solution)/shard_map/ppermute | solution.py:31
  20.0 1.2 shard_map.77
  21.2 8.3 %collective-permute-done.11.refs_2_ = bf16[64,2048]{1,0:T(8,128)(2,1)S(1)} collective-permute-done((bf16[64,2048]{1,0:T(8,128)(2,1)S(1)}, bf16[64,2048]{1,0:T(8,128)(2,1)S(1)}, u32[]{:S(2)}, u32[]{:S(2)}) %collective-permute-start.11) | collective-permute-done | bytes 262176 | tf_op jit(solution)/shard_map/ppermute | solution.py:31
  30.0 1.6 %collective-permute-start.16 = (bf16[64,2048]{1,0:T(8,128)(2,1)S(1)}, bf16[64,2048]{1,0:T(8,128)(2,1)S(1)}, u32[]{:S(2)}, u32[]{:S(2)}) collective-permute-start(bf16[64,2048]{1,0:T(8,128)(2,1)S(1)} %collective-permute-done.15.refs_4_), channel_id=1, source_target_pairs={{0,2},{1,3},{4,0},{5,1},{8,4},{9,5},{12,8},{13,9},{14,12},{15,13},... | collective-permute-start | bytes 786440 | tf_op jit(solution)/shard_map/ppermute | solution.py:31
  32.0 1.6 %collective-permute-start.8 = (bf16[64,2176]{1,0:T(8,128)(2,1)S(1)}, bf16[64,2176]{1,0:T(8,128)(2,1)S(1)}, u32[]{:S(2)}, u32[]{:S(2)}) collective-permute-start(bf16[64,2176]{1,0:T(8,128)(2,1)S(1)} %collective-permute-done.7.refs_3_), channel_id=1, source_target_pairs={{0,2},{1,3},{4,0},{5,1},{8,4},{9,5},{12,8},{13,9},{14,12},{15,13},... | collective-permute-start | bytes 835592 | tf_op jit(solution)/shard_map/ppermute | solution.py:31
  33.6 2.1 %shard_map.75 = (bf16[80,2048]{1,0:T(8,128)(2,1)S(1)}, bf16[80,2048]{1,0:T(8,128)(2,1)S(1)}) custom-call(bf16[80,2048]{1,0:T(8,128)(2,1)S(1)} %get-tuple-element.53.refs_0_, bf16[80,2048]{1,0:T(8,128)(2,1)S(1)} %collective-permute-done.refs_1_, bf16[2048,768]{1,0:T(8,128)(2,1)S(1)} %bitcast.13, bf16[2048,768]{1,0:T(8,128)(2,1)S(1)} %bitcast.19, ...), custom_call_target="tpu_custom_call" | custom-call | flops 4800000000 | tf_op jit(solution)/shard_map/pallas_call | solution.py:55
  35.7 1.2 shard_map.76
  36.9 1.9 %collective-permute-done.12.refs_2_ = bf16[64,2048]{1,0:T(8,128)(2,1)S(1)} collective-permute-done((bf16[64,2048]{1,0:T(8,128)(2,1)S(1)}, bf16[64,2048]{1,0:T(8,128)(2,1)S(1)}, u32[]{:S(2)}, u32[]{:S(2)}) %collective-permute-start.12) | collective-permute-done | bytes 262176 | tf_op jit(solution)/shard_map/ppermute | solution.py:31
  39.5 5.2 %collective-permute-done.4.refs_1_ = bf16[64,2176]{1,0:T(8,128)(2,1)S(1)} collective-permute-done((bf16[64,2176]{1,0:T(8,128)(2,1)S(1)}, bf16[64,2176]{1,0:T(8,128)(2,1)S(1)}, u32[]{:S(2)}, u32[]{:S(2)}) %collective-permute-start.4) | collective-permute-done | bytes 278560 | tf_op jit(solution)/shard_map/ppermute | solution.py:31
  44.7 1.6 %collective-permute-start.17 = (bf16[32,2048]{1,0:T(8,128)(2,1)S(1)}, bf16[32,2048]{1,0:T(8,128)(2,1)S(1)}, u32[]{:S(2)}, u32[]{:S(2)}) collective-permute-start(bf16[32,2048]{1,0:T(8,128)(2,1)S(1)} %slice.19), channel_id=1, source_target_pairs={{0,2},{1,3},{4,0},{5,1},{8,4},{9,5},{12,8},{13,9},{14,12},{15,13},... | collective-permute-start | bytes 393224 | tf_op jit(solution)/shard_map/ppermute | solution.py:31
  46.8 1.2 shard_map.81
  48.0 1.8 %collective-permute-start.9 = (bf16[32,2176]{1,0:T(8,128)(2,1)S(1)}, bf16[32,2176]{1,0:T(8,128)(2,1)S(1)}, u32[]{:S(2)}, u32[]{:S(2)}) collective-permute-start(bf16[32,2176]{1,0:T(8,128)(2,1)S(1)} %slice.17), channel_id=1, source_target_pairs={{0,2},{1,3},{4,0},{5,1},{8,4},{9,5},{12,8},{13,9},{14,12},{15,13},... | collective-permute-start | bytes 417800 | tf_op jit(solution)/shard_map/ppermute | solution.py:31
  49.8 3.2 %shard_map.78 = (bf16[144,2048]{1,0:T(8,128)(2,1)S(1)}, bf16[144,2048]{1,0:T(8,128)(2,1)S(1)}) custom-call(bf16[144,2048]{1,0:T(8,128)(2,1)S(1)} %get-tuple-element.59.refs_0_, bf16[144,2048]{1,0:T(8,128)(2,1)S(1)} %collective-permute-done.19.refs_1_, bf16[2048,768]{1,0:T(8,128)(2,1)S(1)} %bitcast.14, bf16[2048,768]{1,0:T(8,128)(2,1)S(1)} %bitcast.20, ...), custom_call_target="tpu_custom_call" | custom-call | flops 8640000000 | tf_op jit(solution)/shard_map/pallas_call | solution.py:55
  53.1 3.2 %shard_map.79 = (bf16[144,2048]{1,0:T(8,128)(2,1)S(1)}, bf16[144,2048]{1,0:T(8,128)(2,1)S(1)}) custom-call(bf16[144,2048]{1,0:T(8,128)(2,1)S(1)} %get-tuple-element.57.refs_0_, bf16[144,2048]{1,0:T(8,128)(2,1)S(1)} %collective-permute-done.18.refs_1_, bf16[2048,768]{1,0:T(8,128)(2,1)S(1)} %bitcast.15, bf16[2048,768]{1,0:T(8,128)(2,1)S(1)} %bitcast.21, ...), custom_call_target="tpu_custom_call" | custom-call | flops 8640000000 | tf_op jit(solution)/shard_map/pallas_call | solution.py:55
  56.4 1.0 shard_map.80
  58.1 3.2 %shard_map.82 = (bf16[144,2048]{1,0:T(8,128)(2,1)S(1)}, bf16[144,2048]{1,0:T(8,128)(2,1)S(1)}) custom-call(bf16[144,2048]{1,0:T(8,128)(2,1)S(1)} %get-tuple-element.66.refs_0_, bf16[144,2048]{1,0:T(8,128)(2,1)S(1)} %collective-permute-done.21.refs_1_, bf16[2048,768]{1,0:T(8,128)(2,1)S(1)} %bitcast.16, bf16[2048,768]{1,0:T(8,128)(2,1)S(1)} %bitcast.22, ...), custom_call_target="tpu_custom_call" | custom-call | flops 8640000000 | tf_op jit(solution)/shard_map/pallas_call | solution.py:55
  61.8 2.1 %shard_map.83 = (bf16[80,2048]{1,0:T(8,128)(2,1)S(1)}, bf16[80,2048]{1,0:T(8,128)(2,1)S(1)}) custom-call(bf16[80,2048]{1,0:T(8,128)(2,1)S(1)} %get-tuple-element.64.refs_0_, bf16[80,2048]{1,0:T(8,128)(2,1)S(1)} %collective-permute-done.20.refs_1_, bf16[2048,768]{1,0:T(8,128)(2,1)S(1)} %bitcast.17, bf16[2048,768]{1,0:T(8,128)(2,1)S(1)} %bitcast.23, ...), custom_call_target="tpu_custom_call" | custom-call | flops 4800000000 | tf_op jit(solution)/shard_map/pallas_call | solution.py:55
  64.6 1.0 collective-permute-done.22.refs_2_
  66.6 1.6 %collective-permute-start.27 = (bf16[64,2048]{1,0:T(8,128)(2,1)S(1)}, bf16[64,2048]{1,0:T(8,128)(2,1)S(1)}, u32[]{:S(2)}, u32[]{:S(2)}) collective-permute-start(bf16[64,2048]{1,0:T(8,128)(2,1)S(1)} %get-tuple-element.80), channel_id=1, source_target_pairs={{0,2},{1,3},{4,0},{5,1},{8,4},{9,5},{12,8},{13,9},{14,12},{15,13},... | collective-permute-start | bytes 786440 | tf_op jit(solution)/shard_map/ppermute | solution.py:31
  69.2 1.6 %collective-permute-start.31 = (bf16[64,2048]{1,0:T(8,128)(2,1)S(1)}, bf16[64,2048]{1,0:T(8,128)(2,1)S(1)}, u32[]{:S(2)}, u32[]{:S(2)}) collective-permute-start(bf16[64,2048]{1,0:T(8,128)(2,1)S(1)} %get-tuple-element.83), channel_id=1, source_target_pairs={{0,2},{1,3},{4,0},{5,1},{8,4},{9,5},{12,8},{13,9},{14,12},{15,13},... | collective-permute-start | bytes 786440 | tf_op jit(solution)/shard_map/ppermute | solution.py:31
  71.3 4.0 %collective-permute-done.26.refs_6_ = bf16[64,2048]{1,0:T(8,128)(2,1)S(1)} collective-permute-done((bf16[64,2048]{1,0:T(8,128)(2,1)S(1)}, bf16[64,2048]{1,0:T(8,128)(2,1)S(1)}, u32[]{:S(2)}, u32[]{:S(2)}) %collective-permute-start.26) | collective-permute-done | bytes 262176 | tf_op jit(solution)/shard_map/ppermute | solution.py:31
  76.8 1.6 %collective-permute-start.29 = (bf16[64,2048]{1,0:T(8,128)(2,1)S(1)}, bf16[64,2048]{1,0:T(8,128)(2,1)S(1)}, u32[]{:S(2)}, u32[]{:S(2)}) collective-permute-start(bf16[64,2048]{1,0:T(8,128)(2,1)S(1)} %get-tuple-element.82), channel_id=1, source_target_pairs={{0,2},{1,3},{4,0},{5,1},{8,4},{9,5},{12,8},{13,9},{14,12},{15,13},... | collective-permute-start | bytes 786440 | tf_op jit(solution)/shard_map/ppermute | solution.py:31
  78.4 2.5 %collective-permute-done.30.refs_6_ = bf16[64,2048]{1,0:T(8,128)(2,1)S(1)} collective-permute-done((bf16[64,2048]{1,0:T(8,128)(2,1)S(1)}, bf16[64,2048]{1,0:T(8,128)(2,1)S(1)}, u32[]{:S(2)}, u32[]{:S(2)}) %collective-permute-start.30) | collective-permute-done | bytes 262176 | tf_op jit(solution)/shard_map/ppermute | solution.py:31
  82.4 1.6 %collective-permute-start.35 = (bf16[64,2048]{1,0:T(8,128)(2,1)S(1)}, bf16[64,2048]{1,0:T(8,128)(2,1)S(1)}, u32[]{:S(2)}, u32[]{:S(2)}) collective-permute-start(bf16[64,2048]{1,0:T(8,128)(2,1)S(1)} %get-tuple-element.87), channel_id=1, source_target_pairs={{0,2},{1,3},{4,0},{5,1},{8,4},{9,5},{12,8},{13,9},{14,12},{15,13},... | collective-permute-start | bytes 786440 | tf_op jit(solution)/shard_map/ppermute | solution.py:31
  84.0 2.5 %collective-permute-done.28.refs_6_ = bf16[64,2048]{1,0:T(8,128)(2,1)S(1)} collective-permute-done((bf16[64,2048]{1,0:T(8,128)(2,1)S(1)}, bf16[64,2048]{1,0:T(8,128)(2,1)S(1)}, u32[]{:S(2)}, u32[]{:S(2)}) %collective-permute-start.28) | collective-permute-done | bytes 262176 | tf_op jit(solution)/shard_map/ppermute | solution.py:31
  88.1 1.6 %collective-permute-start.33 = (bf16[64,2048]{1,0:T(8,128)(2,1)S(1)}, bf16[64,2048]{1,0:T(8,128)(2,1)S(1)}, u32[]{:S(2)}, u32[]{:S(2)}) collective-permute-start(bf16[64,2048]{1,0:T(8,128)(2,1)S(1)} %get-tuple-element.86), channel_id=1, source_target_pairs={{0,2},{1,3},{4,0},{5,1},{8,4},{9,5},{12,8},{13,9},{14,12},{15,13},... | collective-permute-start | bytes 786440 | tf_op jit(solution)/shard_map/ppermute | solution.py:31
  89.6 2.5 %collective-permute-done.34.refs_6_ = bf16[64,2048]{1,0:T(8,128)(2,1)S(1)} collective-permute-done((bf16[64,2048]{1,0:T(8,128)(2,1)S(1)}, bf16[64,2048]{1,0:T(8,128)(2,1)S(1)}, u32[]{:S(2)}, u32[]{:S(2)}) %collective-permute-start.34) | collective-permute-done | bytes 262176 | tf_op jit(solution)/shard_map/ppermute | solution.py:31
  93.7 1.6 %collective-permute-start.40 = (bf16[64,2048]{1,0:T(8,128)(2,1)S(1)}, bf16[64,2048]{1,0:T(8,128)(2,1)S(1)}, u32[]{:S(2)}, u32[]{:S(2)}) collective-permute-start(bf16[64,2048]{1,0:T(8,128)(2,1)S(1)} %get-tuple-element.92), channel_id=1, source_target_pairs={{0,2},{1,3},{4,0},{5,1},{8,4},{9,5},{12,8},{13,9},{14,12},{15,13},... | collective-permute-start | bytes 786440 | tf_op jit(solution)/shard_map/ppermute | solution.py:31
  95.3 2.5 %collective-permute-done.32.refs_3_.refs_1_ = bf16[64,2048]{1,0:T(8,128)(2,1)S(1)} collective-permute-done((bf16[64,2048]{1,0:T(8,128)(2,1)S(1)}, bf16[64,2048]{1,0:T(8,128)(2,1)S(1)}, u32[]{:S(2)}, u32[]{:S(2)}) %collective-permute-start.32) | collective-permute-done | bytes 262176 | tf_op jit(solution)/shard_map/ppermute | solution.py:31
  99.1 1.6 %collective-permute-start.37 = (bf16[32,2048]{1,0:T(8,128)(2,1)S(1)}, bf16[32,2048]{1,0:T(8,128)(2,1)S(1)}, u32[]{:S(2)}, u32[]{:S(2)}) collective-permute-start(bf16[32,2048]{1,0:T(8,128)(2,1)S(1)} %get-tuple-element.90), channel_id=1, source_target_pairs={{0,2},{1,3},{4,0},{5,1},{8,4},{9,5},{12,8},{13,9},{14,12},{15,13},... | collective-permute-start | bytes 393224 | tf_op jit(solution)/shard_map/ppermute | solution.py:31
  100.7 2.7 %collective-permute-done.39.refs_3_.refs_1_ = bf16[64,2048]{1,0:T(8,128)(2,1)S(1)} collective-permute-done((bf16[64,2048]{1,0:T(8,128)(2,1)S(1)}, bf16[64,2048]{1,0:T(8,128)(2,1)S(1)}, u32[]{:S(2)}, u32[]{:S(2)}) %collective-permute-start.39) | collective-permute-done | bytes 262176 | tf_op jit(solution)/shard_map/ppermute | solution.py:31
  104.8 1.6 %collective-permute-start.42 = (bf16[32,2048]{1,0:T(8,128)(2,1)S(1)}, bf16[32,2048]{1,0:T(8,128)(2,1)S(1)}, u32[]{:S(2)}, u32[]{:S(2)}) collective-permute-start(bf16[32,2048]{1,0:T(8,128)(2,1)S(1)} %get-tuple-element.94), channel_id=1, source_target_pairs={{0,2},{1,3},{4,0},{5,1},{8,4},{9,5},{12,8},{13,9},{14,12},{15,13},... | collective-permute-start | bytes 393224 | tf_op jit(solution)/shard_map/ppermute | solution.py:31
  106.4 1.6 %collective-permute-start.38 = (bf16[64,2048]{1,0:T(8,128)(2,1)S(1)}, bf16[64,2048]{1,0:T(8,128)(2,1)S(1)}, u32[]{:S(2)}, u32[]{:S(2)}) collective-permute-start(bf16[64,2048]{1,0:T(8,128)(2,1)S(1)} %shard_map.92), channel_id=1, source_target_pairs={{0,16},{16,0},{1,17},{17,1},{2,18},{18,2},{3,19},{19,3},{4,20},{20... | collective-permute-start | bytes 786440 | tf_op jit(solution)/shard_map/ppermute | solution.py:41
  108.0 1.3 %collective-permute-done.41.refs_2_ = bf16[32,2048]{1,0:T(8,128)(2,1)S(1)} collective-permute-done((bf16[32,2048]{1,0:T(8,128)(2,1)S(1)}, bf16[32,2048]{1,0:T(8,128)(2,1)S(1)}, u32[]{:S(2)}, u32[]{:S(2)}) %collective-permute-start.41) | collective-permute-done | bytes 131104 | tf_op jit(solution)/shard_map/ppermute | solution.py:31
  109.8 1.6 %collective-permute-start.43 = (bf16[64,2048]{1,0:T(8,128)(2,1)S(1)}, bf16[64,2048]{1,0:T(8,128)(2,1)S(1)}, u32[]{:S(2)}, u32[]{:S(2)}) collective-permute-start(bf16[64,2048]{1,0:T(8,128)(2,1)S(1)} %shard_map.94), channel_id=1, source_target_pairs={{0,16},{16,0},{1,17},{17,1},{2,18},{18,2},{3,19},{19,3},{4,20},{20... | collective-permute-start | bytes 786440 | tf_op jit(solution)/shard_map/ppermute | solution.py:41
  111.4 4.3 %collective-permute-done.38 = bf16[64,2048]{1,0:T(8,128)(2,1)S(1)} collective-permute-done((bf16[64,2048]{1,0:T(8,128)(2,1)S(1)}, bf16[64,2048]{1,0:T(8,128)(2,1)S(1)}, u32[]{:S(2)}, u32[]{:S(2)}) %collective-permute-start.38) | collective-permute-done | bytes 262176 | tf_op jit(solution)/shard_map/ppermute | solution.py:41
  115.7 2.9 %collective-permute-done.43 = bf16[64,2048]{1,0:T(8,128)(2,1)S(1)} collective-permute-done((bf16[64,2048]{1,0:T(8,128)(2,1)S(1)}, bf16[64,2048]{1,0:T(8,128)(2,1)S(1)}, u32[]{:S(2)}, u32[]{:S(2)}) %collective-permute-start.43) | collective-permute-done | bytes 262176 | tf_op jit(solution)/shard_map/ppermute | solution.py:41
  118.7 0.8 maximum_bitcast_fusion
  (90 shorter events, 20.0 us)
Async XLA Ops:
  3.9 10.9 %collective-permute-start.2 = (bf16[64,2176]{1,0:T(8,128)(2,1)S(1)}, bf16[64,2176]{1,0:T(8,128)(2,1)S(1)}, u32[]{:S(2)}, u32[]{:S(2)}) collective-permute-start(bf16[64,2176]{1,0:T(8,128)(2,1)S(1)} %get-tuple-element.50.refs_1_), channel_id=1, source_target_pairs={{0,4},{1,5},{4,8},{5,9},{8,12},{9,13},{12,14},{13,15},{14,10},{15,... | collective-permute-start | bytes 835592 | tf_op jit(solution)/shard_map/ppermute | solution.py:31
  4.4 10.9 %collective-permute-start.6 = (bf16[64,2176]{1,0:T(8,128)(2,1)S(1)}, bf16[64,2176]{1,0:T(8,128)(2,1)S(1)}, u32[]{:S(2)}, u32[]{:S(2)}) collective-permute-start(bf16[64,2176]{1,0:T(8,128)(2,1)S(1)} %get-tuple-element.50.refs_1_), channel_id=1, source_target_pairs={{0,2},{1,3},{4,0},{5,1},{8,4},{9,5},{12,8},{13,9},{14,12},{15,13},... | collective-permute-start | bytes 835592 | tf_op jit(solution)/shard_map/ppermute | solution.py:31
  6.0 12.0 %collective-permute-start.10 = (bf16[64,2048]{1,0:T(8,128)(2,1)S(1)}, bf16[64,2048]{1,0:T(8,128)(2,1)S(1)}, u32[]{:S(2)}, u32[]{:S(2)}) collective-permute-start(bf16[64,2048]{1,0:T(8,128)(2,1)S(1)} %get-tuple-element.51.refs_2_), channel_id=1, source_target_pairs={{0,4},{1,5},{4,8},{5,9},{8,12},{9,13},{12,14},{13,15},{14,10},{15,... | collective-permute-start | bytes 786440 | tf_op jit(solution)/shard_map/ppermute | solution.py:31
  6.4 12.0 %collective-permute-start.14 = (bf16[64,2048]{1,0:T(8,128)(2,1)S(1)}, bf16[64,2048]{1,0:T(8,128)(2,1)S(1)}, u32[]{:S(2)}, u32[]{:S(2)}) collective-permute-start(bf16[64,2048]{1,0:T(8,128)(2,1)S(1)} %get-tuple-element.51.refs_2_), channel_id=1, source_target_pairs={{0,2},{1,3},{4,0},{5,1},{8,4},{9,5},{12,8},{13,9},{14,12},{15,13},... | collective-permute-start | bytes 786440 | tf_op jit(solution)/shard_map/ppermute | solution.py:31
  13.7 19.9 %copy-start.1 = (bf16[1,1,2048,768]{3,2,1,0:T(8,128)(2,1)S(1)}, bf16[1,1,2048,768]{3,2,1,0:T(8,128)(2,1)}, u32[]{:S(2)}) copy-start(bf16[1,1,2048,768]{3,2,1,0:T(8,128)(2,1)} %param.11) | copy-start | bytes 9437188
  13.7 19.9 %copy-start.3 = (bf16[1,1,2048,768]{3,2,1,0:T(8,128)(2,1)S(1)}, bf16[1,1,2048,768]{3,2,1,0:T(8,128)(2,1)}, u32[]{:S(2)}) copy-start(bf16[1,1,2048,768]{3,2,1,0:T(8,128)(2,1)} %param.12) | copy-start | bytes 9437188
  13.7 19.9 %copy-start.5 = (bf16[1,1,768,2048]{3,2,1,0:T(8,128)(2,1)S(1)}, bf16[1,1,768,2048]{3,2,1,0:T(8,128)(2,1)}, u32[]{:S(2)}) copy-start(bf16[1,1,768,2048]{3,2,1,0:T(8,128)(2,1)} %param.13) | copy-start | bytes 9437188
  14.7 6.4 %collective-permute-start = (bf16[80,2048]{1,0:T(8,128)(2,1)S(1)}, bf16[80,2048]{1,0:T(8,128)(2,1)S(1)}, u32[]{:S(2)}, u32[]{:S(2)}) collective-permute-start(bf16[80,2048]{1,0:T(8,128)(2,1)S(1)} %get-tuple-element.54), channel_id=1, source_target_pairs={{0,1},{1,0},{2,3},{3,2},{4,5},{5,4},{6,7},{7,6},{8,9},{9,8},{10,11... | collective-permute-start | bytes 983048 | tf_op jit(solution)/shard_map/ppermute | solution.py:36
  14.8 16.7 %collective-permute-start.3 = (bf16[64,2176]{1,0:T(8,128)(2,1)S(1)}, bf16[64,2176]{1,0:T(8,128)(2,1)S(1)}, u32[]{:S(2)}, u32[]{:S(2)}) collective-permute-start(bf16[64,2176]{1,0:T(8,128)(2,1)S(1)} %collective-permute-done.2.refs_1_), channel_id=1, source_target_pairs={{0,4},{1,5},{4,8},{5,9},{8,12},{9,13},{12,14},{13,15},{14,10},{15,... | collective-permute-start | bytes 835592 | tf_op jit(solution)/shard_map/ppermute | solution.py:31
  15.3 16.7 %collective-permute-start.7 = (bf16[64,2176]{1,0:T(8,128)(2,1)S(1)}, bf16[64,2176]{1,0:T(8,128)(2,1)S(1)}, u32[]{:S(2)}, u32[]{:S(2)}) collective-permute-start(bf16[64,2176]{1,0:T(8,128)(2,1)S(1)} %collective-permute-done.6.refs_3_), channel_id=1, source_target_pairs={{0,2},{1,3},{4,0},{5,1},{8,4},{9,5},{12,8},{13,9},{14,12},{15,13},... | collective-permute-start | bytes 835592 | tf_op jit(solution)/shard_map/ppermute | solution.py:31
  18.0 11.6 %collective-permute-start.11 = (bf16[64,2048]{1,0:T(8,128)(2,1)S(1)}, bf16[64,2048]{1,0:T(8,128)(2,1)S(1)}, u32[]{:S(2)}, u32[]{:S(2)}) collective-permute-start(bf16[64,2048]{1,0:T(8,128)(2,1)S(1)} %collective-permute-done.10.refs_2_), channel_id=1, source_target_pairs={{0,4},{1,5},{4,8},{5,9},{8,12},{9,13},{12,14},{13,15},{14,10},{15,... | collective-permute-start | bytes 786440 | tf_op jit(solution)/shard_map/ppermute | solution.py:31
  18.4 11.6 %collective-permute-start.15 = (bf16[64,2048]{1,0:T(8,128)(2,1)S(1)}, bf16[64,2048]{1,0:T(8,128)(2,1)S(1)}, u32[]{:S(2)}, u32[]{:S(2)}) collective-permute-start(bf16[64,2048]{1,0:T(8,128)(2,1)S(1)} %collective-permute-done.14.refs_4_), channel_id=1, source_target_pairs={{0,2},{1,3},{4,0},{5,1},{8,4},{9,5},{12,8},{13,9},{14,12},{15,13},... | collective-permute-start | bytes 786440 | tf_op jit(solution)/shard_map/ppermute | solution.py:31
  21.2 26.9 %collective-permute-start.19 = (bf16[144,2048]{1,0:T(8,128)(2,1)S(1)}, bf16[144,2048]{1,0:T(8,128)(2,1)S(1)}, u32[]{:S(2)}, u32[]{:S(2)}) collective-permute-start(bf16[144,2048]{1,0:T(8,128)(2,1)S(1)} %get-tuple-element.60), channel_id=1, source_target_pairs={{0,1},{1,0},{2,3},{3,2},{4,5},{5,4},{6,7},{7,6},{8,9},{9,8},{10,11... | collective-permute-start | bytes 1769480 | tf_op jit(solution)/shard_map/ppermute | solution.py:36
  29.5 9.2 %collective-permute-start.12 = (bf16[64,2048]{1,0:T(8,128)(2,1)S(1)}, bf16[64,2048]{1,0:T(8,128)(2,1)S(1)}, u32[]{:S(2)}, u32[]{:S(2)}) collective-permute-start(bf16[64,2048]{1,0:T(8,128)(2,1)S(1)} %collective-permute-done.11.refs_2_), channel_id=1, source_target_pairs={{0,4},{1,5},{4,8},{5,9},{8,12},{9,13},{12,14},{13,15},{14,10},{15,... | collective-permute-start | bytes 786440 | tf_op jit(solution)/shard_map/ppermute | solution.py:31
  30.0 9.2 %collective-permute-start.16 = (bf16[64,2048]{1,0:T(8,128)(2,1)S(1)}, bf16[64,2048]{1,0:T(8,128)(2,1)S(1)}, u32[]{:S(2)}, u32[]{:S(2)}) collective-permute-start(bf16[64,2048]{1,0:T(8,128)(2,1)S(1)} %collective-permute-done.15.refs_4_), channel_id=1, source_target_pairs={{0,2},{1,3},{4,0},{5,1},{8,4},{9,5},{12,8},{13,9},{14,12},{15,13},... | collective-permute-start | bytes 786440 | tf_op jit(solution)/shard_map/ppermute | solution.py:31
  31.6 13.2 %collective-permute-start.4 = (bf16[64,2176]{1,0:T(8,128)(2,1)S(1)}, bf16[64,2176]{1,0:T(8,128)(2,1)S(1)}, u32[]{:S(2)}, u32[]{:S(2)}) collective-permute-start(bf16[64,2176]{1,0:T(8,128)(2,1)S(1)} %collective-permute-done.3.refs_1_), channel_id=1, source_target_pairs={{0,4},{1,5},{4,8},{5,9},{8,12},{9,13},{12,14},{13,15},{14,10},{15,... | collective-permute-start | bytes 835592 | tf_op jit(solution)/shard_map/ppermute | solution.py:31
  32.0 14.3 %collective-permute-start.8 = (bf16[64,2176]{1,0:T(8,128)(2,1)S(1)}, bf16[64,2176]{1,0:T(8,128)(2,1)S(1)}, u32[]{:S(2)}, u32[]{:S(2)}) collective-permute-start(bf16[64,2176]{1,0:T(8,128)(2,1)S(1)} %collective-permute-done.7.refs_3_), channel_id=1, source_target_pairs={{0,2},{1,3},{4,0},{5,1},{8,4},{9,5},{12,8},{13,9},{14,12},{15,13},... | collective-permute-start | bytes 835592 | tf_op jit(solution)/shard_map/ppermute | solution.py:31
  38.8 14.3 %collective-permute-start.18 = (bf16[144,2048]{1,0:T(8,128)(2,1)S(1)}, bf16[144,2048]{1,0:T(8,128)(2,1)S(1)}, u32[]{:S(2)}, u32[]{:S(2)}) collective-permute-start(bf16[144,2048]{1,0:T(8,128)(2,1)S(1)} %get-tuple-element.58), channel_id=1, source_target_pairs={{0,1},{1,0},{2,3},{3,2},{4,5},{5,4},{6,7},{7,6},{8,9},{9,8},{10,11... | collective-permute-start | bytes 1769480 | tf_op jit(solution)/shard_map/ppermute | solution.py:36
  39.2 17.1 %collective-permute-start.13 = (bf16[32,2048]{1,0:T(8,128)(2,1)S(1)}, bf16[32,2048]{1,0:T(8,128)(2,1)S(1)}, u32[]{:S(2)}, u32[]{:S(2)}) collective-permute-start(bf16[32,2048]{1,0:T(8,128)(2,1)S(1)} %slice.18), channel_id=1, source_target_pairs={{0,4},{1,5},{4,8},{5,9},{8,12},{9,13},{12,14},{13,15},{14,10},{15,... | collective-permute-start | bytes 393224 | tf_op jit(solution)/shard_map/ppermute | solution.py:31
  44.7 11.7 %collective-permute-start.17 = (bf16[32,2048]{1,0:T(8,128)(2,1)S(1)}, bf16[32,2048]{1,0:T(8,128)(2,1)S(1)}, u32[]{:S(2)}, u32[]{:S(2)}) collective-permute-start(bf16[32,2048]{1,0:T(8,128)(2,1)S(1)} %slice.19), channel_id=1, source_target_pairs={{0,2},{1,3},{4,0},{5,1},{8,4},{9,5},{12,8},{13,9},{14,12},{15,13},... | collective-permute-start | bytes 393224 | tf_op jit(solution)/shard_map/ppermute | solution.py:31
  46.3 10.1 %collective-permute-start.5 = (bf16[32,2176]{1,0:T(8,128)(2,1)S(1)}, bf16[32,2176]{1,0:T(8,128)(2,1)S(1)}, u32[]{:S(2)}, u32[]{:S(2)}) collective-permute-start(bf16[32,2176]{1,0:T(8,128)(2,1)S(1)} %slice.16), channel_id=1, source_target_pairs={{0,4},{1,5},{4,8},{5,9},{8,12},{9,13},{12,14},{13,15},{14,10},{15,... | collective-permute-start | bytes 417800 | tf_op jit(solution)/shard_map/ppermute | solution.py:31
  48.0 8.4 %collective-permute-start.9 = (bf16[32,2176]{1,0:T(8,128)(2,1)S(1)}, bf16[32,2176]{1,0:T(8,128)(2,1)S(1)}, u32[]{:S(2)}, u32[]{:S(2)}) collective-permute-start(bf16[32,2176]{1,0:T(8,128)(2,1)S(1)} %slice.17), channel_id=1, source_target_pairs={{0,2},{1,3},{4,0},{5,1},{8,4},{9,5},{12,8},{13,9},{14,12},{15,13},... | collective-permute-start | bytes 417800 | tf_op jit(solution)/shard_map/ppermute | solution.py:31
  53.1 5.0 %collective-permute-start.21 = (bf16[144,2048]{1,0:T(8,128)(2,1)S(1)}, bf16[144,2048]{1,0:T(8,128)(2,1)S(1)}, u32[]{:S(2)}, u32[]{:S(2)}) collective-permute-start(bf16[144,2048]{1,0:T(8,128)(2,1)S(1)} %get-tuple-element.67), channel_id=1, source_target_pairs={{0,1},{1,0},{2,3},{3,2},{4,5},{5,4},{6,7},{7,6},{8,9},{9,8},{10,11... | collective-permute-start | bytes 1769480 | tf_op jit(solution)/shard_map/ppermute | solution.py:36
  57.4 4.4 %collective-permute-start.20 = (bf16[80,2048]{1,0:T(8,128)(2,1)S(1)}, bf16[80,2048]{1,0:T(8,128)(2,1)S(1)}, u32[]{:S(2)}, u32[]{:S(2)}) collective-permute-start(bf16[80,2048]{1,0:T(8,128)(2,1)S(1)} %get-tuple-element.65), channel_id=1, source_target_pairs={{0,1},{1,0},{2,3},{3,2},{4,5},{5,4},{6,7},{7,6},{8,9},{9,8},{10,11... | collective-permute-start | bytes 983048 | tf_op jit(solution)/shard_map/ppermute | solution.py:36
  58.0 11.2 %collective-permute-start.24 = (bf16[144,2048]{1,0:T(8,128)(2,1)S(1)}, bf16[144,2048]{1,0:T(8,128)(2,1)S(1)}, u32[]{:S(2)}, u32[]{:S(2)}) collective-permute-start(bf16[144,2048]{1,0:T(8,128)(2,1)S(1)} %get-tuple-element.77), channel_id=1, source_target_pairs={{0,1},{1,0},{2,3},{3,2},{4,5},{5,4},{6,7},{7,6},{8,9},{9,8},{10,11... | collective-permute-start | bytes 1769480 | tf_op jit(solution)/shard_map/ppermute | solution.py:36
  61.3 4.3 %collective-permute-start.23 = (bf16[144,2048]{1,0:T(8,128)(2,1)S(1)}, bf16[144,2048]{1,0:T(8,128)(2,1)S(1)}, u32[]{:S(2)}, u32[]{:S(2)}) collective-permute-start(bf16[144,2048]{1,0:T(8,128)(2,1)S(1)} %get-tuple-element.72), channel_id=1, source_target_pairs={{0,1},{1,0},{2,3},{3,2},{4,5},{5,4},{6,7},{7,6},{8,9},{9,8},{10,11... | collective-permute-start | bytes 1769480 | tf_op jit(solution)/shard_map/ppermute | solution.py:36
  63.9 6.9 %copy-start.7 = (bf16[1,128,2048]{2,1,0:T(8,128)(2,1)S(1)}, bf16[1,128,2048]{2,1,0:T(8,128)(2,1)}, u32[]{:S(2)}) copy-start(bf16[1,128,2048]{2,1,0:T(8,128)(2,1)} %param.7) | copy-start | bytes 1572868
  63.9 1.7 %collective-permute-start.22 = (bf16[80,2048]{1,0:T(8,128)(2,1)S(1)}, bf16[80,2048]{1,0:T(8,128)(2,1)S(1)}, u32[]{:S(2)}, u32[]{:S(2)}) collective-permute-start(bf16[80,2048]{1,0:T(8,128)(2,1)S(1)} %get-tuple-element.70), channel_id=1, source_target_pairs={{0,1},{1,0},{2,3},{3,2},{4,5},{5,4},{6,7},{7,6},{8,9},{9,8},{10,11... | collective-permute-start | bytes 983048 | tf_op jit(solution)/shard_map/ppermute | solution.py:36
  64.0 4.6 %collective-permute-start.1 = (bf16[80,2048]{1,0:T(8,128)(2,1)S(1)}, bf16[80,2048]{1,0:T(8,128)(2,1)S(1)}, u32[]{:S(2)}, u32[]{:S(2)}) collective-permute-start(bf16[80,2048]{1,0:T(8,128)(2,1)S(1)} %get-tuple-element.56), channel_id=1, source_target_pairs={{0,1},{1,0},{2,3},{3,2},{4,5},{5,4},{6,7},{7,6},{8,9},{9,8},{10,11... | collective-permute-start | bytes 983048 | tf_op jit(solution)/shard_map/ppermute | solution.py:36
  64.5 19.6 %collective-permute-start.25 = (bf16[144,2048]{1,0:T(8,128)(2,1)S(1)}, bf16[144,2048]{1,0:T(8,128)(2,1)S(1)}, u32[]{:S(2)}, u32[]{:S(2)}) collective-permute-start(bf16[144,2048]{1,0:T(8,128)(2,1)S(1)} %get-tuple-element.79), channel_id=1, source_target_pairs={{0,1},{1,0},{2,3},{3,2},{4,5},{5,4},{6,7},{7,6},{8,9},{9,8},{10,11... | collective-permute-start | bytes 1769480 | tf_op jit(solution)/shard_map/ppermute | solution.py:36
  66.1 9.2 %collective-permute-start.26 = (bf16[64,2048]{1,0:T(8,128)(2,1)S(1)}, bf16[64,2048]{1,0:T(8,128)(2,1)S(1)}, u32[]{:S(2)}, u32[]{:S(2)}) collective-permute-start(bf16[64,2048]{1,0:T(8,128)(2,1)S(1)} %get-tuple-element.73.refs_6_), channel_id=1, source_target_pairs={{0,4},{1,5},{4,8},{5,9},{8,12},{9,13},{12,14},{13,15},{14,10},{15,... | collective-permute-start | bytes 786440 | tf_op jit(solution)/shard_map/ppermute | solution.py:31
  66.6 9.2 %collective-permute-start.27 = (bf16[64,2048]{1,0:T(8,128)(2,1)S(1)}, bf16[64,2048]{1,0:T(8,128)(2,1)S(1)}, u32[]{:S(2)}, u32[]{:S(2)}) collective-permute-start(bf16[64,2048]{1,0:T(8,128)(2,1)S(1)} %get-tuple-element.80), channel_id=1, source_target_pairs={{0,2},{1,3},{4,0},{5,1},{8,4},{9,5},{12,8},{13,9},{14,12},{15,13},... | collective-permute-start | bytes 786440 | tf_op jit(solution)/shard_map/ppermute | solution.py:31
  68.7 12.2 %collective-permute-start.30 = (bf16[64,2048]{1,0:T(8,128)(2,1)S(1)}, bf16[64,2048]{1,0:T(8,128)(2,1)S(1)}, u32[]{:S(2)}, u32[]{:S(2)}) collective-permute-start(bf16[64,2048]{1,0:T(8,128)(2,1)S(1)} %get-tuple-element.74.refs_4_), channel_id=1, source_target_pairs={{0,4},{1,5},{4,8},{5,9},{8,12},{9,13},{12,14},{13,15},{14,10},{15,... | collective-permute-start | bytes 786440 | tf_op jit(solution)/shard_map/ppermute | solution.py:31
  69.2 12.2 %collective-permute-start.31 = (bf16[64,2048]{1,0:T(8,128)(2,1)S(1)}, bf16[64,2048]{1,0:T(8,128)(2,1)S(1)}, u32[]{:S(2)}, u32[]{:S(2)}) collective-permute-start(bf16[64,2048]{1,0:T(8,128)(2,1)S(1)} %get-tuple-element.83), channel_id=1, source_target_pairs={{0,2},{1,3},{4,0},{5,1},{8,4},{9,5},{12,8},{13,9},{14,12},{15,13},... | collective-permute-start | bytes 786440 | tf_op jit(solution)/shard_map/ppermute | solution.py:31
  76.3 10.2 %collective-permute-start.28 = (bf16[64,2048]{1,0:T(8,128)(2,1)S(1)}, bf16[64,2048]{1,0:T(8,128)(2,1)S(1)}, u32[]{:S(2)}, u32[]{:S(2)}) collective-permute-start(bf16[64,2048]{1,0:T(8,128)(2,1)S(1)} %get-tuple-element.81.refs_8_), channel_id=1, source_target_pairs={{0,4},{1,5},{4,8},{5,9},{8,12},{9,13},{12,14},{13,15},{14,10},{15,... | collective-permute-start | bytes 786440 | tf_op jit(solution)/shard_map/ppermute | solution.py:31
  76.8 10.2 %collective-permute-start.29 = (bf16[64,2048]{1,0:T(8,128)(2,1)S(1)}, bf16[64,2048]{1,0:T(8,128)(2,1)S(1)}, u32[]{:S(2)}, u32[]{:S(2)}) collective-permute-start(bf16[64,2048]{1,0:T(8,128)(2,1)S(1)} %get-tuple-element.82), channel_id=1, source_target_pairs={{0,2},{1,3},{4,0},{5,1},{8,4},{9,5},{12,8},{13,9},{14,12},{15,13},... | collective-permute-start | bytes 786440 | tf_op jit(solution)/shard_map/ppermute | solution.py:31
  81.9 10.2 %collective-permute-start.34 = (bf16[64,2048]{1,0:T(8,128)(2,1)S(1)}, bf16[64,2048]{1,0:T(8,128)(2,1)S(1)}, u32[]{:S(2)}, u32[]{:S(2)}) collective-permute-start(bf16[64,2048]{1,0:T(8,128)(2,1)S(1)} %get-tuple-element.84.refs_8_), channel_id=1, source_target_pairs={{0,4},{1,5},{4,8},{5,9},{8,12},{9,13},{12,14},{13,15},{14,10},{15,... | collective-permute-start | bytes 786440 | tf_op jit(solution)/shard_map/ppermute | solution.py:31
  82.4 10.2 %collective-permute-start.35 = (bf16[64,2048]{1,0:T(8,128)(2,1)S(1)}, bf16[64,2048]{1,0:T(8,128)(2,1)S(1)}, u32[]{:S(2)}, u32[]{:S(2)}) collective-permute-start(bf16[64,2048]{1,0:T(8,128)(2,1)S(1)} %get-tuple-element.87), channel_id=1, source_target_pairs={{0,2},{1,3},{4,0},{5,1},{8,4},{9,5},{12,8},{13,9},{14,12},{15,13},... | collective-permute-start | bytes 786440 | tf_op jit(solution)/shard_map/ppermute | solution.py:31
  87.6 10.2 %collective-permute-start.32 = (bf16[64,2048]{1,0:T(8,128)(2,1)S(1)}, bf16[64,2048]{1,0:T(8,128)(2,1)S(1)}, u32[]{:S(2)}, u32[]{:S(2)}) collective-permute-start(bf16[64,2048]{1,0:T(8,128)(2,1)S(1)} %get-tuple-element.85.refs_8_), channel_id=1, source_target_pairs={{0,4},{1,5},{4,8},{5,9},{8,12},{9,13},{12,14},{13,15},{14,10},{15,... | collective-permute-start | bytes 786440 | tf_op jit(solution)/shard_map/ppermute | solution.py:31
  88.1 10.2 %collective-permute-start.33 = (bf16[64,2048]{1,0:T(8,128)(2,1)S(1)}, bf16[64,2048]{1,0:T(8,128)(2,1)S(1)}, u32[]{:S(2)}, u32[]{:S(2)}) collective-permute-start(bf16[64,2048]{1,0:T(8,128)(2,1)S(1)} %get-tuple-element.86), channel_id=1, source_target_pairs={{0,2},{1,3},{4,0},{5,1},{8,4},{9,5},{12,8},{13,9},{14,12},{15,13},... | collective-permute-start | bytes 786440 | tf_op jit(solution)/shard_map/ppermute | solution.py:31
  93.2 10.2 %collective-permute-start.39 = (bf16[64,2048]{1,0:T(8,128)(2,1)S(1)}, bf16[64,2048]{1,0:T(8,128)(2,1)S(1)}, u32[]{:S(2)}, u32[]{:S(2)}) collective-permute-start(bf16[64,2048]{1,0:T(8,128)(2,1)S(1)} %get-tuple-element.88.refs_5_), channel_id=1, source_target_pairs={{0,4},{1,5},{4,8},{5,9},{8,12},{9,13},{12,14},{13,15},{14,10},{15,... | collective-permute-start | bytes 786440 | tf_op jit(solution)/shard_map/ppermute | solution.py:31
  93.7 10.2 %collective-permute-start.40 = (bf16[64,2048]{1,0:T(8,128)(2,1)S(1)}, bf16[64,2048]{1,0:T(8,128)(2,1)S(1)}, u32[]{:S(2)}, u32[]{:S(2)}) collective-permute-start(bf16[64,2048]{1,0:T(8,128)(2,1)S(1)} %get-tuple-element.92), channel_id=1, source_target_pairs={{0,2},{1,3},{4,0},{5,1},{8,4},{9,5},{12,8},{13,9},{14,12},{15,13},... | collective-permute-start | bytes 786440 | tf_op jit(solution)/shard_map/ppermute | solution.py:31
  98.6 7.7 %collective-permute-start.36 = (bf16[32,2048]{1,0:T(8,128)(2,1)S(1)}, bf16[32,2048]{1,0:T(8,128)(2,1)S(1)}, u32[]{:S(2)}, u32[]{:S(2)}) collective-permute-start(bf16[32,2048]{1,0:T(8,128)(2,1)S(1)} %get-tuple-element.89.refs_5_), channel_id=1, source_target_pairs={{0,4},{1,5},{4,8},{5,9},{8,12},{9,13},{12,14},{13,15},{14,10},{15,... | collective-permute-start | bytes 393224 | tf_op jit(solution)/shard_map/ppermute | solution.py:31
  99.1 7.2 %collective-permute-start.37 = (bf16[32,2048]{1,0:T(8,128)(2,1)S(1)}, bf16[32,2048]{1,0:T(8,128)(2,1)S(1)}, u32[]{:S(2)}, u32[]{:S(2)}) collective-permute-start(bf16[32,2048]{1,0:T(8,128)(2,1)S(1)} %get-tuple-element.90), channel_id=1, source_target_pairs={{0,2},{1,3},{4,0},{5,1},{8,4},{9,5},{12,8},{13,9},{14,12},{15,13},... | collective-permute-start | bytes 393224 | tf_op jit(solution)/shard_map/ppermute | solution.py:31
  104.3 5.0 %collective-permute-start.41 = (bf16[32,2048]{1,0:T(8,128)(2,1)S(1)}, bf16[32,2048]{1,0:T(8,128)(2,1)S(1)}, u32[]{:S(2)}, u32[]{:S(2)}) collective-permute-start(bf16[32,2048]{1,0:T(8,128)(2,1)S(1)} %get-tuple-element.93), channel_id=1, source_target_pairs={{0,4},{1,5},{4,8},{5,9},{8,12},{9,13},{12,14},{13,15},{14,10},{15,... | collective-permute-start | bytes 393224 | tf_op jit(solution)/shard_map/ppermute | solution.py:31
  104.8 5.0 %collective-permute-start.42 = (bf16[32,2048]{1,0:T(8,128)(2,1)S(1)}, bf16[32,2048]{1,0:T(8,128)(2,1)S(1)}, u32[]{:S(2)}, u32[]{:S(2)}) collective-permute-start(bf16[32,2048]{1,0:T(8,128)(2,1)S(1)} %get-tuple-element.94), channel_id=1, source_target_pairs={{0,2},{1,3},{4,0},{5,1},{8,4},{9,5},{12,8},{13,9},{14,12},{15,13},... | collective-permute-start | bytes 393224 | tf_op jit(solution)/shard_map/ppermute | solution.py:31
  106.4 9.3 %collective-permute-start.38 = (bf16[64,2048]{1,0:T(8,128)(2,1)S(1)}, bf16[64,2048]{1,0:T(8,128)(2,1)S(1)}, u32[]{:S(2)}, u32[]{:S(2)}) collective-permute-start(bf16[64,2048]{1,0:T(8,128)(2,1)S(1)} %shard_map.92), channel_id=1, source_target_pairs={{0,16},{16,0},{1,17},{17,1},{2,18},{18,2},{3,19},{19,3},{4,20},{20... | collective-permute-start | bytes 786440 | tf_op jit(solution)/shard_map/ppermute | solution.py:41
  109.8 8.9 %collective-permute-start.43 = (bf16[64,2048]{1,0:T(8,128)(2,1)S(1)}, bf16[64,2048]{1,0:T(8,128)(2,1)S(1)}, u32[]{:S(2)}, u32[]{:S(2)}) collective-permute-start(bf16[64,2048]{1,0:T(8,128)(2,1)S(1)} %shard_map.94), channel_id=1, source_target_pairs={{0,16},{16,0},{1,17},{17,1},{2,18},{18,2},{3,19},{19,3},{4,20},{20... | collective-permute-start | bytes 786440 | tf_op jit(solution)/shard_map/ppermute | solution.py:41
  (7 other events, 8.9 us)

commit v3 on v2

--- a/solution.py
+++ b/solution.py
@@ -42,7 +42,7 @@
 
 
 def call(kernel, out_shapes, operands, after=(), grid=None, in_specs=None, out_specs=None,
-         scratch=(), megabytes=16, flops=0):
+         scratch=(), megabytes=16, flops=0, name=None):
     count = len(operands)
 
     def body(*refs):
@@ -54,6 +54,7 @@
         out_specs = [pl.BlockSpec(memory_space=pltpu.VMEM)] * len(out_shapes)
     return pl.pallas_call(
         body,
+        name=name,
         out_shape=out_shapes,
         grid=grid or (),
         in_specs=list(in_specs) + [pl.BlockSpec(memory_space=pl.ANY)] * len(after),
@@ -75,7 +76,7 @@
     for copy in copies:
         copy.wait()
     tokens, gain, router, routes = held
-    cut, width = high.shape
+    cut, width = low.shape[0], tokens.shape[1]
     experts = router.shape[0]
     wide = tokens[...].astype(F32)
     mean_square = jnp.mean(wide * wide, axis=-1, keepdims=True)
@@ -185,6 +186,10 @@
     high[...] = value[cut:]
 
 
+def tie(array, *tokens):
+    return lax.optimization_barrier((array, *tokens))[0]
+
+
 def final_kernel(mine, up, up_last, down, down_last, target):
     quarter = up_last.shape[0]
     for here, first, second in ((0, up_last, down), (quarter, up, down_last)):
@@ -233,9 +238,11 @@
         prepare_kernel,
         [shape(cut, width + tok_dev), shape(cut, width)],
         sources,
+        name="prepare",
         in_specs=[pl.BlockSpec(memory_space=pltpu.HBM)] * len(sources),
         scratch=[pltpu.VMEM(a.shape, a.dtype) for a in sources]
         + [pltpu.SemaphoreType.DMA((len(sources),))],
+        megabytes=56,
     )
 
     def select(parts, blocks, after, held=()):
@@ -249,6 +256,7 @@
             in_specs=[pl.BlockSpec(memory_space=pltpu.SMEM)]
             + [pl.BlockSpec(memory_space=pltpu.VMEM)] * (len(parts) + len(held)),
             flops=2e8 * blocks,
+            name=f"select{blocks}",
         )
 
     def ffn(own_rows, swapped_rows, after):
@@ -261,6 +269,7 @@
             scratch=[pltpu.VMEM((2 * slots, width), BF16), pltpu.VMEM((2 * slots, width), F32)],
             megabytes=24,
             flops=6e7 * slots,
+            name=f"ffn{1 + (slots > 100)}",
         )
 
     def hop(number, high, came, after):
@@ -279,23 +288,13 @@
             [shape(quarter * len(groups), width)] * 2,
             [array for group, _ in groups for array in outs[group]] + list(came),
             after,
+            name="hop",
         )
 
     def send(pair):
         return [round_ring(pair[0], 1), round_ring(pair[1], -1)]
 
-    ahead, behind = {0: own}, {0: own}
-    for step in range(1, half):
-        ahead[step] = [round_ring(part, 1) for part in ahead[step - 1]]
-        behind[step] = [round_ring(part, -1) for part in behind[step - 1]]
-    far = []
-    for index in range(2):
-        far.append(round_ring(ahead[half - 1][index][:quarter], 1))
-        far.append(round_ring(behind[half - 1][index][quarter:], -1))
-
-    parts = {k: ahead[k] + behind[k] for k in range(1, half)}
-    parts[0], parts[half] = own, far
-    picked, outs = {}, {}
+    picked, outs, parts = {}, {}, {0: own}
 
     def run_select(k, *after):
         own_rows, info, *other_rows = select(
@@ -316,10 +315,21 @@
 
     run_select(0)
     run_ffn(0)
+    ahead, behind = list(own), list(own)
     for k in range(1, half):
-        run_select(k)
-    for k in range(1, half - 1):
-        run_ffn(k, worked(k - 1))
+        ahead = [round_ring(part, 1) for part in ahead]
+        behind = [round_ring(part, -1) for part in behind]
+        parts[k] = ahead + behind
+        run_select(k, *(picked[k - 1][1] if k > 1 else []))
+        if k < half - 1:
+            run_ffn(k, worked(k - 1))
+    early = (worked(half - 3), *picked[half - 2][1])
+    ahead[0], behind[0] = tie(ahead[0], *early), tie(behind[0], *early)
+    far = []
+    for index in range(2):
+        far.append(round_ring(ahead[index][:quarter], 1))
+        far.append(round_ring(behind[index][quarter:], -1))
+    parts[half] = far
     run_select(half, worked(half - 2))
     run_ffn(half - 1, selected(half))
     run_ffn(half, worked(half - 1))
@@ -334,13 +344,13 @@
         high_sums = send(sums)
         kept[number] = (low_sums, high_sums)
         if mine is None:
-            mine = call(own_kernel, [shape(cut, width, F32)] * 2, [*outs[0], rows], last)
+            mine = call(own_kernel, [shape(cut, width, F32)] * 2, [*outs[0], rows], last, name="mine")
             last = (mine[0],)
     received = []
     for index in range(2):
         (up_last, down_last), (up, down) = kept[half][index], kept[half - 1][index]
         total = call(
-            final_kernel, [shape(cut, width)], [mine[index], up, up_last, down, down_last]
+            final_kernel, [shape(cut, width)], [mine[index], up, up_last, down, down_last], name="final"
         )
         received.append(next_section(total[0]))
     return jnp.concatenate(received, axis=0)[None]

time: 121 us -> 116 us (0.959)
  waiting for transfers between devices: 46.7 us -> 40.9 us
  Pallas kernels: 24.4 us -> 26 us
  local copies, waits for them, and re-layouts: 8.98 us -> 7.63 us
    ppermute x32, waiting for transfers between devices: 38.4 us -> 32.9 us  [round_ring(): lax.ppermute(shard, 'expert', ring_pairs(lax.axis_size('expert'), by))]
    pallas_call x22, Pallas kernels: 24.4 us -> 26 us  [call(): pl.pallas_call(body, name=name, out_shape=out_shapes, grid=grid or (), in...]
    unnamed x22 -> x18, local copies, waits for them, and re-layouts: 8.94 us -> 7.59 us
  transfers between devices with their start and end apart: 44 -> 44, of which waited for: 22 -> 22; matrix products, arithmetic and copies ran while one was open for 0% -> 0% of each run, Pallas kernels for 20% -> 21%
where the time goes in v3:
time: 116 us; the launch traced here: 114 us
  waiting for transfers between devices  40.9 us (35%)
  starting transfers between devices  38.5 us (33%)
  Pallas kernels  26 us (22%)
  local copies, waits for them, and re-layouts  7.63 us (7%)
    ppermute x32, starting transfers between devices, round_ring(): lax.ppermute(shard, 'expert', ring_pairs(lax.axis_size('expert'), by))  33.2 us
    ppermute x32, waiting for transfers between devices, round_ring(): lax.ppermute(shard, 'expert', ring_pairs(lax.axis_size('expert'), by))  32.9 us
    pallas_call x22, Pallas kernels, call(): pl.pallas_call(body, name=name, out_shape=out_shapes, grid=grid or (), in...  26 us
    unnamed x18, local copies, waits for them, and re-layouts  7.59 us
    ppermute x2, waiting for transfers between devices, next_section(): lax.ppermute(shard, 'pipe', [(i, (i + 1) % sections) for i in range(secti...  7 us
    ppermute x2, starting transfers between devices, next_section(): lax.ppermute(shard, 'pipe', [(i, (i + 1) % sections) for i in range(secti...  3.18 us
  transfers between devices with their start and end apart: 44, of which 22 were waited for; matrix products, arithmetic and copies ran while one was open for 0% of the time, Pallas kernels for 21%

profile of v3, /device:TPU:10, one launch (start us, length us, event | category | flops | bytes accessed | tf_op | source)
XLA Modules:
  0.0 114.2 jit_solution(7554122378106163919)
XLA Ops:
  0.0 2.2 %prepare.1 = (bf16[64,2176]{1,0:T(8,128)(2,1)}, bf16[64,2048]{1,0:T(8,128)(2,1)}) custom-call(bf16[128,2048]{1,0:T(8,128)(2,1)} %bitcast.30, f32[1,2048]{1,0:T(1,128)} %refs_1_.1, bf16[16,2048]{1,0:T(8,128)(2,1)} %bitcast.32, s32[6,1,128]{2,1,0:T(1,128)} %bitcast.33), custom_call_target="tpu_custom_call" | custom-call | tf_op jit(solution)/shard_map/prepare/pallas_call | solution.py:55
  2.2 1.6 %collective-permute-start.7 = (bf16[64,2048]{1,0:T(8,128)(2,1)}, bf16[64,2048]{1,0:T(8,128)(2,1)S(1)}, u32[]{:S(2)}, u32[]{:S(2)}) collective-permute-start(bf16[64,2048]{1,0:T(8,128)(2,1)} %get-tuple-element.53.refs_2_), channel_id=1, source_target_pairs={{0,2},{1,3},{4,0},{5,1},{8,4},{9,5},{12,8},{13,9},{14,12},{15,13},... | collective-permute-start | bytes 786440 | tf_op jit(solution)/shard_map/ppermute | solution.py:31
  4.3 1.6 %collective-permute-start.6 = (bf16[64,2176]{1,0:T(8,128)(2,1)}, bf16[64,2176]{1,0:T(8,128)(2,1)S(1)}, u32[]{:S(2)}, u32[]{:S(2)}) collective-permute-start(bf16[64,2176]{1,0:T(8,128)(2,1)} %get-tuple-element.52.refs_1_), channel_id=1, source_target_pairs={{0,2},{1,3},{4,0},{5,1},{8,4},{9,5},{12,8},{13,9},{14,12},{15,13},... | collective-permute-start | bytes 835592 | tf_op jit(solution)/shard_map/ppermute | solution.py:31
  6.4 1.9 %copy-done = bf16[1,1,2048,768]{3,2,1,0:T(8,128)(2,1)S(1)} copy-done((bf16[1,1,2048,768]{3,2,1,0:T(8,128)(2,1)S(1)}, bf16[1,1,2048,768]{3,2,1,0:T(8,128)(2,1)}, u32[]{:S(2)}) %copy-start) | copy-done | bytes 3145752
  8.3 1.9 %copy-done.2 = bf16[1,1,2048,768]{3,2,1,0:T(8,128)(2,1)S(1)} copy-done((bf16[1,1,2048,768]{3,2,1,0:T(8,128)(2,1)S(1)}, bf16[1,1,2048,768]{3,2,1,0:T(8,128)(2,1)}, u32[]{:S(2)}) %copy-start.2) | copy-done | bytes 3145752
  10.2 1.9 %copy-done.4 = bf16[1,1,768,2048]{3,2,1,0:T(8,128)(2,1)S(1)} copy-done((bf16[1,1,768,2048]{3,2,1,0:T(8,128)(2,1)S(1)}, bf16[1,1,768,2048]{3,2,1,0:T(8,128)(2,1)}, u32[]{:S(2)}) %copy-start.4) | copy-done | bytes 3145752
  15.1 1.6 %collective-permute-start.11 = (bf16[64,2048]{1,0:T(8,128)(2,1)S(1)}, bf16[64,2048]{1,0:T(8,128)(2,1)S(1)}, u32[]{:S(2)}, u32[]{:S(2)}) collective-permute-start(bf16[64,2048]{1,0:T(8,128)(2,1)S(1)} %collective-permute-done.7.refs_4_), channel_id=1, source_target_pairs={{0,2},{1,3},{4,0},{5,1},{8,4},{9,5},{12,8},{13,9},{14,12},{15,13},... | collective-permute-start | bytes 786440 | tf_op jit(solution)/shard_map/ppermute | solution.py:31
  17.8 1.2 %select2.3 = (bf16[144,2048]{1,0:T(8,128)(2,1)S(1)}, f32[256,128]{1,0:T(8,128)S(1)}, bf16[144,2048]{1,0:T(8,128)(2,1)S(1)}) custom-call(s32[2]{0:T(128)S(1)} %pad_add_fusion.refs_0_, bf16[64,2176]{1,0:T(8,128)(2,1)S(1)} %collective-permute-done.2.refs_1_, bf16[64,2048]{1,0:T(8,128)(2,1)S(1)} %collective-permute-done.5.refs_2_, ...), custom_call_target="tpu_custom_call" | custom-call | flops 400000000 | tf_op jit(solution)/shard_map/select2/pallas_call | solution.py:55
  19.1 1.6 %collective-permute-start.10 = (bf16[64,2176]{1,0:T(8,128)(2,1)S(1)}, bf16[64,2176]{1,0:T(8,128)(2,1)S(1)}, u32[]{:S(2)}, u32[]{:S(2)}) collective-permute-start(bf16[64,2176]{1,0:T(8,128)(2,1)S(1)} %collective-permute-done.6.refs_3_), channel_id=1, source_target_pairs={{0,2},{1,3},{4,0},{5,1},{8,4},{9,5},{12,8},{13,9},{14,12},{15,13},... | collective-permute-start | bytes 835592 | tf_op jit(solution)/shard_map/ppermute | solution.py:31
  21.1 3.1 %collective-permute-done.11.refs_4_ = bf16[64,2048]{1,0:T(8,128)(2,1)S(1)} collective-permute-done((bf16[64,2048]{1,0:T(8,128)(2,1)S(1)}, bf16[64,2048]{1,0:T(8,128)(2,1)S(1)}, u32[]{:S(2)}, u32[]{:S(2)}) %collective-permute-start.11) | collective-permute-done | bytes 262176 | tf_op jit(solution)/shard_map/ppermute | solution.py:31
  24.3 1.6 %collective-permute-start.18 = (bf16[64,2048]{1,0:T(8,128)(2,1)S(1)}, bf16[64,2048]{1,0:T(8,128)(2,1)S(1)}, u32[]{:S(2)}, u32[]{:S(2)}) collective-permute-start(bf16[64,2048]{1,0:T(8,128)(2,1)S(1)} %collective-permute-done.11.refs_4_), channel_id=1, source_target_pairs={{0,2},{1,3},{4,0},{5,1},{8,4},{9,5},{12,8},{13,9},{14,12},{15,13},... | collective-permute-start | bytes 786440 | tf_op jit(solution)/shard_map/ppermute | solution.py:31
  26.3 2.1 %ffn1.2 = (bf16[80,2048]{1,0:T(8,128)(2,1)S(1)}, bf16[80,2048]{1,0:T(8,128)(2,1)S(1)}) custom-call(bf16[80,2048]{1,0:T(8,128)(2,1)S(1)} %get-tuple-element.55.refs_0_, bf16[80,2048]{1,0:T(8,128)(2,1)S(1)} %collective-permute-done.refs_1_, bf16[2048,768]{1,0:T(8,128)(2,1)S(1)} %bitcast.13, bf16[2048,768]{1,0:T(8,128)(2,1)S(1)} %bitcast.19, ...), custom_call_target="tpu_custom_call" | custom-call | flops 4800000000 | tf_op jit(solution)/shard_map/ffn1/pallas_call | solution.py:55
  28.4 1.8 %collective-permute-done.10.refs_3_ = bf16[64,2176]{1,0:T(8,128)(2,1)S(1)} collective-permute-done((bf16[64,2176]{1,0:T(8,128)(2,1)S(1)}, bf16[64,2176]{1,0:T(8,128)(2,1)S(1)}, u32[]{:S(2)}, u32[]{:S(2)}) %collective-permute-start.10) | collective-permute-done | bytes 278560 | tf_op jit(solution)/shard_map/ppermute | solution.py:31
  30.2 1.6 %collective-permute-start.14 = (bf16[64,2176]{1,0:T(8,128)(2,1)S(1)}, bf16[64,2176]{1,0:T(8,128)(2,1)S(1)}, u32[]{:S(2)}, u32[]{:S(2)}) collective-permute-start(bf16[64,2176]{1,0:T(8,128)(2,1)S(1)} %collective-permute-done.10.refs_3_), channel_id=1, source_target_pairs={{0,2},{1,3},{4,0},{5,1},{8,4},{9,5},{12,8},{13,9},{14,12},{15,13},... | collective-permute-start | bytes 835592 | tf_op jit(solution)/shard_map/ppermute | solution.py:31
  32.3 3.5 %collective-permute-done.18.refs_4_ = bf16[64,2048]{1,0:T(8,128)(2,1)S(1)} collective-permute-done((bf16[64,2048]{1,0:T(8,128)(2,1)S(1)}, bf16[64,2048]{1,0:T(8,128)(2,1)S(1)}, u32[]{:S(2)}, u32[]{:S(2)}) %collective-permute-start.18) | collective-permute-done | bytes 262176 | tf_op jit(solution)/shard_map/ppermute | solution.py:31
  35.9 1.6 %collective-permute-start.19 = (bf16[32,2048]{1,0:T(8,128)(2,1)S(1)}, bf16[32,2048]{1,0:T(8,128)(2,1)S(1)}, u32[]{:S(2)}, u32[]{:S(2)}) collective-permute-start(bf16[32,2048]{1,0:T(8,128)(2,1)S(1)} %slice.17), channel_id=1, source_target_pairs={{0,2},{1,3},{4,0},{5,1},{8,4},{9,5},{12,8},{13,9},{14,12},{15,13},... | collective-permute-start | bytes 393224 | tf_op jit(solution)/shard_map/ppermute | solution.py:31
  38.0 1.2 %select2.4 = (bf16[144,2048]{1,0:T(8,128)(2,1)S(1)}, f32[256,128]{1,0:T(8,128)S(1)}, bf16[144,2048]{1,0:T(8,128)(2,1)S(1)}) custom-call(s32[2]{0:T(128)S(1)} %pad_add_fusion.refs_0_, bf16[64,2176]{1,0:T(8,128)(2,1)S(1)} %collective-permute-done.3.refs_1_, bf16[64,2048]{1,0:T(8,128)(2,1)S(1)} %collective-permute-done.9.refs_2_, ...), custom_call_target="tpu_custom_call" | custom-call | flops 400000000 | tf_op jit(solution)/shard_map/select2/pallas_call | solution.py:55
  39.3 3.2 %ffn2.3 = (bf16[144,2048]{1,0:T(8,128)(2,1)S(1)}, bf16[144,2048]{1,0:T(8,128)(2,1)S(1)}) custom-call(bf16[144,2048]{1,0:T(8,128)(2,1)S(1)} %get-tuple-element.59.refs_0_, bf16[144,2048]{1,0:T(8,128)(2,1)S(1)} %collective-permute-done.8.refs_1_.refs_5_, bf16[2048,768]{1,0:T(8,128)(2,1)S(1)} %bitcast.14, bf16[2048,768]{1,0:T(8,128)(2,1)S(1)} %bitcast.20, ...), custom_call_target="tpu_custom_call" | custom-call | flops 8640000000 | tf_op jit(solution)/shard_map/ffn2/pallas_call | solution.py:55
  43.5 1.6 %collective-permute-start.15 = (bf16[32,2176]{1,0:T(8,128)(2,1)S(1)}, bf16[32,2176]{1,0:T(8,128)(2,1)S(1)}, u32[]{:S(2)}, u32[]{:S(2)}) collective-permute-start(bf16[32,2176]{1,0:T(8,128)(2,1)S(1)} %slice.13), channel_id=1, source_target_pairs={{0,2},{1,3},{4,0},{5,1},{8,4},{9,5},{12,8},{13,9},{14,12},{15,13},... | collective-permute-start | bytes 417800 | tf_op jit(solution)/shard_map/ppermute | solution.py:31
  45.5 1.2 %select2.5 = (bf16[144,2048]{1,0:T(8,128)(2,1)S(1)}, f32[256,128]{1,0:T(8,128)S(1)}, bf16[144,2048]{1,0:T(8,128)(2,1)S(1)}) custom-call(s32[2]{0:T(128)S(1)} %pad_add_fusion.refs_0_, bf16[64,2176]{1,0:T(8,128)(2,1)S(1)} %collective-permute-done.4.refs_1_, bf16[64,2048]{1,0:T(8,128)(2,1)S(1)} %collective-permute-done.16.refs_2_, ...), custom_call_target="tpu_custom_call" | custom-call | flops 400000000 | tf_op jit(solution)/shard_map/select2/pallas_call | solution.py:55
  46.8 3.2 %ffn2.4 = (bf16[144,2048]{1,0:T(8,128)(2,1)S(1)}, bf16[144,2048]{1,0:T(8,128)(2,1)S(1)}) custom-call(bf16[144,2048]{1,0:T(8,128)(2,1)S(1)} %get-tuple-element.65.refs_0_, bf16[144,2048]{1,0:T(8,128)(2,1)S(1)} %collective-permute-done.12.refs_1_.refs_5_, bf16[2048,768]{1,0:T(8,128)(2,1)S(1)} %bitcast.15, bf16[2048,768]{1,0:T(8,128)(2,1)S(1)} %bitcast.21, ...), custom_call_target="tpu_custom_call" | custom-call | flops 8640000000 | tf_op jit(solution)/shard_map/ffn2/pallas_call | solution.py:55
  51.7 3.2 %ffn2.5 = (bf16[144,2048]{1,0:T(8,128)(2,1)S(1)}, bf16[144,2048]{1,0:T(8,128)(2,1)S(1)}) custom-call(bf16[144,2048]{1,0:T(8,128)(2,1)S(1)} %get-tuple-element.70.refs_0_, bf16[144,2048]{1,0:T(8,128)(2,1)S(1)} %collective-permute-done.21.refs_1_, bf16[2048,768]{1,0:T(8,128)(2,1)S(1)} %bitcast.16, bf16[2048,768]{1,0:T(8,128)(2,1)S(1)} %bitcast.22, ...), custom_call_target="tpu_custom_call" | custom-call | flops 8640000000 | tf_op jit(solution)/shard_map/ffn2/pallas_call | solution.py:55
  55.5 2.1 %ffn1.3 = (bf16[80,2048]{1,0:T(8,128)(2,1)S(1)}, bf16[80,2048]{1,0:T(8,128)(2,1)S(1)}) custom-call(bf16[80,2048]{1,0:T(8,128)(2,1)S(1)} %get-tuple-element.68.refs_0_, bf16[80,2048]{1,0:T(8,128)(2,1)S(1)} %collective-permute-done.20.refs_1_, bf16[2048,768]{1,0:T(8,128)(2,1)S(1)} %bitcast.17, bf16[2048,768]{1,0:T(8,128)(2,1)S(1)} %bitcast.23, ...), custom_call_target="tpu_custom_call" | custom-call | flops 4800000000 | tf_op jit(solution)/shard_map/ffn1/pallas_call | solution.py:55
  59.8 1.6 %collective-permute-start.27 = (bf16[64,2048]{1,0:T(8,128)(2,1)S(1)}, bf16[64,2048]{1,0:T(8,128)(2,1)S(1)}, u32[]{:S(2)}, u32[]{:S(2)}) collective-permute-start(bf16[64,2048]{1,0:T(8,128)(2,1)S(1)} %get-tuple-element.84), channel_id=1, source_target_pairs={{0,2},{1,3},{4,0},{5,1},{8,4},{9,5},{12,8},{13,9},{14,12},{15,13},... | collective-permute-start | bytes 786440 | tf_op jit(solution)/shard_map/ppermute | solution.py:31
  62.4 1.6 %collective-permute-start.31 = (bf16[64,2048]{1,0:T(8,128)(2,1)S(1)}, bf16[64,2048]{1,0:T(8,128)(2,1)S(1)}, u32[]{:S(2)}, u32[]{:S(2)}) collective-permute-start(bf16[64,2048]{1,0:T(8,128)(2,1)S(1)} %get-tuple-element.87), channel_id=1, source_target_pairs={{0,2},{1,3},{4,0},{5,1},{8,4},{9,5},{12,8},{13,9},{14,12},{15,13},... | collective-permute-start | bytes 786440 | tf_op jit(solution)/shard_map/ppermute | solution.py:31
  65.0 4.0 %collective-permute-done.27.refs_7_ = bf16[64,2048]{1,0:T(8,128)(2,1)S(1)} collective-permute-done((bf16[64,2048]{1,0:T(8,128)(2,1)S(1)}, bf16[64,2048]{1,0:T(8,128)(2,1)S(1)}, u32[]{:S(2)}, u32[]{:S(2)}) %collective-permute-start.27) | collective-permute-done | bytes 262176 | tf_op jit(solution)/shard_map/ppermute | solution.py:31
  69.0 1.6 %collective-permute-done.26.refs_6_ = bf16[64,2048]{1,0:T(8,128)(2,1)S(1)} collective-permute-done((bf16[64,2048]{1,0:T(8,128)(2,1)S(1)}, bf16[64,2048]{1,0:T(8,128)(2,1)S(1)}, u32[]{:S(2)}, u32[]{:S(2)}) %collective-permute-start.26) | collective-permute-done | bytes 262176 | tf_op jit(solution)/shard_map/ppermute | solution.py:31
  71.9 1.3 %collective-permute-start.28 = (bf16[64,2048]{1,0:T(8,128)(2,1)S(1)}, bf16[64,2048]{1,0:T(8,128)(2,1)S(1)}, u32[]{:S(2)}, u32[]{:S(2)}) collective-permute-start(bf16[64,2048]{1,0:T(8,128)(2,1)S(1)} %get-tuple-element.85.refs_8_), channel_id=1, source_target_pairs={{0,4},{1,5},{4,8},{5,9},{8,12},{9,13},{12,14},{13,15},{14,10},{15,... | collective-permute-start | bytes 786440 | tf_op jit(solution)/shard_map/ppermute | solution.py:31
  73.2 1.4 %collective-permute-done.31.refs_7_ = bf16[64,2048]{1,0:T(8,128)(2,1)S(1)} collective-permute-done((bf16[64,2048]{1,0:T(8,128)(2,1)S(1)}, bf16[64,2048]{1,0:T(8,128)(2,1)S(1)}, u32[]{:S(2)}, u32[]{:S(2)}) %collective-permute-start.31) | collective-permute-done | bytes 262176 | tf_op jit(solution)/shard_map/ppermute | solution.py:31
  74.6 1.6 %collective-permute-done.30.refs_6_ = bf16[64,2048]{1,0:T(8,128)(2,1)S(1)} collective-permute-done((bf16[64,2048]{1,0:T(8,128)(2,1)S(1)}, bf16[64,2048]{1,0:T(8,128)(2,1)S(1)}, u32[]{:S(2)}, u32[]{:S(2)}) %collective-permute-start.30) | collective-permute-done | bytes 262176 | tf_op jit(solution)/shard_map/ppermute | solution.py:31
  77.5 1.3 %collective-permute-start.34 = (bf16[64,2048]{1,0:T(8,128)(2,1)S(1)}, bf16[64,2048]{1,0:T(8,128)(2,1)S(1)}, u32[]{:S(2)}, u32[]{:S(2)}) collective-permute-start(bf16[64,2048]{1,0:T(8,128)(2,1)S(1)} %get-tuple-element.88.refs_8_), channel_id=1, source_target_pairs={{0,4},{1,5},{4,8},{5,9},{8,12},{9,13},{12,14},{13,15},{14,10},{15,... | collective-permute-start | bytes 786440 | tf_op jit(solution)/shard_map/ppermute | solution.py:31
  78.8 1.6 %collective-permute-done.29.refs_7_ = bf16[64,2048]{1,0:T(8,128)(2,1)S(1)} collective-permute-done((bf16[64,2048]{1,0:T(8,128)(2,1)S(1)}, bf16[64,2048]{1,0:T(8,128)(2,1)S(1)}, u32[]{:S(2)}, u32[]{:S(2)}) %collective-permute-start.29) | collective-permute-done | bytes 262176 | tf_op jit(solution)/shard_map/ppermute | solution.py:31
  80.4 1.4 %collective-permute-done.28.refs_6_ = bf16[64,2048]{1,0:T(8,128)(2,1)S(1)} collective-permute-done((bf16[64,2048]{1,0:T(8,128)(2,1)S(1)}, bf16[64,2048]{1,0:T(8,128)(2,1)S(1)}, u32[]{:S(2)}, u32[]{:S(2)}) %collective-permute-start.28) | collective-permute-done | bytes 262176 | tf_op jit(solution)/shard_map/ppermute | solution.py:31
  83.1 1.3 %collective-permute-start.32 = (bf16[64,2048]{1,0:T(8,128)(2,1)S(1)}, bf16[64,2048]{1,0:T(8,128)(2,1)S(1)}, u32[]{:S(2)}, u32[]{:S(2)}) collective-permute-start(bf16[64,2048]{1,0:T(8,128)(2,1)S(1)} %get-tuple-element.89.refs_8_), channel_id=1, source_target_pairs={{0,4},{1,5},{4,8},{5,9},{8,12},{9,13},{12,14},{13,15},{14,10},{15,... | collective-permute-start | bytes 786440 | tf_op jit(solution)/shard_map/ppermute | solution.py:31
  84.4 1.6 %collective-permute-done.35.refs_7_ = bf16[64,2048]{1,0:T(8,128)(2,1)S(1)} collective-permute-done((bf16[64,2048]{1,0:T(8,128)(2,1)S(1)}, bf16[64,2048]{1,0:T(8,128)(2,1)S(1)}, u32[]{:S(2)}, u32[]{:S(2)}) %collective-permute-start.35) | collective-permute-done | bytes 262176 | tf_op jit(solution)/shard_map/ppermute | solution.py:31
  86.0 1.4 %collective-permute-done.34.refs_6_ = bf16[64,2048]{1,0:T(8,128)(2,1)S(1)} collective-permute-done((bf16[64,2048]{1,0:T(8,128)(2,1)S(1)}, bf16[64,2048]{1,0:T(8,128)(2,1)S(1)}, u32[]{:S(2)}, u32[]{:S(2)}) %collective-permute-start.34) | collective-permute-done | bytes 262176 | tf_op jit(solution)/shard_map/ppermute | solution.py:31
  88.7 1.3 %collective-permute-start.39 = (bf16[64,2048]{1,0:T(8,128)(2,1)S(1)}, bf16[64,2048]{1,0:T(8,128)(2,1)S(1)}, u32[]{:S(2)}, u32[]{:S(2)}) collective-permute-start(bf16[64,2048]{1,0:T(8,128)(2,1)S(1)} %get-tuple-element.92.refs_5_), channel_id=1, source_target_pairs={{0,4},{1,5},{4,8},{5,9},{8,12},{9,13},{12,14},{13,15},{14,10},{15,... | collective-permute-start | bytes 786440 | tf_op jit(solution)/shard_map/ppermute | solution.py:31
  90.1 1.6 %collective-permute-done.33.refs_4_.refs_3_ = bf16[64,2048]{1,0:T(8,128)(2,1)S(1)} collective-permute-done((bf16[64,2048]{1,0:T(8,128)(2,1)S(1)}, bf16[64,2048]{1,0:T(8,128)(2,1)S(1)}, u32[]{:S(2)}, u32[]{:S(2)}) %collective-permute-start.33) | collective-permute-done | bytes 262176 | tf_op jit(solution)/shard_map/ppermute | solution.py:31
  91.7 1.4 %collective-permute-done.32.refs_3_.refs_1_ = bf16[64,2048]{1,0:T(8,128)(2,1)S(1)} collective-permute-done((bf16[64,2048]{1,0:T(8,128)(2,1)S(1)}, bf16[64,2048]{1,0:T(8,128)(2,1)S(1)}, u32[]{:S(2)}, u32[]{:S(2)}) %collective-permute-start.32) | collective-permute-done | bytes 262176 | tf_op jit(solution)/shard_map/ppermute | solution.py:31
  94.2 1.3 %collective-permute-start.36 = (bf16[32,2048]{1,0:T(8,128)(2,1)S(1)}, bf16[32,2048]{1,0:T(8,128)(2,1)S(1)}, u32[]{:S(2)}, u32[]{:S(2)}) collective-permute-start(bf16[32,2048]{1,0:T(8,128)(2,1)S(1)} %get-tuple-element.93.refs_5_), channel_id=1, source_target_pairs={{0,4},{1,5},{4,8},{5,9},{8,12},{9,13},{12,14},{13,15},{14,10},{15,... | collective-permute-start | bytes 393224 | tf_op jit(solution)/shard_map/ppermute | solution.py:31
  95.5 1.8 %collective-permute-done.40.refs_4_.refs_3_ = bf16[64,2048]{1,0:T(8,128)(2,1)S(1)} collective-permute-done((bf16[64,2048]{1,0:T(8,128)(2,1)S(1)}, bf16[64,2048]{1,0:T(8,128)(2,1)S(1)}, u32[]{:S(2)}, u32[]{:S(2)}) %collective-permute-start.40) | collective-permute-done | bytes 262176 | tf_op jit(solution)/shard_map/ppermute | solution.py:31
  97.3 1.4 %collective-permute-done.39.refs_3_.refs_1_ = bf16[64,2048]{1,0:T(8,128)(2,1)S(1)} collective-permute-done((bf16[64,2048]{1,0:T(8,128)(2,1)S(1)}, bf16[64,2048]{1,0:T(8,128)(2,1)S(1)}, u32[]{:S(2)}, u32[]{:S(2)}) %collective-permute-start.39) | collective-permute-done | bytes 262176 | tf_op jit(solution)/shard_map/ppermute | solution.py:31
  99.7 1.4 %collective-permute-start.42 = (bf16[32,2048]{1,0:T(8,128)(2,1)S(1)}, bf16[32,2048]{1,0:T(8,128)(2,1)S(1)}, u32[]{:S(2)}, u32[]{:S(2)}) collective-permute-start(bf16[32,2048]{1,0:T(8,128)(2,1)S(1)} %get-tuple-element.98), channel_id=1, source_target_pairs={{0,2},{1,3},{4,0},{5,1},{8,4},{9,5},{12,8},{13,9},{14,12},{15,13},... | collective-permute-start | bytes 393224 | tf_op jit(solution)/shard_map/ppermute | solution.py:31
  101.2 1.6 %collective-permute-start.38 = (bf16[64,2048]{1,0:T(8,128)(2,1)S(1)}, bf16[64,2048]{1,0:T(8,128)(2,1)S(1)}, u32[]{:S(2)}, u32[]{:S(2)}) collective-permute-start(bf16[64,2048]{1,0:T(8,128)(2,1)S(1)} %final.2), channel_id=1, source_target_pairs={{0,16},{16,0},{1,17},{17,1},{2,18},{18,2},{3,19},{19,3},{4,20},{20... | collective-permute-start | bytes 786440 | tf_op jit(solution)/shard_map/ppermute | solution.py:41
  102.8 1.3 %collective-permute-done.41.refs_2_ = bf16[32,2048]{1,0:T(8,128)(2,1)S(1)} collective-permute-done((bf16[32,2048]{1,0:T(8,128)(2,1)S(1)}, bf16[32,2048]{1,0:T(8,128)(2,1)S(1)}, u32[]{:S(2)}, u32[]{:S(2)}) %collective-permute-start.41) | collective-permute-done | bytes 131104 | tf_op jit(solution)/shard_map/ppermute | solution.py:31
  104.8 1.6 %collective-permute-start.43 = (bf16[64,2048]{1,0:T(8,128)(2,1)S(1)}, bf16[64,2048]{1,0:T(8,128)(2,1)S(1)}, u32[]{:S(2)}, u32[]{:S(2)}) collective-permute-start(bf16[64,2048]{1,0:T(8,128)(2,1)S(1)} %final.3), channel_id=1, source_target_pairs={{0,16},{16,0},{1,17},{17,1},{2,18},{18,2},{3,19},{19,3},{4,20},{20... | collective-permute-start | bytes 786440 | tf_op jit(solution)/shard_map/ppermute | solution.py:41
  106.4 4.2 %collective-permute-done.38 = bf16[64,2048]{1,0:T(8,128)(2,1)S(1)} collective-permute-done((bf16[64,2048]{1,0:T(8,128)(2,1)S(1)}, bf16[64,2048]{1,0:T(8,128)(2,1)S(1)}, u32[]{:S(2)}, u32[]{:S(2)}) %collective-permute-start.38) | collective-permute-done | bytes 262176 | tf_op jit(solution)/shard_map/ppermute | solution.py:41
  110.5 2.8 %collective-permute-done.43 = bf16[64,2048]{1,0:T(8,128)(2,1)S(1)} collective-permute-done((bf16[64,2048]{1,0:T(8,128)(2,1)S(1)}, bf16[64,2048]{1,0:T(8,128)(2,1)S(1)}, u32[]{:S(2)}, u32[]{:S(2)}) %collective-permute-start.43) | collective-permute-done | bytes 262176 | tf_op jit(solution)/shard_map/ppermute | solution.py:41
  (86 shorter events, 23.7 us)
Async XLA Ops:
  2.2 12.8 %collective-permute-start.7 = (bf16[64,2048]{1,0:T(8,128)(2,1)}, bf16[64,2048]{1,0:T(8,128)(2,1)S(1)}, u32[]{:S(2)}, u32[]{:S(2)}) collective-permute-start(bf16[64,2048]{1,0:T(8,128)(2,1)} %get-tuple-element.53.refs_2_), channel_id=1, source_target_pairs={{0,2},{1,3},{4,0},{5,1},{8,4},{9,5},{12,8},{13,9},{14,12},{15,13},... | collective-permute-start | bytes 786440 | tf_op jit(solution)/shard_map/ppermute | solution.py:31
  3.9 12.9 %collective-permute-start.5 = (bf16[64,2048]{1,0:T(8,128)(2,1)}, bf16[64,2048]{1,0:T(8,128)(2,1)S(1)}, u32[]{:S(2)}, u32[]{:S(2)}) collective-permute-start(bf16[64,2048]{1,0:T(8,128)(2,1)} %get-tuple-element.53.refs_2_), channel_id=1, source_target_pairs={{0,4},{1,5},{4,8},{5,9},{8,12},{9,13},{12,14},{13,15},{14,10},{15,... | collective-permute-start | bytes 786440 | tf_op jit(solution)/shard_map/ppermute | solution.py:31
  4.3 12.9 %collective-permute-start.6 = (bf16[64,2176]{1,0:T(8,128)(2,1)}, bf16[64,2176]{1,0:T(8,128)(2,1)S(1)}, u32[]{:S(2)}, u32[]{:S(2)}) collective-permute-start(bf16[64,2176]{1,0:T(8,128)(2,1)} %get-tuple-element.52.refs_1_), channel_id=1, source_target_pairs={{0,2},{1,3},{4,0},{5,1},{8,4},{9,5},{12,8},{13,9},{14,12},{15,13},... | collective-permute-start | bytes 835592 | tf_op jit(solution)/shard_map/ppermute | solution.py:31
  5.9 11.9 %collective-permute-start.2 = (bf16[64,2176]{1,0:T(8,128)(2,1)}, bf16[64,2176]{1,0:T(8,128)(2,1)S(1)}, u32[]{:S(2)}, u32[]{:S(2)}) collective-permute-start(bf16[64,2176]{1,0:T(8,128)(2,1)} %get-tuple-element.52.refs_1_), channel_id=1, source_target_pairs={{0,4},{1,5},{4,8},{5,9},{8,12},{9,13},{12,14},{13,15},{14,10},{15,... | collective-permute-start | bytes 835592 | tf_op jit(solution)/shard_map/ppermute | solution.py:31
  14.0 12.3 %copy-start.1 = (bf16[1,1,2048,768]{3,2,1,0:T(8,128)(2,1)S(1)}, bf16[1,1,2048,768]{3,2,1,0:T(8,128)(2,1)}, u32[]{:S(2)}) copy-start(bf16[1,1,2048,768]{3,2,1,0:T(8,128)(2,1)} %param.11) | copy-start | bytes 9437188
  14.0 12.3 %copy-start.3 = (bf16[1,1,2048,768]{3,2,1,0:T(8,128)(2,1)S(1)}, bf16[1,1,2048,768]{3,2,1,0:T(8,128)(2,1)}, u32[]{:S(2)}) copy-start(bf16[1,1,2048,768]{3,2,1,0:T(8,128)(2,1)} %param.12) | copy-start | bytes 9437188
  14.0 12.3 %copy-start.5 = (bf16[1,1,768,2048]{3,2,1,0:T(8,128)(2,1)S(1)}, bf16[1,1,768,2048]{3,2,1,0:T(8,128)(2,1)}, u32[]{:S(2)}) copy-start(bf16[1,1,768,2048]{3,2,1,0:T(8,128)(2,1)} %param.13) | copy-start | bytes 9437188
  15.0 5.7 %collective-permute-start = (bf16[80,2048]{1,0:T(8,128)(2,1)S(1)}, bf16[80,2048]{1,0:T(8,128)(2,1)S(1)}, u32[]{:S(2)}, u32[]{:S(2)}) collective-permute-start(bf16[80,2048]{1,0:T(8,128)(2,1)S(1)} %get-tuple-element.56), channel_id=1, source_target_pairs={{0,1},{1,0},{2,3},{3,2},{4,5},{5,4},{6,7},{7,6},{8,9},{9,8},{10,11... | collective-permute-start | bytes 983048 | tf_op jit(solution)/shard_map/ppermute | solution.py:36
  15.1 9.2 %collective-permute-start.11 = (bf16[64,2048]{1,0:T(8,128)(2,1)S(1)}, bf16[64,2048]{1,0:T(8,128)(2,1)S(1)}, u32[]{:S(2)}, u32[]{:S(2)}) collective-permute-start(bf16[64,2048]{1,0:T(8,128)(2,1)S(1)} %collective-permute-done.7.refs_4_), channel_id=1, source_target_pairs={{0,2},{1,3},{4,0},{5,1},{8,4},{9,5},{12,8},{13,9},{14,12},{15,13},... | collective-permute-start | bytes 786440 | tf_op jit(solution)/shard_map/ppermute | solution.py:31
  16.7 9.2 %collective-permute-start.9 = (bf16[64,2048]{1,0:T(8,128)(2,1)S(1)}, bf16[64,2048]{1,0:T(8,128)(2,1)S(1)}, u32[]{:S(2)}, u32[]{:S(2)}) collective-permute-start(bf16[64,2048]{1,0:T(8,128)(2,1)S(1)} %collective-permute-done.5.refs_2_), channel_id=1, source_target_pairs={{0,4},{1,5},{4,8},{5,9},{8,12},{9,13},{12,14},{13,15},{14,10},{15,... | collective-permute-start | bytes 786440 | tf_op jit(solution)/shard_map/ppermute | solution.py:31
  19.0 19.0 %collective-permute-start.8 = (bf16[144,2048]{1,0:T(8,128)(2,1)S(1)}, bf16[144,2048]{1,0:T(8,128)(2,1)S(1)}, u32[]{:S(2)}, u32[]{:S(2)}) collective-permute-start(bf16[144,2048]{1,0:T(8,128)(2,1)S(1)} %get-tuple-element.60), channel_id=1, source_target_pairs={{0,1},{1,0},{2,3},{3,2},{4,5},{5,4},{6,7},{7,6},{8,9},{9,8},{10,11... | collective-permute-start | bytes 1769480 | tf_op jit(solution)/shard_map/ppermute | solution.py:36
  19.1 11.2 %collective-permute-start.10 = (bf16[64,2176]{1,0:T(8,128)(2,1)S(1)}, bf16[64,2176]{1,0:T(8,128)(2,1)S(1)}, u32[]{:S(2)}, u32[]{:S(2)}) collective-permute-start(bf16[64,2176]{1,0:T(8,128)(2,1)S(1)} %collective-permute-done.6.refs_3_), channel_id=1, source_target_pairs={{0,2},{1,3},{4,0},{5,1},{8,4},{9,5},{12,8},{13,9},{14,12},{15,13},... | collective-permute-start | bytes 835592 | tf_op jit(solution)/shard_map/ppermute | solution.py:31
  20.7 11.2 %collective-permute-start.3 = (bf16[64,2176]{1,0:T(8,128)(2,1)S(1)}, bf16[64,2176]{1,0:T(8,128)(2,1)S(1)}, u32[]{:S(2)}, u32[]{:S(2)}) collective-permute-start(bf16[64,2176]{1,0:T(8,128)(2,1)S(1)} %collective-permute-done.2.refs_1_), channel_id=1, source_target_pairs={{0,4},{1,5},{4,8},{5,9},{8,12},{9,13},{12,14},{13,15},{14,10},{15,... | collective-permute-start | bytes 835592 | tf_op jit(solution)/shard_map/ppermute | solution.py:31
  24.3 11.6 %collective-permute-start.18 = (bf16[64,2048]{1,0:T(8,128)(2,1)S(1)}, bf16[64,2048]{1,0:T(8,128)(2,1)S(1)}, u32[]{:S(2)}, u32[]{:S(2)}) collective-permute-start(bf16[64,2048]{1,0:T(8,128)(2,1)S(1)} %collective-permute-done.11.refs_4_), channel_id=1, source_target_pairs={{0,2},{1,3},{4,0},{5,1},{8,4},{9,5},{12,8},{13,9},{14,12},{15,13},... | collective-permute-start | bytes 786440 | tf_op jit(solution)/shard_map/ppermute | solution.py:31
  25.9 11.6 %collective-permute-start.16 = (bf16[64,2048]{1,0:T(8,128)(2,1)S(1)}, bf16[64,2048]{1,0:T(8,128)(2,1)S(1)}, u32[]{:S(2)}, u32[]{:S(2)}) collective-permute-start(bf16[64,2048]{1,0:T(8,128)(2,1)S(1)} %collective-permute-done.9.refs_2_), channel_id=1, source_target_pairs={{0,4},{1,5},{4,8},{5,9},{8,12},{9,13},{12,14},{13,15},{14,10},{15,... | collective-permute-start | bytes 786440 | tf_op jit(solution)/shard_map/ppermute | solution.py:31
  30.2 12.3 %collective-permute-start.14 = (bf16[64,2176]{1,0:T(8,128)(2,1)S(1)}, bf16[64,2176]{1,0:T(8,128)(2,1)S(1)}, u32[]{:S(2)}, u32[]{:S(2)}) collective-permute-start(bf16[64,2176]{1,0:T(8,128)(2,1)S(1)} %collective-permute-done.10.refs_3_), channel_id=1, source_target_pairs={{0,2},{1,3},{4,0},{5,1},{8,4},{9,5},{12,8},{13,9},{14,12},{15,13},... | collective-permute-start | bytes 835592 | tf_op jit(solution)/shard_map/ppermute | solution.py:31
  31.9 11.6 %collective-permute-start.4 = (bf16[64,2176]{1,0:T(8,128)(2,1)S(1)}, bf16[64,2176]{1,0:T(8,128)(2,1)S(1)}, u32[]{:S(2)}, u32[]{:S(2)}) collective-permute-start(bf16[64,2176]{1,0:T(8,128)(2,1)S(1)} %collective-permute-done.3.refs_1_), channel_id=1, source_target_pairs={{0,4},{1,5},{4,8},{5,9},{8,12},{9,13},{12,14},{13,15},{14,10},{15,... | collective-permute-start | bytes 835592 | tf_op jit(solution)/shard_map/ppermute | solution.py:31
  35.9 14.2 %collective-permute-start.19 = (bf16[32,2048]{1,0:T(8,128)(2,1)S(1)}, bf16[32,2048]{1,0:T(8,128)(2,1)S(1)}, u32[]{:S(2)}, u32[]{:S(2)}) collective-permute-start(bf16[32,2048]{1,0:T(8,128)(2,1)S(1)} %slice.17), channel_id=1, source_target_pairs={{0,2},{1,3},{4,0},{5,1},{8,4},{9,5},{12,8},{13,9},{14,12},{15,13},... | collective-permute-start | bytes 393224 | tf_op jit(solution)/shard_map/ppermute | solution.py:31
  37.5 13.1 %collective-permute-start.17 = (bf16[32,2048]{1,0:T(8,128)(2,1)S(1)}, bf16[32,2048]{1,0:T(8,128)(2,1)S(1)}, u32[]{:S(2)}, u32[]{:S(2)}) collective-permute-start(bf16[32,2048]{1,0:T(8,128)(2,1)S(1)} %slice.16), channel_id=1, source_target_pairs={{0,4},{1,5},{4,8},{5,9},{8,12},{9,13},{12,14},{13,15},{14,10},{15,... | collective-permute-start | bytes 393224 | tf_op jit(solution)/shard_map/ppermute | solution.py:31
  39.2 3.3 %collective-permute-start.12 = (bf16[144,2048]{1,0:T(8,128)(2,1)S(1)}, bf16[144,2048]{1,0:T(8,128)(2,1)S(1)}, u32[]{:S(2)}, u32[]{:S(2)}) collective-permute-start(bf16[144,2048]{1,0:T(8,128)(2,1)S(1)} %get-tuple-element.62), channel_id=1, source_target_pairs={{0,1},{1,0},{2,3},{3,2},{4,5},{5,4},{6,7},{7,6},{8,9},{9,8},{10,11... | collective-permute-start | bytes 1769480 | tf_op jit(solution)/shard_map/ppermute | solution.py:36
  43.5 7.1 %collective-permute-start.15 = (bf16[32,2176]{1,0:T(8,128)(2,1)S(1)}, bf16[32,2176]{1,0:T(8,128)(2,1)S(1)}, u32[]{:S(2)}, u32[]{:S(2)}) collective-permute-start(bf16[32,2176]{1,0:T(8,128)(2,1)S(1)} %slice.13), channel_id=1, source_target_pairs={{0,2},{1,3},{4,0},{5,1},{8,4},{9,5},{12,8},{13,9},{14,12},{15,13},... | collective-permute-start | bytes 417800 | tf_op jit(solution)/shard_map/ppermute | solution.py:31
  45.1 5.5 %collective-permute-start.13 = (bf16[32,2176]{1,0:T(8,128)(2,1)S(1)}, bf16[32,2176]{1,0:T(8,128)(2,1)S(1)}, u32[]{:S(2)}, u32[]{:S(2)}) collective-permute-start(bf16[32,2176]{1,0:T(8,128)(2,1)S(1)} %slice.12), channel_id=1, source_target_pairs={{0,4},{1,5},{4,8},{5,9},{8,12},{9,13},{12,14},{13,15},{14,10},{15,... | collective-permute-start | bytes 417800 | tf_op jit(solution)/shard_map/ppermute | solution.py:31
  46.7 5.0 %collective-permute-start.21 = (bf16[144,2048]{1,0:T(8,128)(2,1)S(1)}, bf16[144,2048]{1,0:T(8,128)(2,1)S(1)}, u32[]{:S(2)}, u32[]{:S(2)}) collective-permute-start(bf16[144,2048]{1,0:T(8,128)(2,1)S(1)} %get-tuple-element.71), channel_id=1, source_target_pairs={{0,1},{1,0},{2,3},{3,2},{4,5},{5,4},{6,7},{7,6},{8,9},{9,8},{10,11... | collective-permute-start | bytes 1769480 | tf_op jit(solution)/shard_map/ppermute | solution.py:36
  50.0 14.0 %collective-permute-start.24 = (bf16[144,2048]{1,0:T(8,128)(2,1)S(1)}, bf16[144,2048]{1,0:T(8,128)(2,1)S(1)}, u32[]{:S(2)}, u32[]{:S(2)}) collective-permute-start(bf16[144,2048]{1,0:T(8,128)(2,1)S(1)} %get-tuple-element.81), channel_id=1, source_target_pairs={{0,1},{1,0},{2,3},{3,2},{4,5},{5,4},{6,7},{7,6},{8,9},{9,8},{10,11... | collective-permute-start | bytes 1769480 | tf_op jit(solution)/shard_map/ppermute | solution.py:36
  51.6 3.9 %collective-permute-start.20 = (bf16[80,2048]{1,0:T(8,128)(2,1)S(1)}, bf16[80,2048]{1,0:T(8,128)(2,1)S(1)}, u32[]{:S(2)}, u32[]{:S(2)}) collective-permute-start(bf16[80,2048]{1,0:T(8,128)(2,1)S(1)} %get-tuple-element.69), channel_id=1, source_target_pairs={{0,1},{1,0},{2,3},{3,2},{4,5},{5,4},{6,7},{7,6},{8,9},{9,8},{10,11... | collective-permute-start | bytes 983048 | tf_op jit(solution)/shard_map/ppermute | solution.py:36
  55.0 4.3 %collective-permute-start.23 = (bf16[144,2048]{1,0:T(8,128)(2,1)S(1)}, bf16[144,2048]{1,0:T(8,128)(2,1)S(1)}, u32[]{:S(2)}, u32[]{:S(2)}) collective-permute-start(bf16[144,2048]{1,0:T(8,128)(2,1)S(1)} %get-tuple-element.76), channel_id=1, source_target_pairs={{0,1},{1,0},{2,3},{3,2},{4,5},{5,4},{6,7},{7,6},{8,9},{9,8},{10,11... | collective-permute-start | bytes 1769480 | tf_op jit(solution)/shard_map/ppermute | solution.py:36
  57.6 6.9 %copy-start.6 = (bf16[1,128,2048]{2,1,0:T(8,128)(2,1)S(1)}, bf16[1,128,2048]{2,1,0:T(8,128)(2,1)}, u32[]{:S(2)}) copy-start(bf16[1,128,2048]{2,1,0:T(8,128)(2,1)} %param.7) | copy-start | bytes 1572868
  57.6 1.7 %collective-permute-start.22 = (bf16[80,2048]{1,0:T(8,128)(2,1)S(1)}, bf16[80,2048]{1,0:T(8,128)(2,1)S(1)}, u32[]{:S(2)}, u32[]{:S(2)}) collective-permute-start(bf16[80,2048]{1,0:T(8,128)(2,1)S(1)} %get-tuple-element.74), channel_id=1, source_target_pairs={{0,1},{1,0},{2,3},{3,2},{4,5},{5,4},{6,7},{7,6},{8,9},{9,8},{10,11... | collective-permute-start | bytes 983048 | tf_op jit(solution)/shard_map/ppermute | solution.py:36
  57.7 4.7 %collective-permute-start.1 = (bf16[80,2048]{1,0:T(8,128)(2,1)S(1)}, bf16[80,2048]{1,0:T(8,128)(2,1)S(1)}, u32[]{:S(2)}, u32[]{:S(2)}) collective-permute-start(bf16[80,2048]{1,0:T(8,128)(2,1)S(1)} %get-tuple-element.58), channel_id=1, source_target_pairs={{0,1},{1,0},{2,3},{3,2},{4,5},{5,4},{6,7},{7,6},{8,9},{9,8},{10,11... | collective-permute-start | bytes 983048 | tf_op jit(solution)/shard_map/ppermute | solution.py:36
  58.2 20.7 %collective-permute-start.25 = (bf16[144,2048]{1,0:T(8,128)(2,1)S(1)}, bf16[144,2048]{1,0:T(8,128)(2,1)S(1)}, u32[]{:S(2)}, u32[]{:S(2)}) collective-permute-start(bf16[144,2048]{1,0:T(8,128)(2,1)S(1)} %get-tuple-element.83), channel_id=1, source_target_pairs={{0,1},{1,0},{2,3},{3,2},{4,5},{5,4},{6,7},{7,6},{8,9},{9,8},{10,11... | collective-permute-start | bytes 1769480 | tf_op jit(solution)/shard_map/ppermute | solution.py:36
  59.8 9.2 %collective-permute-start.27 = (bf16[64,2048]{1,0:T(8,128)(2,1)S(1)}, bf16[64,2048]{1,0:T(8,128)(2,1)S(1)}, u32[]{:S(2)}, u32[]{:S(2)}) collective-permute-start(bf16[64,2048]{1,0:T(8,128)(2,1)S(1)} %get-tuple-element.84), channel_id=1, source_target_pairs={{0,2},{1,3},{4,0},{5,1},{8,4},{9,5},{12,8},{13,9},{14,12},{15,13},... | collective-permute-start | bytes 786440 | tf_op jit(solution)/shard_map/ppermute | solution.py:31
  61.4 9.2 %collective-permute-start.26 = (bf16[64,2048]{1,0:T(8,128)(2,1)S(1)}, bf16[64,2048]{1,0:T(8,128)(2,1)S(1)}, u32[]{:S(2)}, u32[]{:S(2)}) collective-permute-start(bf16[64,2048]{1,0:T(8,128)(2,1)S(1)} %get-tuple-element.77.refs_6_), channel_id=1, source_target_pairs={{0,4},{1,5},{4,8},{5,9},{8,12},{9,13},{12,14},{13,15},{14,10},{15,... | collective-permute-start | bytes 786440 | tf_op jit(solution)/shard_map/ppermute | solution.py:31
  62.4 12.2 %collective-permute-start.31 = (bf16[64,2048]{1,0:T(8,128)(2,1)S(1)}, bf16[64,2048]{1,0:T(8,128)(2,1)S(1)}, u32[]{:S(2)}, u32[]{:S(2)}) collective-permute-start(bf16[64,2048]{1,0:T(8,128)(2,1)S(1)} %get-tuple-element.87), channel_id=1, source_target_pairs={{0,2},{1,3},{4,0},{5,1},{8,4},{9,5},{12,8},{13,9},{14,12},{15,13},... | collective-permute-start | bytes 786440 | tf_op jit(solution)/shard_map/ppermute | solution.py:31
  64.0 12.2 %collective-permute-start.30 = (bf16[64,2048]{1,0:T(8,128)(2,1)S(1)}, bf16[64,2048]{1,0:T(8,128)(2,1)S(1)}, u32[]{:S(2)}, u32[]{:S(2)}) collective-permute-start(bf16[64,2048]{1,0:T(8,128)(2,1)S(1)} %get-tuple-element.78.refs_4_), channel_id=1, source_target_pairs={{0,4},{1,5},{4,8},{5,9},{8,12},{9,13},{12,14},{13,15},{14,10},{15,... | collective-permute-start | bytes 786440 | tf_op jit(solution)/shard_map/ppermute | solution.py:31
  71.1 9.3 %collective-permute-start.29 = (bf16[64,2048]{1,0:T(8,128)(2,1)S(1)}, bf16[64,2048]{1,0:T(8,128)(2,1)S(1)}, u32[]{:S(2)}, u32[]{:S(2)}) collective-permute-start(bf16[64,2048]{1,0:T(8,128)(2,1)S(1)} %get-tuple-element.86), channel_id=1, source_target_pairs={{0,2},{1,3},{4,0},{5,1},{8,4},{9,5},{12,8},{13,9},{14,12},{15,13},... | collective-permute-start | bytes 786440 | tf_op jit(solution)/shard_map/ppermute | solution.py:31
  71.9 10.0 %collective-permute-start.28 = (bf16[64,2048]{1,0:T(8,128)(2,1)S(1)}, bf16[64,2048]{1,0:T(8,128)(2,1)S(1)}, u32[]{:S(2)}, u32[]{:S(2)}) collective-permute-start(bf16[64,2048]{1,0:T(8,128)(2,1)S(1)} %get-tuple-element.85.refs_8_), channel_id=1, source_target_pairs={{0,4},{1,5},{4,8},{5,9},{8,12},{9,13},{12,14},{13,15},{14,10},{15,... | collective-permute-start | bytes 786440 | tf_op jit(solution)/shard_map/ppermute | solution.py:31
  76.7 9.3 %collective-permute-start.35 = (bf16[64,2048]{1,0:T(8,128)(2,1)S(1)}, bf16[64,2048]{1,0:T(8,128)(2,1)S(1)}, u32[]{:S(2)}, u32[]{:S(2)}) collective-permute-start(bf16[64,2048]{1,0:T(8,128)(2,1)S(1)} %get-tuple-element.91), channel_id=1, source_target_pairs={{0,2},{1,3},{4,0},{5,1},{8,4},{9,5},{12,8},{13,9},{14,12},{15,13},... | collective-permute-start | bytes 786440 | tf_op jit(solution)/shard_map/ppermute | solution.py:31
  77.5 10.0 %collective-permute-start.34 = (bf16[64,2048]{1,0:T(8,128)(2,1)S(1)}, bf16[64,2048]{1,0:T(8,128)(2,1)S(1)}, u32[]{:S(2)}, u32[]{:S(2)}) collective-permute-start(bf16[64,2048]{1,0:T(8,128)(2,1)S(1)} %get-tuple-element.88.refs_8_), channel_id=1, source_target_pairs={{0,4},{1,5},{4,8},{5,9},{8,12},{9,13},{12,14},{13,15},{14,10},{15,... | collective-permute-start | bytes 786440 | tf_op jit(solution)/shard_map/ppermute | solution.py:31
  82.4 9.3 %collective-permute-start.33 = (bf16[64,2048]{1,0:T(8,128)(2,1)S(1)}, bf16[64,2048]{1,0:T(8,128)(2,1)S(1)}, u32[]{:S(2)}, u32[]{:S(2)}) collective-permute-start(bf16[64,2048]{1,0:T(8,128)(2,1)S(1)} %get-tuple-element.90), channel_id=1, source_target_pairs={{0,2},{1,3},{4,0},{5,1},{8,4},{9,5},{12,8},{13,9},{14,12},{15,13},... | collective-permute-start | bytes 786440 | tf_op jit(solution)/shard_map/ppermute | solution.py:31
  83.1 10.0 %collective-permute-start.32 = (bf16[64,2048]{1,0:T(8,128)(2,1)S(1)}, bf16[64,2048]{1,0:T(8,128)(2,1)S(1)}, u32[]{:S(2)}, u32[]{:S(2)}) collective-permute-start(bf16[64,2048]{1,0:T(8,128)(2,1)S(1)} %get-tuple-element.89.refs_8_), channel_id=1, source_target_pairs={{0,4},{1,5},{4,8},{5,9},{8,12},{9,13},{12,14},{13,15},{14,10},{15,... | collective-permute-start | bytes 786440 | tf_op jit(solution)/shard_map/ppermute | solution.py:31
  88.0 9.3 %collective-permute-start.40 = (bf16[64,2048]{1,0:T(8,128)(2,1)S(1)}, bf16[64,2048]{1,0:T(8,128)(2,1)S(1)}, u32[]{:S(2)}, u32[]{:S(2)}) collective-permute-start(bf16[64,2048]{1,0:T(8,128)(2,1)S(1)} %get-tuple-element.96), channel_id=1, source_target_pairs={{0,2},{1,3},{4,0},{5,1},{8,4},{9,5},{12,8},{13,9},{14,12},{15,13},... | collective-permute-start | bytes 786440 | tf_op jit(solution)/shard_map/ppermute | solution.py:31
  88.7 10.0 %collective-permute-start.39 = (bf16[64,2048]{1,0:T(8,128)(2,1)S(1)}, bf16[64,2048]{1,0:T(8,128)(2,1)S(1)}, u32[]{:S(2)}, u32[]{:S(2)}) collective-permute-start(bf16[64,2048]{1,0:T(8,128)(2,1)S(1)} %get-tuple-element.92.refs_5_), channel_id=1, source_target_pairs={{0,4},{1,5},{4,8},{5,9},{8,12},{9,13},{12,14},{13,15},{14,10},{15,... | collective-permute-start | bytes 786440 | tf_op jit(solution)/shard_map/ppermute | solution.py:31
  93.4 7.7 %collective-permute-start.37 = (bf16[32,2048]{1,0:T(8,128)(2,1)S(1)}, bf16[32,2048]{1,0:T(8,128)(2,1)S(1)}, u32[]{:S(2)}, u32[]{:S(2)}) collective-permute-start(bf16[32,2048]{1,0:T(8,128)(2,1)S(1)} %get-tuple-element.94), channel_id=1, source_target_pairs={{0,2},{1,3},{4,0},{5,1},{8,4},{9,5},{12,8},{13,9},{14,12},{15,13},... | collective-permute-start | bytes 393224 | tf_op jit(solution)/shard_map/ppermute | solution.py:31
  94.2 7.0 %collective-permute-start.36 = (bf16[32,2048]{1,0:T(8,128)(2,1)S(1)}, bf16[32,2048]{1,0:T(8,128)(2,1)S(1)}, u32[]{:S(2)}, u32[]{:S(2)}) collective-permute-start(bf16[32,2048]{1,0:T(8,128)(2,1)S(1)} %get-tuple-element.93.refs_5_), channel_id=1, source_target_pairs={{0,4},{1,5},{4,8},{5,9},{8,12},{9,13},{12,14},{13,15},{14,10},{15,... | collective-permute-start | bytes 393224 | tf_op jit(solution)/shard_map/ppermute | solution.py:31
  99.1 5.0 %collective-permute-start.41 = (bf16[32,2048]{1,0:T(8,128)(2,1)S(1)}, bf16[32,2048]{1,0:T(8,128)(2,1)S(1)}, u32[]{:S(2)}, u32[]{:S(2)}) collective-permute-start(bf16[32,2048]{1,0:T(8,128)(2,1)S(1)} %get-tuple-element.97), channel_id=1, source_target_pairs={{0,4},{1,5},{4,8},{5,9},{8,12},{9,13},{12,14},{13,15},{14,10},{15,... | collective-permute-start | bytes 393224 | tf_op jit(solution)/shard_map/ppermute | solution.py:31
  99.7 5.0 %collective-permute-start.42 = (bf16[32,2048]{1,0:T(8,128)(2,1)S(1)}, bf16[32,2048]{1,0:T(8,128)(2,1)S(1)}, u32[]{:S(2)}, u32[]{:S(2)}) collective-permute-start(bf16[32,2048]{1,0:T(8,128)(2,1)S(1)} %get-tuple-element.98), channel_id=1, source_target_pairs={{0,2},{1,3},{4,0},{5,1},{8,4},{9,5},{12,8},{13,9},{14,12},{15,13},... | collective-permute-start | bytes 393224 | tf_op jit(solution)/shard_map/ppermute | solution.py:31
  101.2 9.3 %collective-permute-start.38 = (bf16[64,2048]{1,0:T(8,128)(2,1)S(1)}, bf16[64,2048]{1,0:T(8,128)(2,1)S(1)}, u32[]{:S(2)}, u32[]{:S(2)}) collective-permute-start(bf16[64,2048]{1,0:T(8,128)(2,1)S(1)} %final.2), channel_id=1, source_target_pairs={{0,16},{16,0},{1,17},{17,1},{2,18},{18,2},{3,19},{19,3},{4,20},{20... | collective-permute-start | bytes 786440 | tf_op jit(solution)/shard_map/ppermute | solution.py:41
  104.8 8.6 %collective-permute-start.43 = (bf16[64,2048]{1,0:T(8,128)(2,1)S(1)}, bf16[64,2048]{1,0:T(8,128)(2,1)S(1)}, u32[]{:S(2)}, u32[]{:S(2)}) collective-permute-start(bf16[64,2048]{1,0:T(8,128)(2,1)S(1)} %final.3), channel_id=1, source_target_pairs={{0,16},{16,0},{1,17},{17,1},{2,18},{18,2},{3,19},{19,3},{4,20},{20... | collective-permute-start | bytes 786440 | tf_op jit(solution)/shard_map/ppermute | solution.py:41
  (5 other events, 7.6 us)

commit v4 on v3

--- a/solution.py
+++ b/solution.py
@@ -131,29 +131,18 @@
     info[...] = jnp.concatenate([lines, spare], axis=0).T
 
 
-def ffn_kernel(tile, own, *refs):
+def ffn_kernel(own, *refs):
     swapped, (gate, up, down), refs = refs[:SWAPS], refs[SWAPS : SWAPS + 3], refs[SWAPS + 3 :]
-    own_out, swapped_outs, (rows, total) = refs[0], refs[1 : 1 + SWAPS], refs[1 + SWAPS :]
+    own_out, swapped_outs, rows = refs[0], refs[1 : 1 + SWAPS], refs[1 + SWAPS]
     slots, span = swapped[0].shape
     rows[:slots] = own[...]
     for index, part in enumerate(swapped):
         rows[slots:, index * span : (index + 1) * span] = part[...]
 
-    def terms(step):
-        columns = pl.ds(pl.multiple_of(step * tile, tile), tile)
-        gate_part = jnp.dot(rows[...], gate[:, columns], preferred_element_type=F32)
-        up_part = jnp.dot(rows[...], up[:, columns], preferred_element_type=F32)
-        hidden = (gate_part / (1.0 + jnp.exp(-gate_part)) * up_part).astype(BF16)
-        return jnp.dot(hidden, down[columns, :], preferred_element_type=F32)
-
-    steps = gate.shape[1] // tile
-    total[...] = terms(0)
-
-    @pl.loop(1, steps - 1)
-    def _(step):
-        total[...] += terms(step)
-
-    result = total[...] + terms(steps - 1)
+    gate_part = jnp.dot(rows[...], gate[...], preferred_element_type=F32)
+    up_part = jnp.dot(rows[...], up[...], preferred_element_type=F32)
+    hidden = (gate_part / (1.0 + jnp.exp(-gate_part)) * up_part).astype(BF16)
+    result = jnp.dot(hidden, down[...], preferred_element_type=F32)
     own_out[...] = result[:slots].astype(BF16)
     for index, target in enumerate(swapped_outs):
         target[...] = result[slots:, index * span : (index + 1) * span].astype(BF16)
@@ -230,8 +219,6 @@
     device = lax.axis_index("expert")
     names = jnp.stack([device, device ^ 1]).astype(jnp.int32)
     gate, up, down = w_gate[0, 0], w_up[0, 0], w_down[0, 0]
-    hidden = gate.shape[1]
-    tile = 256 if hidden % 256 == 0 else hidden
 
     sources = [rows, norm_gain, router_weight[0].T, jnp.transpose(routes, (2, 0, 1))]
     own = call(
@@ -262,11 +249,11 @@
     def ffn(own_rows, swapped_rows, after):
         slots = own_rows.shape[0]
         return call(
-            functools.partial(ffn_kernel, tile),
+            ffn_kernel,
             [shape(slots, width)] + [shape(slots, width // SWAPS)] * SWAPS,
             [own_rows, *swapped_rows, gate, up, down],
             after,
-            scratch=[pltpu.VMEM((2 * slots, width), BF16), pltpu.VMEM((2 * slots, width), F32)],
+            scratch=[pltpu.VMEM((2 * slots, width), BF16)],
             megabytes=24,
             flops=6e7 * slots,
             name=f"ffn{1 + (slots > 100)}",

time: 116 us -> 115 us (level)
  Pallas kernels: 26 us -> 24.5 us
    pallas_call x22, Pallas kernels: 26 us -> 24.5 us  [call(): pl.pallas_call(body, name=name, out_shape=out_shapes, grid=grid or (), in...]
  transfers between devices with their start and end apart: 44 -> 44, of which waited for: 22 -> 22; matrix products, arithmetic and copies ran while one was open for 0% -> 0% of each run, Pallas kernels for 21% -> 20%
where the time goes in v4:
time: 115 us; the launch traced here: 113 us
  waiting for transfers between devices  41.5 us (36%)
  starting transfers between devices  38.4 us (33%)
  Pallas kernels  24.5 us (21%)
  local copies, waits for them, and re-layouts  7.63 us (7%)
    ppermute x32, waiting for transfers between devices, round_ring(): lax.ppermute(shard, 'expert', ring_pairs(lax.axis_size('expert'), by))  33.5 us
    ppermute x32, starting transfers between devices, round_ring(): lax.ppermute(shard, 'expert', ring_pairs(lax.axis_size('expert'), by))  33.2 us
    pallas_call x22, Pallas kernels, call(): pl.pallas_call(body, name=name, out_shape=out_shapes, grid=grid or (), in...  24.5 us
    unnamed x18, local copies, waits for them, and re-layouts  7.59 us
    ppermute x2, waiting for transfers between devices, next_section(): lax.ppermute(shard, 'pipe', [(i, (i + 1) % sections) for i in range(secti...  6.95 us
    ppermute x2, starting transfers between devices, next_section(): lax.ppermute(shard, 'pipe', [(i, (i + 1) % sections) for i in range(secti...  3.14 us
  transfers between devices with their start and end apart: 44, of which 22 were waited for; matrix products, arithmetic and copies ran while one was open for 0% of the time, Pallas kernels for 20%

profile of v4, /device:TPU:10, one launch (start us, length us, event | category | flops | bytes accessed | tf_op | source)
XLA Modules:
  0.0 113.3 jit_solution(10424757732888767049)
XLA Ops:
  0.0 2.2 %prepare.1 = (bf16[64,2176]{1,0:T(8,128)(2,1)}, bf16[64,2048]{1,0:T(8,128)(2,1)}) custom-call(bf16[128,2048]{1,0:T(8,128)(2,1)} %bitcast.30, f32[1,2048]{1,0:T(1,128)} %refs_1_.1, bf16[16,2048]{1,0:T(8,128)(2,1)} %bitcast.32, s32[6,1,128]{2,1,0:T(1,128)} %bitcast.33), custom_call_target="tpu_custom_call" | custom-call | tf_op jit(solution)/shard_map/prepare/pallas_call | solution.py:55
  2.2 1.6 %collective-permute-start.7 = (bf16[64,2048]{1,0:T(8,128)(2,1)}, bf16[64,2048]{1,0:T(8,128)(2,1)S(1)}, u32[]{:S(2)}, u32[]{:S(2)}) collective-permute-start(bf16[64,2048]{1,0:T(8,128)(2,1)} %get-tuple-element.53.refs_2_), channel_id=1, source_target_pairs={{0,2},{1,3},{4,0},{5,1},{8,4},{9,5},{12,8},{13,9},{14,12},{15,13},... | collective-permute-start | bytes 786440 | tf_op jit(solution)/shard_map/ppermute | solution.py:31
  4.3 1.6 %collective-permute-start.6 = (bf16[64,2176]{1,0:T(8,128)(2,1)}, bf16[64,2176]{1,0:T(8,128)(2,1)S(1)}, u32[]{:S(2)}, u32[]{:S(2)}) collective-permute-start(bf16[64,2176]{1,0:T(8,128)(2,1)} %get-tuple-element.52.refs_1_), channel_id=1, source_target_pairs={{0,2},{1,3},{4,0},{5,1},{8,4},{9,5},{12,8},{13,9},{14,12},{15,13},... | collective-permute-start | bytes 835592 | tf_op jit(solution)/shard_map/ppermute | solution.py:31
  6.4 1.9 %copy-done = bf16[1,1,2048,768]{3,2,1,0:T(8,128)(2,1)S(1)} copy-done((bf16[1,1,2048,768]{3,2,1,0:T(8,128)(2,1)S(1)}, bf16[1,1,2048,768]{3,2,1,0:T(8,128)(2,1)}, u32[]{:S(2)}) %copy-start) | copy-done | bytes 3145752
  8.3 1.9 %copy-done.2 = bf16[1,1,2048,768]{3,2,1,0:T(8,128)(2,1)S(1)} copy-done((bf16[1,1,2048,768]{3,2,1,0:T(8,128)(2,1)S(1)}, bf16[1,1,2048,768]{3,2,1,0:T(8,128)(2,1)}, u32[]{:S(2)}) %copy-start.2) | copy-done | bytes 3145752
  10.2 1.9 %copy-done.4 = bf16[1,1,768,2048]{3,2,1,0:T(8,128)(2,1)S(1)} copy-done((bf16[1,1,768,2048]{3,2,1,0:T(8,128)(2,1)S(1)}, bf16[1,1,768,2048]{3,2,1,0:T(8,128)(2,1)}, u32[]{:S(2)}) %copy-start.4) | copy-done | bytes 3145752
  15.1 1.6 %collective-permute-start.11 = (bf16[64,2048]{1,0:T(8,128)(2,1)S(1)}, bf16[64,2048]{1,0:T(8,128)(2,1)S(1)}, u32[]{:S(2)}, u32[]{:S(2)}) collective-permute-start(bf16[64,2048]{1,0:T(8,128)(2,1)S(1)} %collective-permute-done.7.refs_4_), channel_id=1, source_target_pairs={{0,2},{1,3},{4,0},{5,1},{8,4},{9,5},{12,8},{13,9},{14,12},{15,13},... | collective-permute-start | bytes 786440 | tf_op jit(solution)/shard_map/ppermute | solution.py:31
  19.1 1.6 %collective-permute-start.10 = (bf16[64,2176]{1,0:T(8,128)(2,1)S(1)}, bf16[64,2176]{1,0:T(8,128)(2,1)S(1)}, u32[]{:S(2)}, u32[]{:S(2)}) collective-permute-start(bf16[64,2176]{1,0:T(8,128)(2,1)S(1)} %collective-permute-done.6.refs_3_), channel_id=1, source_target_pairs={{0,2},{1,3},{4,0},{5,1},{8,4},{9,5},{12,8},{13,9},{14,12},{15,13},... | collective-permute-start | bytes 835592 | tf_op jit(solution)/shard_map/ppermute | solution.py:31
  21.1 3.1 %collective-permute-done.11.refs_4_ = bf16[64,2048]{1,0:T(8,128)(2,1)S(1)} collective-permute-done((bf16[64,2048]{1,0:T(8,128)(2,1)S(1)}, bf16[64,2048]{1,0:T(8,128)(2,1)S(1)}, u32[]{:S(2)}, u32[]{:S(2)}) %collective-permute-start.11) | collective-permute-done | bytes 262176 | tf_op jit(solution)/shard_map/ppermute | solution.py:31
  24.3 1.6 %collective-permute-start.18 = (bf16[64,2048]{1,0:T(8,128)(2,1)S(1)}, bf16[64,2048]{1,0:T(8,128)(2,1)S(1)}, u32[]{:S(2)}, u32[]{:S(2)}) collective-permute-start(bf16[64,2048]{1,0:T(8,128)(2,1)S(1)} %collective-permute-done.11.refs_4_), channel_id=1, source_target_pairs={{0,2},{1,3},{4,0},{5,1},{8,4},{9,5},{12,8},{13,9},{14,12},{15,13},... | collective-permute-start | bytes 786440 | tf_op jit(solution)/shard_map/ppermute | solution.py:31
  26.3 1.8 %ffn1.2 = (bf16[80,2048]{1,0:T(8,128)(2,1)S(1)}, bf16[80,2048]{1,0:T(8,128)(2,1)S(1)}) custom-call(bf16[80,2048]{1,0:T(8,128)(2,1)S(1)} %get-tuple-element.55.refs_0_, bf16[80,2048]{1,0:T(8,128)(2,1)S(1)} %collective-permute-done.refs_1_, bf16[2048,768]{1,0:T(8,128)(2,1)S(1)} %bitcast.13, bf16[2048,768]{1,0:T(8,128)(2,1)S(1)} %bitcast.19, ...), custom_call_target="tpu_custom_call" | custom-call | flops 4800000000 | tf_op jit(solution)/shard_map/ffn1/pallas_call | solution.py:55
  28.1 2.1 %collective-permute-done.10.refs_3_ = bf16[64,2176]{1,0:T(8,128)(2,1)S(1)} collective-permute-done((bf16[64,2176]{1,0:T(8,128)(2,1)S(1)}, bf16[64,2176]{1,0:T(8,128)(2,1)S(1)}, u32[]{:S(2)}, u32[]{:S(2)}) %collective-permute-start.10) | collective-permute-done | bytes 278560 | tf_op jit(solution)/shard_map/ppermute | solution.py:31
  30.2 1.6 %collective-permute-start.14 = (bf16[64,2176]{1,0:T(8,128)(2,1)S(1)}, bf16[64,2176]{1,0:T(8,128)(2,1)S(1)}, u32[]{:S(2)}, u32[]{:S(2)}) collective-permute-start(bf16[64,2176]{1,0:T(8,128)(2,1)S(1)} %collective-permute-done.10.refs_3_), channel_id=1, source_target_pairs={{0,2},{1,3},{4,0},{5,1},{8,4},{9,5},{12,8},{13,9},{14,12},{15,13},... | collective-permute-start | bytes 835592 | tf_op jit(solution)/shard_map/ppermute | solution.py:31
  32.3 3.5 %collective-permute-done.18.refs_4_ = bf16[64,2048]{1,0:T(8,128)(2,1)S(1)} collective-permute-done((bf16[64,2048]{1,0:T(8,128)(2,1)S(1)}, bf16[64,2048]{1,0:T(8,128)(2,1)S(1)}, u32[]{:S(2)}, u32[]{:S(2)}) %collective-permute-start.18) | collective-permute-done | bytes 262176 | tf_op jit(solution)/shard_map/ppermute | solution.py:31
  35.9 1.6 %collective-permute-start.19 = (bf16[32,2048]{1,0:T(8,128)(2,1)S(1)}, bf16[32,2048]{1,0:T(8,128)(2,1)S(1)}, u32[]{:S(2)}, u32[]{:S(2)}) collective-permute-start(bf16[32,2048]{1,0:T(8,128)(2,1)S(1)} %slice.17), channel_id=1, source_target_pairs={{0,2},{1,3},{4,0},{5,1},{8,4},{9,5},{12,8},{13,9},{14,12},{15,13},... | collective-permute-start | bytes 393224 | tf_op jit(solution)/shard_map/ppermute | solution.py:31
  38.0 1.2 %select2.4 = (bf16[144,2048]{1,0:T(8,128)(2,1)S(1)}, f32[256,128]{1,0:T(8,128)S(1)}, bf16[144,2048]{1,0:T(8,128)(2,1)S(1)}) custom-call(s32[2]{0:T(128)S(1)} %pad_add_fusion.refs_0_, bf16[64,2176]{1,0:T(8,128)(2,1)S(1)} %collective-permute-done.3.refs_1_, bf16[64,2048]{1,0:T(8,128)(2,1)S(1)} %collective-permute-done.9.refs_2_, ...), custom_call_target="tpu_custom_call" | custom-call | flops 400000000 | tf_op jit(solution)/shard_map/select2/pallas_call | solution.py:55
  39.3 3.0 %ffn2.3 = (bf16[144,2048]{1,0:T(8,128)(2,1)S(1)}, bf16[144,2048]{1,0:T(8,128)(2,1)S(1)}) custom-call(bf16[144,2048]{1,0:T(8,128)(2,1)S(1)} %get-tuple-element.59.refs_0_, bf16[144,2048]{1,0:T(8,128)(2,1)S(1)} %collective-permute-done.8.refs_1_.refs_5_, bf16[2048,768]{1,0:T(8,128)(2,1)S(1)} %bitcast.14, bf16[2048,768]{1,0:T(8,128)(2,1)S(1)} %bitcast.20, ...), custom_call_target="tpu_custom_call" | custom-call | flops 8640000000 | tf_op jit(solution)/shard_map/ffn2/pallas_call | solution.py:55
  42.2 1.2 %collective-permute-done.4.refs_1_ = bf16[64,2176]{1,0:T(8,128)(2,1)S(1)} collective-permute-done((bf16[64,2176]{1,0:T(8,128)(2,1)S(1)}, bf16[64,2176]{1,0:T(8,128)(2,1)S(1)}, u32[]{:S(2)}, u32[]{:S(2)}) %collective-permute-start.4) | collective-permute-done | bytes 278560 | tf_op jit(solution)/shard_map/ppermute | solution.py:31
  43.5 1.6 %collective-permute-start.15 = (bf16[32,2176]{1,0:T(8,128)(2,1)S(1)}, bf16[32,2176]{1,0:T(8,128)(2,1)S(1)}, u32[]{:S(2)}, u32[]{:S(2)}) collective-permute-start(bf16[32,2176]{1,0:T(8,128)(2,1)S(1)} %slice.13), channel_id=1, source_target_pairs={{0,2},{1,3},{4,0},{5,1},{8,4},{9,5},{12,8},{13,9},{14,12},{15,13},... | collective-permute-start | bytes 417800 | tf_op jit(solution)/shard_map/ppermute | solution.py:31
  45.5 1.2 %select2.5 = (bf16[144,2048]{1,0:T(8,128)(2,1)S(1)}, f32[256,128]{1,0:T(8,128)S(1)}, bf16[144,2048]{1,0:T(8,128)(2,1)S(1)}) custom-call(s32[2]{0:T(128)S(1)} %pad_add_fusion.refs_0_, bf16[64,2176]{1,0:T(8,128)(2,1)S(1)} %collective-permute-done.4.refs_1_, bf16[64,2048]{1,0:T(8,128)(2,1)S(1)} %collective-permute-done.16.refs_2_, ...), custom_call_target="tpu_custom_call" | custom-call | flops 400000000 | tf_op jit(solution)/shard_map/select2/pallas_call | solution.py:55
  46.8 3.0 %ffn2.4 = (bf16[144,2048]{1,0:T(8,128)(2,1)S(1)}, bf16[144,2048]{1,0:T(8,128)(2,1)S(1)}) custom-call(bf16[144,2048]{1,0:T(8,128)(2,1)S(1)} %get-tuple-element.65.refs_0_, bf16[144,2048]{1,0:T(8,128)(2,1)S(1)} %collective-permute-done.12.refs_1_.refs_5_, bf16[2048,768]{1,0:T(8,128)(2,1)S(1)} %bitcast.15, bf16[2048,768]{1,0:T(8,128)(2,1)S(1)} %bitcast.21, ...), custom_call_target="tpu_custom_call" | custom-call | flops 8640000000 | tf_op jit(solution)/shard_map/ffn2/pallas_call | solution.py:55
  51.5 3.0 %ffn2.5 = (bf16[144,2048]{1,0:T(8,128)(2,1)S(1)}, bf16[144,2048]{1,0:T(8,128)(2,1)S(1)}) custom-call(bf16[144,2048]{1,0:T(8,128)(2,1)S(1)} %get-tuple-element.70.refs_0_, bf16[144,2048]{1,0:T(8,128)(2,1)S(1)} %collective-permute-done.21.refs_1_, bf16[2048,768]{1,0:T(8,128)(2,1)S(1)} %bitcast.16, bf16[2048,768]{1,0:T(8,128)(2,1)S(1)} %bitcast.22, ...), custom_call_target="tpu_custom_call" | custom-call | flops 8640000000 | tf_op jit(solution)/shard_map/ffn2/pallas_call | solution.py:55
  55.0 1.8 %ffn1.3 = (bf16[80,2048]{1,0:T(8,128)(2,1)S(1)}, bf16[80,2048]{1,0:T(8,128)(2,1)S(1)}) custom-call(bf16[80,2048]{1,0:T(8,128)(2,1)S(1)} %get-tuple-element.68.refs_0_, bf16[80,2048]{1,0:T(8,128)(2,1)S(1)} %collective-permute-done.20.refs_1_, bf16[2048,768]{1,0:T(8,128)(2,1)S(1)} %bitcast.17, bf16[2048,768]{1,0:T(8,128)(2,1)S(1)} %bitcast.23, ...), custom_call_target="tpu_custom_call" | custom-call | flops 4800000000 | tf_op jit(solution)/shard_map/ffn1/pallas_call | solution.py:55
  58.9 1.6 %collective-permute-start.27 = (bf16[64,2048]{1,0:T(8,128)(2,1)S(1)}, bf16[64,2048]{1,0:T(8,128)(2,1)S(1)}, u32[]{:S(2)}, u32[]{:S(2)}) collective-permute-start(bf16[64,2048]{1,0:T(8,128)(2,1)S(1)} %get-tuple-element.84), channel_id=1, source_target_pairs={{0,2},{1,3},{4,0},{5,1},{8,4},{9,5},{12,8},{13,9},{14,12},{15,13},... | collective-permute-start | bytes 786440 | tf_op jit(solution)/shard_map/ppermute | solution.py:31
  61.5 1.6 %collective-permute-start.31 = (bf16[64,2048]{1,0:T(8,128)(2,1)S(1)}, bf16[64,2048]{1,0:T(8,128)(2,1)S(1)}, u32[]{:S(2)}, u32[]{:S(2)}) collective-permute-start(bf16[64,2048]{1,0:T(8,128)(2,1)S(1)} %get-tuple-element.87), channel_id=1, source_target_pairs={{0,2},{1,3},{4,0},{5,1},{8,4},{9,5},{12,8},{13,9},{14,12},{15,13},... | collective-permute-start | bytes 786440 | tf_op jit(solution)/shard_map/ppermute | solution.py:31
  64.1 4.0 %collective-permute-done.27.refs_7_ = bf16[64,2048]{1,0:T(8,128)(2,1)S(1)} collective-permute-done((bf16[64,2048]{1,0:T(8,128)(2,1)S(1)}, bf16[64,2048]{1,0:T(8,128)(2,1)S(1)}, u32[]{:S(2)}, u32[]{:S(2)}) %collective-permute-start.27) | collective-permute-done | bytes 262176 | tf_op jit(solution)/shard_map/ppermute | solution.py:31
  68.1 1.6 %collective-permute-done.26.refs_6_ = bf16[64,2048]{1,0:T(8,128)(2,1)S(1)} collective-permute-done((bf16[64,2048]{1,0:T(8,128)(2,1)S(1)}, bf16[64,2048]{1,0:T(8,128)(2,1)S(1)}, u32[]{:S(2)}, u32[]{:S(2)}) %collective-permute-start.26) | collective-permute-done | bytes 262176 | tf_op jit(solution)/shard_map/ppermute | solution.py:31
  70.9 1.5 %collective-permute-start.28 = (bf16[64,2048]{1,0:T(8,128)(2,1)S(1)}, bf16[64,2048]{1,0:T(8,128)(2,1)S(1)}, u32[]{:S(2)}, u32[]{:S(2)}) collective-permute-start(bf16[64,2048]{1,0:T(8,128)(2,1)S(1)} %get-tuple-element.85.refs_8_), channel_id=1, source_target_pairs={{0,4},{1,5},{4,8},{5,9},{8,12},{9,13},{12,14},{13,15},{14,10},{15,... | collective-permute-start | bytes 786440 | tf_op jit(solution)/shard_map/ppermute | solution.py:31
  72.4 1.4 %collective-permute-done.31.refs_7_ = bf16[64,2048]{1,0:T(8,128)(2,1)S(1)} collective-permute-done((bf16[64,2048]{1,0:T(8,128)(2,1)S(1)}, bf16[64,2048]{1,0:T(8,128)(2,1)S(1)}, u32[]{:S(2)}, u32[]{:S(2)}) %collective-permute-start.31) | collective-permute-done | bytes 262176 | tf_op jit(solution)/shard_map/ppermute | solution.py:31
  73.8 1.6 %collective-permute-done.30.refs_6_ = bf16[64,2048]{1,0:T(8,128)(2,1)S(1)} collective-permute-done((bf16[64,2048]{1,0:T(8,128)(2,1)S(1)}, bf16[64,2048]{1,0:T(8,128)(2,1)S(1)}, u32[]{:S(2)}, u32[]{:S(2)}) %collective-permute-start.30) | collective-permute-done | bytes 262176 | tf_op jit(solution)/shard_map/ppermute | solution.py:31
  76.5 1.5 %collective-permute-start.34 = (bf16[64,2048]{1,0:T(8,128)(2,1)S(1)}, bf16[64,2048]{1,0:T(8,128)(2,1)S(1)}, u32[]{:S(2)}, u32[]{:S(2)}) collective-permute-start(bf16[64,2048]{1,0:T(8,128)(2,1)S(1)} %get-tuple-element.88.refs_8_), channel_id=1, source_target_pairs={{0,4},{1,5},{4,8},{5,9},{8,12},{9,13},{12,14},{13,15},{14,10},{15,... | collective-permute-start | bytes 786440 | tf_op jit(solution)/shard_map/ppermute | solution.py:31
  78.0 1.6 %collective-permute-done.29.refs_7_ = bf16[64,2048]{1,0:T(8,128)(2,1)S(1)} collective-permute-done((bf16[64,2048]{1,0:T(8,128)(2,1)S(1)}, bf16[64,2048]{1,0:T(8,128)(2,1)S(1)}, u32[]{:S(2)}, u32[]{:S(2)}) %collective-permute-start.29) | collective-permute-done | bytes 262176 | tf_op jit(solution)/shard_map/ppermute | solution.py:31
  79.6 1.4 %collective-permute-done.28.refs_6_ = bf16[64,2048]{1,0:T(8,128)(2,1)S(1)} collective-permute-done((bf16[64,2048]{1,0:T(8,128)(2,1)S(1)}, bf16[64,2048]{1,0:T(8,128)(2,1)S(1)}, u32[]{:S(2)}, u32[]{:S(2)}) %collective-permute-start.28) | collective-permute-done | bytes 262176 | tf_op jit(solution)/shard_map/ppermute | solution.py:31
  82.1 1.5 %collective-permute-start.32 = (bf16[64,2048]{1,0:T(8,128)(2,1)S(1)}, bf16[64,2048]{1,0:T(8,128)(2,1)S(1)}, u32[]{:S(2)}, u32[]{:S(2)}) collective-permute-start(bf16[64,2048]{1,0:T(8,128)(2,1)S(1)} %get-tuple-element.89.refs_8_), channel_id=1, source_target_pairs={{0,4},{1,5},{4,8},{5,9},{8,12},{9,13},{12,14},{13,15},{14,10},{15,... | collective-permute-start | bytes 786440 | tf_op jit(solution)/shard_map/ppermute | solution.py:31
  83.6 1.6 %collective-permute-done.35.refs_7_ = bf16[64,2048]{1,0:T(8,128)(2,1)S(1)} collective-permute-done((bf16[64,2048]{1,0:T(8,128)(2,1)S(1)}, bf16[64,2048]{1,0:T(8,128)(2,1)S(1)}, u32[]{:S(2)}, u32[]{:S(2)}) %collective-permute-start.35) | collective-permute-done | bytes 262176 | tf_op jit(solution)/shard_map/ppermute | solution.py:31
  85.2 1.4 %collective-permute-done.34.refs_6_ = bf16[64,2048]{1,0:T(8,128)(2,1)S(1)} collective-permute-done((bf16[64,2048]{1,0:T(8,128)(2,1)S(1)}, bf16[64,2048]{1,0:T(8,128)(2,1)S(1)}, u32[]{:S(2)}, u32[]{:S(2)}) %collective-permute-start.34) | collective-permute-done | bytes 262176 | tf_op jit(solution)/shard_map/ppermute | solution.py:31
  87.7 1.5 %collective-permute-start.39 = (bf16[64,2048]{1,0:T(8,128)(2,1)S(1)}, bf16[64,2048]{1,0:T(8,128)(2,1)S(1)}, u32[]{:S(2)}, u32[]{:S(2)}) collective-permute-start(bf16[64,2048]{1,0:T(8,128)(2,1)S(1)} %get-tuple-element.92.refs_5_), channel_id=1, source_target_pairs={{0,4},{1,5},{4,8},{5,9},{8,12},{9,13},{12,14},{13,15},{14,10},{15,... | collective-permute-start | bytes 786440 | tf_op jit(solution)/shard_map/ppermute | solution.py:31
  89.2 1.6 %collective-permute-done.33.refs_4_.refs_3_ = bf16[64,2048]{1,0:T(8,128)(2,1)S(1)} collective-permute-done((bf16[64,2048]{1,0:T(8,128)(2,1)S(1)}, bf16[64,2048]{1,0:T(8,128)(2,1)S(1)}, u32[]{:S(2)}, u32[]{:S(2)}) %collective-permute-start.33) | collective-permute-done | bytes 262176 | tf_op jit(solution)/shard_map/ppermute | solution.py:31
  90.8 1.4 %collective-permute-done.32.refs_3_.refs_1_ = bf16[64,2048]{1,0:T(8,128)(2,1)S(1)} collective-permute-done((bf16[64,2048]{1,0:T(8,128)(2,1)S(1)}, bf16[64,2048]{1,0:T(8,128)(2,1)S(1)}, u32[]{:S(2)}, u32[]{:S(2)}) %collective-permute-start.32) | collective-permute-done | bytes 262176 | tf_op jit(solution)/shard_map/ppermute | solution.py:31
  93.2 1.5 %collective-permute-start.36 = (bf16[32,2048]{1,0:T(8,128)(2,1)S(1)}, bf16[32,2048]{1,0:T(8,128)(2,1)S(1)}, u32[]{:S(2)}, u32[]{:S(2)}) collective-permute-start(bf16[32,2048]{1,0:T(8,128)(2,1)S(1)} %get-tuple-element.93.refs_5_), channel_id=1, source_target_pairs={{0,4},{1,5},{4,8},{5,9},{8,12},{9,13},{12,14},{13,15},{14,10},{15,... | collective-permute-start | bytes 393224 | tf_op jit(solution)/shard_map/ppermute | solution.py:31
  94.7 1.8 %collective-permute-done.40.refs_4_.refs_3_ = bf16[64,2048]{1,0:T(8,128)(2,1)S(1)} collective-permute-done((bf16[64,2048]{1,0:T(8,128)(2,1)S(1)}, bf16[64,2048]{1,0:T(8,128)(2,1)S(1)}, u32[]{:S(2)}, u32[]{:S(2)}) %collective-permute-start.40) | collective-permute-done | bytes 262176 | tf_op jit(solution)/shard_map/ppermute | solution.py:31
  96.4 1.4 %collective-permute-done.39.refs_3_.refs_1_ = bf16[64,2048]{1,0:T(8,128)(2,1)S(1)} collective-permute-done((bf16[64,2048]{1,0:T(8,128)(2,1)S(1)}, bf16[64,2048]{1,0:T(8,128)(2,1)S(1)}, u32[]{:S(2)}, u32[]{:S(2)}) %collective-permute-start.39) | collective-permute-done | bytes 262176 | tf_op jit(solution)/shard_map/ppermute | solution.py:31
  98.9 1.4 %collective-permute-start.42 = (bf16[32,2048]{1,0:T(8,128)(2,1)S(1)}, bf16[32,2048]{1,0:T(8,128)(2,1)S(1)}, u32[]{:S(2)}, u32[]{:S(2)}) collective-permute-start(bf16[32,2048]{1,0:T(8,128)(2,1)S(1)} %get-tuple-element.98), channel_id=1, source_target_pairs={{0,2},{1,3},{4,0},{5,1},{8,4},{9,5},{12,8},{13,9},{14,12},{15,13},... | collective-permute-start | bytes 393224 | tf_op jit(solution)/shard_map/ppermute | solution.py:31
  100.4 1.6 %collective-permute-start.38 = (bf16[64,2048]{1,0:T(8,128)(2,1)S(1)}, bf16[64,2048]{1,0:T(8,128)(2,1)S(1)}, u32[]{:S(2)}, u32[]{:S(2)}) collective-permute-start(bf16[64,2048]{1,0:T(8,128)(2,1)S(1)} %final.2), channel_id=1, source_target_pairs={{0,16},{16,0},{1,17},{17,1},{2,18},{18,2},{3,19},{19,3},{4,20},{20... | collective-permute-start | bytes 786440 | tf_op jit(solution)/shard_map/ppermute | solution.py:41
  102.0 1.3 %collective-permute-done.41.refs_2_ = bf16[32,2048]{1,0:T(8,128)(2,1)S(1)} collective-permute-done((bf16[32,2048]{1,0:T(8,128)(2,1)S(1)}, bf16[32,2048]{1,0:T(8,128)(2,1)S(1)}, u32[]{:S(2)}, u32[]{:S(2)}) %collective-permute-start.41) | collective-permute-done | bytes 131104 | tf_op jit(solution)/shard_map/ppermute | solution.py:31
  103.9 1.6 %collective-permute-start.43 = (bf16[64,2048]{1,0:T(8,128)(2,1)S(1)}, bf16[64,2048]{1,0:T(8,128)(2,1)S(1)}, u32[]{:S(2)}, u32[]{:S(2)}) collective-permute-start(bf16[64,2048]{1,0:T(8,128)(2,1)S(1)} %final.3), channel_id=1, source_target_pairs={{0,16},{16,0},{1,17},{17,1},{2,18},{18,2},{3,19},{19,3},{4,20},{20... | collective-permute-start | bytes 786440 | tf_op jit(solution)/shard_map/ppermute | solution.py:41
  105.5 4.1 %collective-permute-done.38 = bf16[64,2048]{1,0:T(8,128)(2,1)S(1)} collective-permute-done((bf16[64,2048]{1,0:T(8,128)(2,1)S(1)}, bf16[64,2048]{1,0:T(8,128)(2,1)S(1)}, u32[]{:S(2)}, u32[]{:S(2)}) %collective-permute-start.38) | collective-permute-done | bytes 262176 | tf_op jit(solution)/shard_map/ppermute | solution.py:41
  109.7 2.8 %collective-permute-done.43 = bf16[64,2048]{1,0:T(8,128)(2,1)S(1)} collective-permute-done((bf16[64,2048]{1,0:T(8,128)(2,1)S(1)}, bf16[64,2048]{1,0:T(8,128)(2,1)S(1)}, u32[]{:S(2)}, u32[]{:S(2)}) %collective-permute-start.43) | collective-permute-done | bytes 262176 | tf_op jit(solution)/shard_map/ppermute | solution.py:41
  (86 shorter events, 23.2 us)
Async XLA Ops:
  2.2 12.8 %collective-permute-start.7 = (bf16[64,2048]{1,0:T(8,128)(2,1)}, bf16[64,2048]{1,0:T(8,128)(2,1)S(1)}, u32[]{:S(2)}, u32[]{:S(2)}) collective-permute-start(bf16[64,2048]{1,0:T(8,128)(2,1)} %get-tuple-element.53.refs_2_), channel_id=1, source_target_pairs={{0,2},{1,3},{4,0},{5,1},{8,4},{9,5},{12,8},{13,9},{14,12},{15,13},... | collective-permute-start | bytes 786440 | tf_op jit(solution)/shard_map/ppermute | solution.py:31
  3.9 12.9 %collective-permute-start.5 = (bf16[64,2048]{1,0:T(8,128)(2,1)}, bf16[64,2048]{1,0:T(8,128)(2,1)S(1)}, u32[]{:S(2)}, u32[]{:S(2)}) collective-permute-start(bf16[64,2048]{1,0:T(8,128)(2,1)} %get-tuple-element.53.refs_2_), channel_id=1, source_target_pairs={{0,4},{1,5},{4,8},{5,9},{8,12},{9,13},{12,14},{13,15},{14,10},{15,... | collective-permute-start | bytes 786440 | tf_op jit(solution)/shard_map/ppermute | solution.py:31
  4.3 12.9 %collective-permute-start.6 = (bf16[64,2176]{1,0:T(8,128)(2,1)}, bf16[64,2176]{1,0:T(8,128)(2,1)S(1)}, u32[]{:S(2)}, u32[]{:S(2)}) collective-permute-start(bf16[64,2176]{1,0:T(8,128)(2,1)} %get-tuple-element.52.refs_1_), channel_id=1, source_target_pairs={{0,2},{1,3},{4,0},{5,1},{8,4},{9,5},{12,8},{13,9},{14,12},{15,13},... | collective-permute-start | bytes 835592 | tf_op jit(solution)/shard_map/ppermute | solution.py:31
  5.9 11.9 %collective-permute-start.2 = (bf16[64,2176]{1,0:T(8,128)(2,1)}, bf16[64,2176]{1,0:T(8,128)(2,1)S(1)}, u32[]{:S(2)}, u32[]{:S(2)}) collective-permute-start(bf16[64,2176]{1,0:T(8,128)(2,1)} %get-tuple-element.52.refs_1_), channel_id=1, source_target_pairs={{0,4},{1,5},{4,8},{5,9},{8,12},{9,13},{12,14},{13,15},{14,10},{15,... | collective-permute-start | bytes 835592 | tf_op jit(solution)/shard_map/ppermute | solution.py:31
  14.0 12.3 %copy-start.1 = (bf16[1,1,2048,768]{3,2,1,0:T(8,128)(2,1)S(1)}, bf16[1,1,2048,768]{3,2,1,0:T(8,128)(2,1)}, u32[]{:S(2)}) copy-start(bf16[1,1,2048,768]{3,2,1,0:T(8,128)(2,1)} %param.11) | copy-start | bytes 9437188
  14.0 12.3 %copy-start.3 = (bf16[1,1,2048,768]{3,2,1,0:T(8,128)(2,1)S(1)}, bf16[1,1,2048,768]{3,2,1,0:T(8,128)(2,1)}, u32[]{:S(2)}) copy-start(bf16[1,1,2048,768]{3,2,1,0:T(8,128)(2,1)} %param.12) | copy-start | bytes 9437188
  14.0 12.3 %copy-start.5 = (bf16[1,1,768,2048]{3,2,1,0:T(8,128)(2,1)S(1)}, bf16[1,1,768,2048]{3,2,1,0:T(8,128)(2,1)}, u32[]{:S(2)}) copy-start(bf16[1,1,768,2048]{3,2,1,0:T(8,128)(2,1)} %param.13) | copy-start | bytes 9437188
  15.0 5.7 %collective-permute-start = (bf16[80,2048]{1,0:T(8,128)(2,1)S(1)}, bf16[80,2048]{1,0:T(8,128)(2,1)S(1)}, u32[]{:S(2)}, u32[]{:S(2)}) collective-permute-start(bf16[80,2048]{1,0:T(8,128)(2,1)S(1)} %get-tuple-element.56), channel_id=1, source_target_pairs={{0,1},{1,0},{2,3},{3,2},{4,5},{5,4},{6,7},{7,6},{8,9},{9,8},{10,11... | collective-permute-start | bytes 983048 | tf_op jit(solution)/shard_map/ppermute | solution.py:36
  15.1 9.2 %collective-permute-start.11 = (bf16[64,2048]{1,0:T(8,128)(2,1)S(1)}, bf16[64,2048]{1,0:T(8,128)(2,1)S(1)}, u32[]{:S(2)}, u32[]{:S(2)}) collective-permute-start(bf16[64,2048]{1,0:T(8,128)(2,1)S(1)} %collective-permute-done.7.refs_4_), channel_id=1, source_target_pairs={{0,2},{1,3},{4,0},{5,1},{8,4},{9,5},{12,8},{13,9},{14,12},{15,13},... | collective-permute-start | bytes 786440 | tf_op jit(solution)/shard_map/ppermute | solution.py:31
  16.7 9.2 %collective-permute-start.9 = (bf16[64,2048]{1,0:T(8,128)(2,1)S(1)}, bf16[64,2048]{1,0:T(8,128)(2,1)S(1)}, u32[]{:S(2)}, u32[]{:S(2)}) collective-permute-start(bf16[64,2048]{1,0:T(8,128)(2,1)S(1)} %collective-permute-done.5.refs_2_), channel_id=1, source_target_pairs={{0,4},{1,5},{4,8},{5,9},{8,12},{9,13},{12,14},{13,15},{14,10},{15,... | collective-permute-start | bytes 786440 | tf_op jit(solution)/shard_map/ppermute | solution.py:31
  19.0 19.0 %collective-permute-start.8 = (bf16[144,2048]{1,0:T(8,128)(2,1)S(1)}, bf16[144,2048]{1,0:T(8,128)(2,1)S(1)}, u32[]{:S(2)}, u32[]{:S(2)}) collective-permute-start(bf16[144,2048]{1,0:T(8,128)(2,1)S(1)} %get-tuple-element.60), channel_id=1, source_target_pairs={{0,1},{1,0},{2,3},{3,2},{4,5},{5,4},{6,7},{7,6},{8,9},{9,8},{10,11... | collective-permute-start | bytes 1769480 | tf_op jit(solution)/shard_map/ppermute | solution.py:36
  19.1 11.2 %collective-permute-start.10 = (bf16[64,2176]{1,0:T(8,128)(2,1)S(1)}, bf16[64,2176]{1,0:T(8,128)(2,1)S(1)}, u32[]{:S(2)}, u32[]{:S(2)}) collective-permute-start(bf16[64,2176]{1,0:T(8,128)(2,1)S(1)} %collective-permute-done.6.refs_3_), channel_id=1, source_target_pairs={{0,2},{1,3},{4,0},{5,1},{8,4},{9,5},{12,8},{13,9},{14,12},{15,13},... | collective-permute-start | bytes 835592 | tf_op jit(solution)/shard_map/ppermute | solution.py:31
  20.7 11.2 %collective-permute-start.3 = (bf16[64,2176]{1,0:T(8,128)(2,1)S(1)}, bf16[64,2176]{1,0:T(8,128)(2,1)S(1)}, u32[]{:S(2)}, u32[]{:S(2)}) collective-permute-start(bf16[64,2176]{1,0:T(8,128)(2,1)S(1)} %collective-permute-done.2.refs_1_), channel_id=1, source_target_pairs={{0,4},{1,5},{4,8},{5,9},{8,12},{9,13},{12,14},{13,15},{14,10},{15,... | collective-permute-start | bytes 835592 | tf_op jit(solution)/shard_map/ppermute | solution.py:31
  24.3 11.6 %collective-permute-start.18 = (bf16[64,2048]{1,0:T(8,128)(2,1)S(1)}, bf16[64,2048]{1,0:T(8,128)(2,1)S(1)}, u32[]{:S(2)}, u32[]{:S(2)}) collective-permute-start(bf16[64,2048]{1,0:T(8,128)(2,1)S(1)} %collective-permute-done.11.refs_4_), channel_id=1, source_target_pairs={{0,2},{1,3},{4,0},{5,1},{8,4},{9,5},{12,8},{13,9},{14,12},{15,13},... | collective-permute-start | bytes 786440 | tf_op jit(solution)/shard_map/ppermute | solution.py:31
  25.9 11.6 %collective-permute-start.16 = (bf16[64,2048]{1,0:T(8,128)(2,1)S(1)}, bf16[64,2048]{1,0:T(8,128)(2,1)S(1)}, u32[]{:S(2)}, u32[]{:S(2)}) collective-permute-start(bf16[64,2048]{1,0:T(8,128)(2,1)S(1)} %collective-permute-done.9.refs_2_), channel_id=1, source_target_pairs={{0,4},{1,5},{4,8},{5,9},{8,12},{9,13},{12,14},{13,15},{14,10},{15,... | collective-permute-start | bytes 786440 | tf_op jit(solution)/shard_map/ppermute | solution.py:31
  30.2 12.0 %collective-permute-start.14 = (bf16[64,2176]{1,0:T(8,128)(2,1)S(1)}, bf16[64,2176]{1,0:T(8,128)(2,1)S(1)}, u32[]{:S(2)}, u32[]{:S(2)}) collective-permute-start(bf16[64,2176]{1,0:T(8,128)(2,1)S(1)} %collective-permute-done.10.refs_3_), channel_id=1, source_target_pairs={{0,2},{1,3},{4,0},{5,1},{8,4},{9,5},{12,8},{13,9},{14,12},{15,13},... | collective-permute-start | bytes 835592 | tf_op jit(solution)/shard_map/ppermute | solution.py:31
  31.9 11.6 %collective-permute-start.4 = (bf16[64,2176]{1,0:T(8,128)(2,1)S(1)}, bf16[64,2176]{1,0:T(8,128)(2,1)S(1)}, u32[]{:S(2)}, u32[]{:S(2)}) collective-permute-start(bf16[64,2176]{1,0:T(8,128)(2,1)S(1)} %collective-permute-done.3.refs_1_), channel_id=1, source_target_pairs={{0,4},{1,5},{4,8},{5,9},{8,12},{9,13},{12,14},{13,15},{14,10},{15,... | collective-permute-start | bytes 835592 | tf_op jit(solution)/shard_map/ppermute | solution.py:31
  35.9 13.9 %collective-permute-start.19 = (bf16[32,2048]{1,0:T(8,128)(2,1)S(1)}, bf16[32,2048]{1,0:T(8,128)(2,1)S(1)}, u32[]{:S(2)}, u32[]{:S(2)}) collective-permute-start(bf16[32,2048]{1,0:T(8,128)(2,1)S(1)} %slice.17), channel_id=1, source_target_pairs={{0,2},{1,3},{4,0},{5,1},{8,4},{9,5},{12,8},{13,9},{14,12},{15,13},... | collective-permute-start | bytes 393224 | tf_op jit(solution)/shard_map/ppermute | solution.py:31
  37.5 12.8 %collective-permute-start.17 = (bf16[32,2048]{1,0:T(8,128)(2,1)S(1)}, bf16[32,2048]{1,0:T(8,128)(2,1)S(1)}, u32[]{:S(2)}, u32[]{:S(2)}) collective-permute-start(bf16[32,2048]{1,0:T(8,128)(2,1)S(1)} %slice.16), channel_id=1, source_target_pairs={{0,4},{1,5},{4,8},{5,9},{8,12},{9,13},{12,14},{13,15},{14,10},{15,... | collective-permute-start | bytes 393224 | tf_op jit(solution)/shard_map/ppermute | solution.py:31
  39.2 3.1 %collective-permute-start.12 = (bf16[144,2048]{1,0:T(8,128)(2,1)S(1)}, bf16[144,2048]{1,0:T(8,128)(2,1)S(1)}, u32[]{:S(2)}, u32[]{:S(2)}) collective-permute-start(bf16[144,2048]{1,0:T(8,128)(2,1)S(1)} %get-tuple-element.62), channel_id=1, source_target_pairs={{0,1},{1,0},{2,3},{3,2},{4,5},{5,4},{6,7},{7,6},{8,9},{9,8},{10,11... | collective-permute-start | bytes 1769480 | tf_op jit(solution)/shard_map/ppermute | solution.py:36
  43.5 6.9 %collective-permute-start.15 = (bf16[32,2176]{1,0:T(8,128)(2,1)S(1)}, bf16[32,2176]{1,0:T(8,128)(2,1)S(1)}, u32[]{:S(2)}, u32[]{:S(2)}) collective-permute-start(bf16[32,2176]{1,0:T(8,128)(2,1)S(1)} %slice.13), channel_id=1, source_target_pairs={{0,2},{1,3},{4,0},{5,1},{8,4},{9,5},{12,8},{13,9},{14,12},{15,13},... | collective-permute-start | bytes 417800 | tf_op jit(solution)/shard_map/ppermute | solution.py:31
  45.1 5.2 %collective-permute-start.13 = (bf16[32,2176]{1,0:T(8,128)(2,1)S(1)}, bf16[32,2176]{1,0:T(8,128)(2,1)S(1)}, u32[]{:S(2)}, u32[]{:S(2)}) collective-permute-start(bf16[32,2176]{1,0:T(8,128)(2,1)S(1)} %slice.12), channel_id=1, source_target_pairs={{0,4},{1,5},{4,8},{5,9},{8,12},{9,13},{12,14},{13,15},{14,10},{15,... | collective-permute-start | bytes 417800 | tf_op jit(solution)/shard_map/ppermute | solution.py:31
  46.7 4.7 %collective-permute-start.21 = (bf16[144,2048]{1,0:T(8,128)(2,1)S(1)}, bf16[144,2048]{1,0:T(8,128)(2,1)S(1)}, u32[]{:S(2)}, u32[]{:S(2)}) collective-permute-start(bf16[144,2048]{1,0:T(8,128)(2,1)S(1)} %get-tuple-element.71), channel_id=1, source_target_pairs={{0,1},{1,0},{2,3},{3,2},{4,5},{5,4},{6,7},{7,6},{8,9},{9,8},{10,11... | collective-permute-start | bytes 1769480 | tf_op jit(solution)/shard_map/ppermute | solution.py:36
  49.8 13.4 %collective-permute-start.24 = (bf16[144,2048]{1,0:T(8,128)(2,1)S(1)}, bf16[144,2048]{1,0:T(8,128)(2,1)S(1)}, u32[]{:S(2)}, u32[]{:S(2)}) collective-permute-start(bf16[144,2048]{1,0:T(8,128)(2,1)S(1)} %get-tuple-element.81), channel_id=1, source_target_pairs={{0,1},{1,0},{2,3},{3,2},{4,5},{5,4},{6,7},{7,6},{8,9},{9,8},{10,11... | collective-permute-start | bytes 1769480 | tf_op jit(solution)/shard_map/ppermute | solution.py:36
  51.4 3.6 %collective-permute-start.20 = (bf16[80,2048]{1,0:T(8,128)(2,1)S(1)}, bf16[80,2048]{1,0:T(8,128)(2,1)S(1)}, u32[]{:S(2)}, u32[]{:S(2)}) collective-permute-start(bf16[80,2048]{1,0:T(8,128)(2,1)S(1)} %get-tuple-element.69), channel_id=1, source_target_pairs={{0,1},{1,0},{2,3},{3,2},{4,5},{5,4},{6,7},{7,6},{8,9},{9,8},{10,11... | collective-permute-start | bytes 983048 | tf_op jit(solution)/shard_map/ppermute | solution.py:36
  54.4 4.0 %collective-permute-start.23 = (bf16[144,2048]{1,0:T(8,128)(2,1)S(1)}, bf16[144,2048]{1,0:T(8,128)(2,1)S(1)}, u32[]{:S(2)}, u32[]{:S(2)}) collective-permute-start(bf16[144,2048]{1,0:T(8,128)(2,1)S(1)} %get-tuple-element.76), channel_id=1, source_target_pairs={{0,1},{1,0},{2,3},{3,2},{4,5},{5,4},{6,7},{7,6},{8,9},{9,8},{10,11... | collective-permute-start | bytes 1769480 | tf_op jit(solution)/shard_map/ppermute | solution.py:36
  56.7 6.9 %copy-start.6 = (bf16[1,128,2048]{2,1,0:T(8,128)(2,1)S(1)}, bf16[1,128,2048]{2,1,0:T(8,128)(2,1)}, u32[]{:S(2)}) copy-start(bf16[1,128,2048]{2,1,0:T(8,128)(2,1)} %param.7) | copy-start | bytes 1572868
  56.7 1.7 %collective-permute-start.22 = (bf16[80,2048]{1,0:T(8,128)(2,1)S(1)}, bf16[80,2048]{1,0:T(8,128)(2,1)S(1)}, u32[]{:S(2)}, u32[]{:S(2)}) collective-permute-start(bf16[80,2048]{1,0:T(8,128)(2,1)S(1)} %get-tuple-element.74), channel_id=1, source_target_pairs={{0,1},{1,0},{2,3},{3,2},{4,5},{5,4},{6,7},{7,6},{8,9},{9,8},{10,11... | collective-permute-start | bytes 983048 | tf_op jit(solution)/shard_map/ppermute | solution.py:36
  56.8 4.7 %collective-permute-start.1 = (bf16[80,2048]{1,0:T(8,128)(2,1)S(1)}, bf16[80,2048]{1,0:T(8,128)(2,1)S(1)}, u32[]{:S(2)}, u32[]{:S(2)}) collective-permute-start(bf16[80,2048]{1,0:T(8,128)(2,1)S(1)} %get-tuple-element.58), channel_id=1, source_target_pairs={{0,1},{1,0},{2,3},{3,2},{4,5},{5,4},{6,7},{7,6},{8,9},{9,8},{10,11... | collective-permute-start | bytes 983048 | tf_op jit(solution)/shard_map/ppermute | solution.py:36
  57.3 20.7 %collective-permute-start.25 = (bf16[144,2048]{1,0:T(8,128)(2,1)S(1)}, bf16[144,2048]{1,0:T(8,128)(2,1)S(1)}, u32[]{:S(2)}, u32[]{:S(2)}) collective-permute-start(bf16[144,2048]{1,0:T(8,128)(2,1)S(1)} %get-tuple-element.83), channel_id=1, source_target_pairs={{0,1},{1,0},{2,3},{3,2},{4,5},{5,4},{6,7},{7,6},{8,9},{9,8},{10,11... | collective-permute-start | bytes 1769480 | tf_op jit(solution)/shard_map/ppermute | solution.py:36
  58.9 9.2 %collective-permute-start.27 = (bf16[64,2048]{1,0:T(8,128)(2,1)S(1)}, bf16[64,2048]{1,0:T(8,128)(2,1)S(1)}, u32[]{:S(2)}, u32[]{:S(2)}) collective-permute-start(bf16[64,2048]{1,0:T(8,128)(2,1)S(1)} %get-tuple-element.84), channel_id=1, source_target_pairs={{0,2},{1,3},{4,0},{5,1},{8,4},{9,5},{12,8},{13,9},{14,12},{15,13},... | collective-permute-start | bytes 786440 | tf_op jit(solution)/shard_map/ppermute | solution.py:31
  60.6 9.2 %collective-permute-start.26 = (bf16[64,2048]{1,0:T(8,128)(2,1)S(1)}, bf16[64,2048]{1,0:T(8,128)(2,1)S(1)}, u32[]{:S(2)}, u32[]{:S(2)}) collective-permute-start(bf16[64,2048]{1,0:T(8,128)(2,1)S(1)} %get-tuple-element.77.refs_6_), channel_id=1, source_target_pairs={{0,4},{1,5},{4,8},{5,9},{8,12},{9,13},{12,14},{13,15},{14,10},{15,... | collective-permute-start | bytes 786440 | tf_op jit(solution)/shard_map/ppermute | solution.py:31
  61.5 12.2 %collective-permute-start.31 = (bf16[64,2048]{1,0:T(8,128)(2,1)S(1)}, bf16[64,2048]{1,0:T(8,128)(2,1)S(1)}, u32[]{:S(2)}, u32[]{:S(2)}) collective-permute-start(bf16[64,2048]{1,0:T(8,128)(2,1)S(1)} %get-tuple-element.87), channel_id=1, source_target_pairs={{0,2},{1,3},{4,0},{5,1},{8,4},{9,5},{12,8},{13,9},{14,12},{15,13},... | collective-permute-start | bytes 786440 | tf_op jit(solution)/shard_map/ppermute | solution.py:31
  63.2 12.2 %collective-permute-start.30 = (bf16[64,2048]{1,0:T(8,128)(2,1)S(1)}, bf16[64,2048]{1,0:T(8,128)(2,1)S(1)}, u32[]{:S(2)}, u32[]{:S(2)}) collective-permute-start(bf16[64,2048]{1,0:T(8,128)(2,1)S(1)} %get-tuple-element.78.refs_4_), channel_id=1, source_target_pairs={{0,4},{1,5},{4,8},{5,9},{8,12},{9,13},{12,14},{13,15},{14,10},{15,... | collective-permute-start | bytes 786440 | tf_op jit(solution)/shard_map/ppermute | solution.py:31
  70.3 9.3 %collective-permute-start.29 = (bf16[64,2048]{1,0:T(8,128)(2,1)S(1)}, bf16[64,2048]{1,0:T(8,128)(2,1)S(1)}, u32[]{:S(2)}, u32[]{:S(2)}) collective-permute-start(bf16[64,2048]{1,0:T(8,128)(2,1)S(1)} %get-tuple-element.86), channel_id=1, source_target_pairs={{0,2},{1,3},{4,0},{5,1},{8,4},{9,5},{12,8},{13,9},{14,12},{15,13},... | collective-permute-start | bytes 786440 | tf_op jit(solution)/shard_map/ppermute | solution.py:31
  70.9 10.1 %collective-permute-start.28 = (bf16[64,2048]{1,0:T(8,128)(2,1)S(1)}, bf16[64,2048]{1,0:T(8,128)(2,1)S(1)}, u32[]{:S(2)}, u32[]{:S(2)}) collective-permute-start(bf16[64,2048]{1,0:T(8,128)(2,1)S(1)} %get-tuple-element.85.refs_8_), channel_id=1, source_target_pairs={{0,4},{1,5},{4,8},{5,9},{8,12},{9,13},{12,14},{13,15},{14,10},{15,... | collective-permute-start | bytes 786440 | tf_op jit(solution)/shard_map/ppermute | solution.py:31
  75.9 9.3 %collective-permute-start.35 = (bf16[64,2048]{1,0:T(8,128)(2,1)S(1)}, bf16[64,2048]{1,0:T(8,128)(2,1)S(1)}, u32[]{:S(2)}, u32[]{:S(2)}) collective-permute-start(bf16[64,2048]{1,0:T(8,128)(2,1)S(1)} %get-tuple-element.91), channel_id=1, source_target_pairs={{0,2},{1,3},{4,0},{5,1},{8,4},{9,5},{12,8},{13,9},{14,12},{15,13},... | collective-permute-start | bytes 786440 | tf_op jit(solution)/shard_map/ppermute | solution.py:31
  76.5 10.1 %collective-permute-start.34 = (bf16[64,2048]{1,0:T(8,128)(2,1)S(1)}, bf16[64,2048]{1,0:T(8,128)(2,1)S(1)}, u32[]{:S(2)}, u32[]{:S(2)}) collective-permute-start(bf16[64,2048]{1,0:T(8,128)(2,1)S(1)} %get-tuple-element.88.refs_8_), channel_id=1, source_target_pairs={{0,4},{1,5},{4,8},{5,9},{8,12},{9,13},{12,14},{13,15},{14,10},{15,... | collective-permute-start | bytes 786440 | tf_op jit(solution)/shard_map/ppermute | solution.py:31
  81.5 9.3 %collective-permute-start.33 = (bf16[64,2048]{1,0:T(8,128)(2,1)S(1)}, bf16[64,2048]{1,0:T(8,128)(2,1)S(1)}, u32[]{:S(2)}, u32[]{:S(2)}) collective-permute-start(bf16[64,2048]{1,0:T(8,128)(2,1)S(1)} %get-tuple-element.90), channel_id=1, source_target_pairs={{0,2},{1,3},{4,0},{5,1},{8,4},{9,5},{12,8},{13,9},{14,12},{15,13},... | collective-permute-start | bytes 786440 | tf_op jit(solution)/shard_map/ppermute | solution.py:31
  82.1 10.1 %collective-permute-start.32 = (bf16[64,2048]{1,0:T(8,128)(2,1)S(1)}, bf16[64,2048]{1,0:T(8,128)(2,1)S(1)}, u32[]{:S(2)}, u32[]{:S(2)}) collective-permute-start(bf16[64,2048]{1,0:T(8,128)(2,1)S(1)} %get-tuple-element.89.refs_8_), channel_id=1, source_target_pairs={{0,4},{1,5},{4,8},{5,9},{8,12},{9,13},{12,14},{13,15},{14,10},{15,... | collective-permute-start | bytes 786440 | tf_op jit(solution)/shard_map/ppermute | solution.py:31
  87.2 9.3 %collective-permute-start.40 = (bf16[64,2048]{1,0:T(8,128)(2,1)S(1)}, bf16[64,2048]{1,0:T(8,128)(2,1)S(1)}, u32[]{:S(2)}, u32[]{:S(2)}) collective-permute-start(bf16[64,2048]{1,0:T(8,128)(2,1)S(1)} %get-tuple-element.96), channel_id=1, source_target_pairs={{0,2},{1,3},{4,0},{5,1},{8,4},{9,5},{12,8},{13,9},{14,12},{15,13},... | collective-permute-start | bytes 786440 | tf_op jit(solution)/shard_map/ppermute | solution.py:31
  87.7 10.1 %collective-permute-start.39 = (bf16[64,2048]{1,0:T(8,128)(2,1)S(1)}, bf16[64,2048]{1,0:T(8,128)(2,1)S(1)}, u32[]{:S(2)}, u32[]{:S(2)}) collective-permute-start(bf16[64,2048]{1,0:T(8,128)(2,1)S(1)} %get-tuple-element.92.refs_5_), channel_id=1, source_target_pairs={{0,4},{1,5},{4,8},{5,9},{8,12},{9,13},{12,14},{13,15},{14,10},{15,... | collective-permute-start | bytes 786440 | tf_op jit(solution)/shard_map/ppermute | solution.py:31
  92.6 7.7 %collective-permute-start.37 = (bf16[32,2048]{1,0:T(8,128)(2,1)S(1)}, bf16[32,2048]{1,0:T(8,128)(2,1)S(1)}, u32[]{:S(2)}, u32[]{:S(2)}) collective-permute-start(bf16[32,2048]{1,0:T(8,128)(2,1)S(1)} %get-tuple-element.94), channel_id=1, source_target_pairs={{0,2},{1,3},{4,0},{5,1},{8,4},{9,5},{12,8},{13,9},{14,12},{15,13},... | collective-permute-start | bytes 393224 | tf_op jit(solution)/shard_map/ppermute | solution.py:31
  93.2 7.1 %collective-permute-start.36 = (bf16[32,2048]{1,0:T(8,128)(2,1)S(1)}, bf16[32,2048]{1,0:T(8,128)(2,1)S(1)}, u32[]{:S(2)}, u32[]{:S(2)}) collective-permute-start(bf16[32,2048]{1,0:T(8,128)(2,1)S(1)} %get-tuple-element.93.refs_5_), channel_id=1, source_target_pairs={{0,4},{1,5},{4,8},{5,9},{8,12},{9,13},{12,14},{13,15},{14,10},{15,... | collective-permute-start | bytes 393224 | tf_op jit(solution)/shard_map/ppermute | solution.py:31
  98.2 5.0 %collective-permute-start.41 = (bf16[32,2048]{1,0:T(8,128)(2,1)S(1)}, bf16[32,2048]{1,0:T(8,128)(2,1)S(1)}, u32[]{:S(2)}, u32[]{:S(2)}) collective-permute-start(bf16[32,2048]{1,0:T(8,128)(2,1)S(1)} %get-tuple-element.97), channel_id=1, source_target_pairs={{0,4},{1,5},{4,8},{5,9},{8,12},{9,13},{12,14},{13,15},{14,10},{15,... | collective-permute-start | bytes 393224 | tf_op jit(solution)/shard_map/ppermute | solution.py:31
  98.9 5.0 %collective-permute-start.42 = (bf16[32,2048]{1,0:T(8,128)(2,1)S(1)}, bf16[32,2048]{1,0:T(8,128)(2,1)S(1)}, u32[]{:S(2)}, u32[]{:S(2)}) collective-permute-start(bf16[32,2048]{1,0:T(8,128)(2,1)S(1)} %get-tuple-element.98), channel_id=1, source_target_pairs={{0,2},{1,3},{4,0},{5,1},{8,4},{9,5},{12,8},{13,9},{14,12},{15,13},... | collective-permute-start | bytes 393224 | tf_op jit(solution)/shard_map/ppermute | solution.py:31
  100.4 9.3 %collective-permute-start.38 = (bf16[64,2048]{1,0:T(8,128)(2,1)S(1)}, bf16[64,2048]{1,0:T(8,128)(2,1)S(1)}, u32[]{:S(2)}, u32[]{:S(2)}) collective-permute-start(bf16[64,2048]{1,0:T(8,128)(2,1)S(1)} %final.2), channel_id=1, source_target_pairs={{0,16},{16,0},{1,17},{17,1},{2,18},{18,2},{3,19},{19,3},{4,20},{20... | collective-permute-start | bytes 786440 | tf_op jit(solution)/shard_map/ppermute | solution.py:41
  103.9 8.5 %collective-permute-start.43 = (bf16[64,2048]{1,0:T(8,128)(2,1)S(1)}, bf16[64,2048]{1,0:T(8,128)(2,1)S(1)}, u32[]{:S(2)}, u32[]{:S(2)}) collective-permute-start(bf16[64,2048]{1,0:T(8,128)(2,1)S(1)} %final.3), channel_id=1, source_target_pairs={{0,16},{16,0},{1,17},{17,1},{2,18},{18,2},{3,19},{19,3},{4,20},{20... | collective-permute-start | bytes 786440 | tf_op jit(solution)/shard_map/ppermute | solution.py:41
  (5 other events, 7.6 us)

commit v5 on v4

--- a/solution.py
+++ b/solution.py
@@ -119,13 +119,12 @@
     ranks = jnp.where(named, ranks, -1.0)
     slot = lax.broadcasted_iota(jnp.int32, (slots, both), 0).astype(F32)
     rows = jnp.concatenate([part[:, :width] for part in parts], axis=0)
-    hits = jnp.where(slot == ranks[1:2], 1.0, 0.0).astype(BF16)
+    hits = [jnp.where(slot == ranks[e : e + 1], 1.0, 0.0).astype(BF16) for e in range(2)]
+    taken = jnp.dot(jnp.concatenate(hits, axis=0), rows, preferred_element_type=F32).astype(BF16)
+    own[...] = taken[:slots]
     span = width // SWAPS
     for index, other in enumerate(others):
-        part = rows[:, index * span : (index + 1) * span]
-        other[...] = jnp.dot(hits, part, preferred_element_type=F32).astype(BF16)
-    hits = jnp.where(slot == ranks[0:1], 1.0, 0.0).astype(BF16)
-    own[...] = jnp.dot(hits, rows, preferred_element_type=F32).astype(BF16)
+        other[...] = taken[slots:, index * span : (index + 1) * span]
     lines = jnp.where(line < 2, gates, pltpu.roll(ranks, 2, 0))
     spare = jnp.zeros((128 - 8, both), F32)
     info[...] = jnp.concatenate([lines, spare], axis=0).T

time: 115 us -> 115 us (level)
  no operation moved by 1% of the time
where the time goes in v5:
time: 115 us; the launch traced here: 113 us
  waiting for transfers between devices  41.4 us (36%)
  starting transfers between devices  38.5 us (33%)
  Pallas kernels  24.5 us (21%)
  local copies, waits for them, and re-layouts  7.63 us (7%)
    ppermute x32, waiting for transfers between devices, round_ring(): lax.ppermute(shard, 'expert', ring_pairs(lax.axis_size('expert'), by))  33.5 us
    ppermute x32, starting transfers between devices, round_ring(): lax.ppermute(shard, 'expert', ring_pairs(lax.axis_size('expert'), by))  33.2 us
    pallas_call x22, Pallas kernels, call(): pl.pallas_call(body, name=name, out_shape=out_shapes, grid=grid or (), in...  24.5 us
    unnamed x18, local copies, waits for them, and re-layouts  7.59 us
    ppermute x2, waiting for transfers between devices, next_section(): lax.ppermute(shard, 'pipe', [(i, (i + 1) % sections) for i in range(secti...  6.93 us
    ppermute x2, starting transfers between devices, next_section(): lax.ppermute(shard, 'pipe', [(i, (i + 1) % sections) for i in range(secti...  3.2 us
  transfers between devices with their start and end apart: 44, of which 22 were waited for; matrix products, arithmetic and copies ran while one was open for 0% of the time, Pallas kernels for 20%

profile of v5, /device:TPU:10, one launch (start us, length us, event | category | flops | bytes accessed | tf_op | source)
XLA Modules:
  0.0 113.3 jit_solution(5402167038352105395)
XLA Ops:
  0.0 2.2 %prepare.1 = (bf16[64,2176]{1,0:T(8,128)(2,1)}, bf16[64,2048]{1,0:T(8,128)(2,1)}) custom-call(bf16[128,2048]{1,0:T(8,128)(2,1)} %bitcast.30, f32[1,2048]{1,0:T(1,128)} %refs_1_.1, bf16[16,2048]{1,0:T(8,128)(2,1)} %bitcast.32, s32[6,1,128]{2,1,0:T(1,128)} %bitcast.33), custom_call_target="tpu_custom_call" | custom-call | tf_op jit(solution)/shard_map/prepare/pallas_call | solution.py:55
  2.2 1.6 %collective-permute-start.7 = (bf16[64,2048]{1,0:T(8,128)(2,1)}, bf16[64,2048]{1,0:T(8,128)(2,1)S(1)}, u32[]{:S(2)}, u32[]{:S(2)}) collective-permute-start(bf16[64,2048]{1,0:T(8,128)(2,1)} %get-tuple-element.53.refs_2_), channel_id=1, source_target_pairs={{0,2},{1,3},{4,0},{5,1},{8,4},{9,5},{12,8},{13,9},{14,12},{15,13},... | collective-permute-start | bytes 786440 | tf_op jit(solution)/shard_map/ppermute | solution.py:31
  4.3 1.6 %collective-permute-start.6 = (bf16[64,2176]{1,0:T(8,128)(2,1)}, bf16[64,2176]{1,0:T(8,128)(2,1)S(1)}, u32[]{:S(2)}, u32[]{:S(2)}) collective-permute-start(bf16[64,2176]{1,0:T(8,128)(2,1)} %get-tuple-element.52.refs_1_), channel_id=1, source_target_pairs={{0,2},{1,3},{4,0},{5,1},{8,4},{9,5},{12,8},{13,9},{14,12},{15,13},... | collective-permute-start | bytes 835592 | tf_op jit(solution)/shard_map/ppermute | solution.py:31
  6.4 1.9 %copy-done = bf16[1,1,2048,768]{3,2,1,0:T(8,128)(2,1)S(1)} copy-done((bf16[1,1,2048,768]{3,2,1,0:T(8,128)(2,1)S(1)}, bf16[1,1,2048,768]{3,2,1,0:T(8,128)(2,1)}, u32[]{:S(2)}) %copy-start) | copy-done | bytes 3145752
  8.3 1.9 %copy-done.2 = bf16[1,1,2048,768]{3,2,1,0:T(8,128)(2,1)S(1)} copy-done((bf16[1,1,2048,768]{3,2,1,0:T(8,128)(2,1)S(1)}, bf16[1,1,2048,768]{3,2,1,0:T(8,128)(2,1)}, u32[]{:S(2)}) %copy-start.2) | copy-done | bytes 3145752
  10.2 1.9 %copy-done.4 = bf16[1,1,768,2048]{3,2,1,0:T(8,128)(2,1)S(1)} copy-done((bf16[1,1,768,2048]{3,2,1,0:T(8,128)(2,1)S(1)}, bf16[1,1,768,2048]{3,2,1,0:T(8,128)(2,1)}, u32[]{:S(2)}) %copy-start.4) | copy-done | bytes 3145752
  15.1 1.6 %collective-permute-start.11 = (bf16[64,2048]{1,0:T(8,128)(2,1)S(1)}, bf16[64,2048]{1,0:T(8,128)(2,1)S(1)}, u32[]{:S(2)}, u32[]{:S(2)}) collective-permute-start(bf16[64,2048]{1,0:T(8,128)(2,1)S(1)} %collective-permute-done.7.refs_4_), channel_id=1, source_target_pairs={{0,2},{1,3},{4,0},{5,1},{8,4},{9,5},{12,8},{13,9},{14,12},{15,13},... | collective-permute-start | bytes 786440 | tf_op jit(solution)/shard_map/ppermute | solution.py:31
  17.8 1.1 %select2.3 = (bf16[144,2048]{1,0:T(8,128)(2,1)S(1)}, f32[256,128]{1,0:T(8,128)S(1)}, bf16[144,2048]{1,0:T(8,128)(2,1)S(1)}) custom-call(s32[2]{0:T(128)S(1)} %pad_add_fusion.refs_0_, bf16[64,2176]{1,0:T(8,128)(2,1)S(1)} %collective-permute-done.2.refs_1_, bf16[64,2048]{1,0:T(8,128)(2,1)S(1)} %collective-permute-done.5.refs_2_, ...), custom_call_target="tpu_custom_call" | custom-call | flops 400000000 | tf_op jit(solution)/shard_map/select2/pallas_call | solution.py:55
  19.0 1.6 %collective-permute-start.10 = (bf16[64,2176]{1,0:T(8,128)(2,1)S(1)}, bf16[64,2176]{1,0:T(8,128)(2,1)S(1)}, u32[]{:S(2)}, u32[]{:S(2)}) collective-permute-start(bf16[64,2176]{1,0:T(8,128)(2,1)S(1)} %collective-permute-done.6.refs_3_), channel_id=1, source_target_pairs={{0,2},{1,3},{4,0},{5,1},{8,4},{9,5},{12,8},{13,9},{14,12},{15,13},... | collective-permute-start | bytes 835592 | tf_op jit(solution)/shard_map/ppermute | solution.py:31
  21.1 3.1 %collective-permute-done.11.refs_4_ = bf16[64,2048]{1,0:T(8,128)(2,1)S(1)} collective-permute-done((bf16[64,2048]{1,0:T(8,128)(2,1)S(1)}, bf16[64,2048]{1,0:T(8,128)(2,1)S(1)}, u32[]{:S(2)}, u32[]{:S(2)}) %collective-permute-start.11) | collective-permute-done | bytes 262176 | tf_op jit(solution)/shard_map/ppermute | solution.py:31
  24.2 1.6 %collective-permute-start.18 = (bf16[64,2048]{1,0:T(8,128)(2,1)S(1)}, bf16[64,2048]{1,0:T(8,128)(2,1)S(1)}, u32[]{:S(2)}, u32[]{:S(2)}) collective-permute-start(bf16[64,2048]{1,0:T(8,128)(2,1)S(1)} %collective-permute-done.11.refs_4_), channel_id=1, source_target_pairs={{0,2},{1,3},{4,0},{5,1},{8,4},{9,5},{12,8},{13,9},{14,12},{15,13},... | collective-permute-start | bytes 786440 | tf_op jit(solution)/shard_map/ppermute | solution.py:31
  26.3 1.8 %ffn1.2 = (bf16[80,2048]{1,0:T(8,128)(2,1)S(1)}, bf16[80,2048]{1,0:T(8,128)(2,1)S(1)}) custom-call(bf16[80,2048]{1,0:T(8,128)(2,1)S(1)} %get-tuple-element.55.refs_0_, bf16[80,2048]{1,0:T(8,128)(2,1)S(1)} %collective-permute-done.refs_1_, bf16[2048,768]{1,0:T(8,128)(2,1)S(1)} %bitcast.13, bf16[2048,768]{1,0:T(8,128)(2,1)S(1)} %bitcast.19, ...), custom_call_target="tpu_custom_call" | custom-call | flops 4800000000 | tf_op jit(solution)/shard_map/ffn1/pallas_call | solution.py:55
  28.1 2.1 %collective-permute-done.10.refs_3_ = bf16[64,2176]{1,0:T(8,128)(2,1)S(1)} collective-permute-done((bf16[64,2176]{1,0:T(8,128)(2,1)S(1)}, bf16[64,2176]{1,0:T(8,128)(2,1)S(1)}, u32[]{:S(2)}, u32[]{:S(2)}) %collective-permute-start.10) | collective-permute-done | bytes 278560 | tf_op jit(solution)/shard_map/ppermute | solution.py:31
  30.2 1.6 %collective-permute-start.14 = (bf16[64,2176]{1,0:T(8,128)(2,1)S(1)}, bf16[64,2176]{1,0:T(8,128)(2,1)S(1)}, u32[]{:S(2)}, u32[]{:S(2)}) collective-permute-start(bf16[64,2176]{1,0:T(8,128)(2,1)S(1)} %collective-permute-done.10.refs_3_), channel_id=1, source_target_pairs={{0,2},{1,3},{4,0},{5,1},{8,4},{9,5},{12,8},{13,9},{14,12},{15,13},... | collective-permute-start | bytes 835592 | tf_op jit(solution)/shard_map/ppermute | solution.py:31
  32.3 3.5 %collective-permute-done.18.refs_4_ = bf16[64,2048]{1,0:T(8,128)(2,1)S(1)} collective-permute-done((bf16[64,2048]{1,0:T(8,128)(2,1)S(1)}, bf16[64,2048]{1,0:T(8,128)(2,1)S(1)}, u32[]{:S(2)}, u32[]{:S(2)}) %collective-permute-start.18) | collective-permute-done | bytes 262176 | tf_op jit(solution)/shard_map/ppermute | solution.py:31
  35.8 1.6 %collective-permute-start.19 = (bf16[32,2048]{1,0:T(8,128)(2,1)S(1)}, bf16[32,2048]{1,0:T(8,128)(2,1)S(1)}, u32[]{:S(2)}, u32[]{:S(2)}) collective-permute-start(bf16[32,2048]{1,0:T(8,128)(2,1)S(1)} %slice.17), channel_id=1, source_target_pairs={{0,2},{1,3},{4,0},{5,1},{8,4},{9,5},{12,8},{13,9},{14,12},{15,13},... | collective-permute-start | bytes 393224 | tf_op jit(solution)/shard_map/ppermute | solution.py:31
  38.0 1.1 %select2.4 = (bf16[144,2048]{1,0:T(8,128)(2,1)S(1)}, f32[256,128]{1,0:T(8,128)S(1)}, bf16[144,2048]{1,0:T(8,128)(2,1)S(1)}) custom-call(s32[2]{0:T(128)S(1)} %pad_add_fusion.refs_0_, bf16[64,2176]{1,0:T(8,128)(2,1)S(1)} %collective-permute-done.3.refs_1_, bf16[64,2048]{1,0:T(8,128)(2,1)S(1)} %collective-permute-done.9.refs_2_, ...), custom_call_target="tpu_custom_call" | custom-call | flops 400000000 | tf_op jit(solution)/shard_map/select2/pallas_call | solution.py:55
  39.2 3.0 %ffn2.3 = (bf16[144,2048]{1,0:T(8,128)(2,1)S(1)}, bf16[144,2048]{1,0:T(8,128)(2,1)S(1)}) custom-call(bf16[144,2048]{1,0:T(8,128)(2,1)S(1)} %get-tuple-element.59.refs_0_, bf16[144,2048]{1,0:T(8,128)(2,1)S(1)} %collective-permute-done.8.refs_1_.refs_5_, bf16[2048,768]{1,0:T(8,128)(2,1)S(1)} %bitcast.14, bf16[2048,768]{1,0:T(8,128)(2,1)S(1)} %bitcast.20, ...), custom_call_target="tpu_custom_call" | custom-call | flops 8640000000 | tf_op jit(solution)/shard_map/ffn2/pallas_call | solution.py:55
  42.2 1.2 %collective-permute-done.4.refs_1_ = bf16[64,2176]{1,0:T(8,128)(2,1)S(1)} collective-permute-done((bf16[64,2176]{1,0:T(8,128)(2,1)S(1)}, bf16[64,2176]{1,0:T(8,128)(2,1)S(1)}, u32[]{:S(2)}, u32[]{:S(2)}) %collective-permute-start.4) | collective-permute-done | bytes 278560 | tf_op jit(solution)/shard_map/ppermute | solution.py:31
  43.5 1.6 %collective-permute-start.15 = (bf16[32,2176]{1,0:T(8,128)(2,1)S(1)}, bf16[32,2176]{1,0:T(8,128)(2,1)S(1)}, u32[]{:S(2)}, u32[]{:S(2)}) collective-permute-start(bf16[32,2176]{1,0:T(8,128)(2,1)S(1)} %slice.13), channel_id=1, source_target_pairs={{0,2},{1,3},{4,0},{5,1},{8,4},{9,5},{12,8},{13,9},{14,12},{15,13},... | collective-permute-start | bytes 417800 | tf_op jit(solution)/shard_map/ppermute | solution.py:31
  46.8 3.0 %ffn2.4 = (bf16[144,2048]{1,0:T(8,128)(2,1)S(1)}, bf16[144,2048]{1,0:T(8,128)(2,1)S(1)}) custom-call(bf16[144,2048]{1,0:T(8,128)(2,1)S(1)} %get-tuple-element.65.refs_0_, bf16[144,2048]{1,0:T(8,128)(2,1)S(1)} %collective-permute-done.12.refs_1_.refs_5_, bf16[2048,768]{1,0:T(8,128)(2,1)S(1)} %bitcast.15, bf16[2048,768]{1,0:T(8,128)(2,1)S(1)} %bitcast.21, ...), custom_call_target="tpu_custom_call" | custom-call | flops 8640000000 | tf_op jit(solution)/shard_map/ffn2/pallas_call | solution.py:55
  51.4 3.0 %ffn2.5 = (bf16[144,2048]{1,0:T(8,128)(2,1)S(1)}, bf16[144,2048]{1,0:T(8,128)(2,1)S(1)}) custom-call(bf16[144,2048]{1,0:T(8,128)(2,1)S(1)} %get-tuple-element.70.refs_0_, bf16[144,2048]{1,0:T(8,128)(2,1)S(1)} %collective-permute-done.21.refs_1_, bf16[2048,768]{1,0:T(8,128)(2,1)S(1)} %bitcast.16, bf16[2048,768]{1,0:T(8,128)(2,1)S(1)} %bitcast.22, ...), custom_call_target="tpu_custom_call" | custom-call | flops 8640000000 | tf_op jit(solution)/shard_map/ffn2/pallas_call | solution.py:55
  54.9 1.8 %ffn1.3 = (bf16[80,2048]{1,0:T(8,128)(2,1)S(1)}, bf16[80,2048]{1,0:T(8,128)(2,1)S(1)}) custom-call(bf16[80,2048]{1,0:T(8,128)(2,1)S(1)} %get-tuple-element.68.refs_0_, bf16[80,2048]{1,0:T(8,128)(2,1)S(1)} %collective-permute-done.20.refs_1_, bf16[2048,768]{1,0:T(8,128)(2,1)S(1)} %bitcast.17, bf16[2048,768]{1,0:T(8,128)(2,1)S(1)} %bitcast.23, ...), custom_call_target="tpu_custom_call" | custom-call | flops 4800000000 | tf_op jit(solution)/shard_map/ffn1/pallas_call | solution.py:55
  58.9 1.6 %collective-permute-start.27 = (bf16[64,2048]{1,0:T(8,128)(2,1)S(1)}, bf16[64,2048]{1,0:T(8,128)(2,1)S(1)}, u32[]{:S(2)}, u32[]{:S(2)}) collective-permute-start(bf16[64,2048]{1,0:T(8,128)(2,1)S(1)} %get-tuple-element.84), channel_id=1, source_target_pairs={{0,2},{1,3},{4,0},{5,1},{8,4},{9,5},{12,8},{13,9},{14,12},{15,13},... | collective-permute-start | bytes 786440 | tf_op jit(solution)/shard_map/ppermute | solution.py:31
  61.5 1.6 %collective-permute-start.31 = (bf16[64,2048]{1,0:T(8,128)(2,1)S(1)}, bf16[64,2048]{1,0:T(8,128)(2,1)S(1)}, u32[]{:S(2)}, u32[]{:S(2)}) collective-permute-start(bf16[64,2048]{1,0:T(8,128)(2,1)S(1)} %get-tuple-element.87), channel_id=1, source_target_pairs={{0,2},{1,3},{4,0},{5,1},{8,4},{9,5},{12,8},{13,9},{14,12},{15,13},... | collective-permute-start | bytes 786440 | tf_op jit(solution)/shard_map/ppermute | solution.py:31
  64.1 4.0 %collective-permute-done.27.refs_7_ = bf16[64,2048]{1,0:T(8,128)(2,1)S(1)} collective-permute-done((bf16[64,2048]{1,0:T(8,128)(2,1)S(1)}, bf16[64,2048]{1,0:T(8,128)(2,1)S(1)}, u32[]{:S(2)}, u32[]{:S(2)}) %collective-permute-start.27) | collective-permute-done | bytes 262176 | tf_op jit(solution)/shard_map/ppermute | solution.py:31
  68.1 1.6 %collective-permute-done.26.refs_6_ = bf16[64,2048]{1,0:T(8,128)(2,1)S(1)} collective-permute-done((bf16[64,2048]{1,0:T(8,128)(2,1)S(1)}, bf16[64,2048]{1,0:T(8,128)(2,1)S(1)}, u32[]{:S(2)}, u32[]{:S(2)}) %collective-permute-start.26) | collective-permute-done | bytes 262176 | tf_op jit(solution)/shard_map/ppermute | solution.py:31
  70.8 1.5 %collective-permute-start.28 = (bf16[64,2048]{1,0:T(8,128)(2,1)S(1)}, bf16[64,2048]{1,0:T(8,128)(2,1)S(1)}, u32[]{:S(2)}, u32[]{:S(2)}) collective-permute-start(bf16[64,2048]{1,0:T(8,128)(2,1)S(1)} %get-tuple-element.85.refs_8_), channel_id=1, source_target_pairs={{0,4},{1,5},{4,8},{5,9},{8,12},{9,13},{12,14},{13,15},{14,10},{15,... | collective-permute-start | bytes 786440 | tf_op jit(solution)/shard_map/ppermute | solution.py:31
  72.3 1.4 %collective-permute-done.31.refs_7_ = bf16[64,2048]{1,0:T(8,128)(2,1)S(1)} collective-permute-done((bf16[64,2048]{1,0:T(8,128)(2,1)S(1)}, bf16[64,2048]{1,0:T(8,128)(2,1)S(1)}, u32[]{:S(2)}, u32[]{:S(2)}) %collective-permute-start.31) | collective-permute-done | bytes 262176 | tf_op jit(solution)/shard_map/ppermute | solution.py:31
  73.7 1.6 %collective-permute-done.30.refs_6_ = bf16[64,2048]{1,0:T(8,128)(2,1)S(1)} collective-permute-done((bf16[64,2048]{1,0:T(8,128)(2,1)S(1)}, bf16[64,2048]{1,0:T(8,128)(2,1)S(1)}, u32[]{:S(2)}, u32[]{:S(2)}) %collective-permute-start.30) | collective-permute-done | bytes 262176 | tf_op jit(solution)/shard_map/ppermute | solution.py:31
  76.4 1.5 %collective-permute-start.34 = (bf16[64,2048]{1,0:T(8,128)(2,1)S(1)}, bf16[64,2048]{1,0:T(8,128)(2,1)S(1)}, u32[]{:S(2)}, u32[]{:S(2)}) collective-permute-start(bf16[64,2048]{1,0:T(8,128)(2,1)S(1)} %get-tuple-element.88.refs_8_), channel_id=1, source_target_pairs={{0,4},{1,5},{4,8},{5,9},{8,12},{9,13},{12,14},{13,15},{14,10},{15,... | collective-permute-start | bytes 786440 | tf_op jit(solution)/shard_map/ppermute | solution.py:31
  77.9 1.6 %collective-permute-done.29.refs_7_ = bf16[64,2048]{1,0:T(8,128)(2,1)S(1)} collective-permute-done((bf16[64,2048]{1,0:T(8,128)(2,1)S(1)}, bf16[64,2048]{1,0:T(8,128)(2,1)S(1)}, u32[]{:S(2)}, u32[]{:S(2)}) %collective-permute-start.29) | collective-permute-done | bytes 262176 | tf_op jit(solution)/shard_map/ppermute | solution.py:31
  79.5 1.4 %collective-permute-done.28.refs_6_ = bf16[64,2048]{1,0:T(8,128)(2,1)S(1)} collective-permute-done((bf16[64,2048]{1,0:T(8,128)(2,1)S(1)}, bf16[64,2048]{1,0:T(8,128)(2,1)S(1)}, u32[]{:S(2)}, u32[]{:S(2)}) %collective-permute-start.28) | collective-permute-done | bytes 262176 | tf_op jit(solution)/shard_map/ppermute | solution.py:31
  82.1 1.5 %collective-permute-start.32 = (bf16[64,2048]{1,0:T(8,128)(2,1)S(1)}, bf16[64,2048]{1,0:T(8,128)(2,1)S(1)}, u32[]{:S(2)}, u32[]{:S(2)}) collective-permute-start(bf16[64,2048]{1,0:T(8,128)(2,1)S(1)} %get-tuple-element.89.refs_8_), channel_id=1, source_target_pairs={{0,4},{1,5},{4,8},{5,9},{8,12},{9,13},{12,14},{13,15},{14,10},{15,... | collective-permute-start | bytes 786440 | tf_op jit(solution)/shard_map/ppermute | solution.py:31
  83.6 1.6 %collective-permute-done.35.refs_7_ = bf16[64,2048]{1,0:T(8,128)(2,1)S(1)} collective-permute-done((bf16[64,2048]{1,0:T(8,128)(2,1)S(1)}, bf16[64,2048]{1,0:T(8,128)(2,1)S(1)}, u32[]{:S(2)}, u32[]{:S(2)}) %collective-permute-start.35) | collective-permute-done | bytes 262176 | tf_op jit(solution)/shard_map/ppermute | solution.py:31
  85.2 1.4 %collective-permute-done.34.refs_6_ = bf16[64,2048]{1,0:T(8,128)(2,1)S(1)} collective-permute-done((bf16[64,2048]{1,0:T(8,128)(2,1)S(1)}, bf16[64,2048]{1,0:T(8,128)(2,1)S(1)}, u32[]{:S(2)}, u32[]{:S(2)}) %collective-permute-start.34) | collective-permute-done | bytes 262176 | tf_op jit(solution)/shard_map/ppermute | solution.py:31
  87.7 1.5 %collective-permute-start.39 = (bf16[64,2048]{1,0:T(8,128)(2,1)S(1)}, bf16[64,2048]{1,0:T(8,128)(2,1)S(1)}, u32[]{:S(2)}, u32[]{:S(2)}) collective-permute-start(bf16[64,2048]{1,0:T(8,128)(2,1)S(1)} %get-tuple-element.92.refs_5_), channel_id=1, source_target_pairs={{0,4},{1,5},{4,8},{5,9},{8,12},{9,13},{12,14},{13,15},{14,10},{15,... | collective-permute-start | bytes 786440 | tf_op jit(solution)/shard_map/ppermute | solution.py:31
  89.2 1.6 %collective-permute-done.33.refs_4_.refs_3_ = bf16[64,2048]{1,0:T(8,128)(2,1)S(1)} collective-permute-done((bf16[64,2048]{1,0:T(8,128)(2,1)S(1)}, bf16[64,2048]{1,0:T(8,128)(2,1)S(1)}, u32[]{:S(2)}, u32[]{:S(2)}) %collective-permute-start.33) | collective-permute-done | bytes 262176 | tf_op jit(solution)/shard_map/ppermute | solution.py:31
  90.8 1.4 %collective-permute-done.32.refs_3_.refs_1_ = bf16[64,2048]{1,0:T(8,128)(2,1)S(1)} collective-permute-done((bf16[64,2048]{1,0:T(8,128)(2,1)S(1)}, bf16[64,2048]{1,0:T(8,128)(2,1)S(1)}, u32[]{:S(2)}, u32[]{:S(2)}) %collective-permute-start.32) | collective-permute-done | bytes 262176 | tf_op jit(solution)/shard_map/ppermute | solution.py:31
  93.1 1.5 %collective-permute-start.36 = (bf16[32,2048]{1,0:T(8,128)(2,1)S(1)}, bf16[32,2048]{1,0:T(8,128)(2,1)S(1)}, u32[]{:S(2)}, u32[]{:S(2)}) collective-permute-start(bf16[32,2048]{1,0:T(8,128)(2,1)S(1)} %get-tuple-element.93.refs_5_), channel_id=1, source_target_pairs={{0,4},{1,5},{4,8},{5,9},{8,12},{9,13},{12,14},{13,15},{14,10},{15,... | collective-permute-start | bytes 393224 | tf_op jit(solution)/shard_map/ppermute | solution.py:31
  94.6 1.8 %collective-permute-done.40.refs_4_.refs_3_ = bf16[64,2048]{1,0:T(8,128)(2,1)S(1)} collective-permute-done((bf16[64,2048]{1,0:T(8,128)(2,1)S(1)}, bf16[64,2048]{1,0:T(8,128)(2,1)S(1)}, u32[]{:S(2)}, u32[]{:S(2)}) %collective-permute-start.40) | collective-permute-done | bytes 262176 | tf_op jit(solution)/shard_map/ppermute | solution.py:31
  96.4 1.4 %collective-permute-done.39.refs_3_.refs_1_ = bf16[64,2048]{1,0:T(8,128)(2,1)S(1)} collective-permute-done((bf16[64,2048]{1,0:T(8,128)(2,1)S(1)}, bf16[64,2048]{1,0:T(8,128)(2,1)S(1)}, u32[]{:S(2)}, u32[]{:S(2)}) %collective-permute-start.39) | collective-permute-done | bytes 262176 | tf_op jit(solution)/shard_map/ppermute | solution.py:31
  98.8 1.4 %collective-permute-start.42 = (bf16[32,2048]{1,0:T(8,128)(2,1)S(1)}, bf16[32,2048]{1,0:T(8,128)(2,1)S(1)}, u32[]{:S(2)}, u32[]{:S(2)}) collective-permute-start(bf16[32,2048]{1,0:T(8,128)(2,1)S(1)} %get-tuple-element.98), channel_id=1, source_target_pairs={{0,2},{1,3},{4,0},{5,1},{8,4},{9,5},{12,8},{13,9},{14,12},{15,13},... | collective-permute-start | bytes 393224 | tf_op jit(solution)/shard_map/ppermute | solution.py:31
  100.3 1.6 %collective-permute-start.38 = (bf16[64,2048]{1,0:T(8,128)(2,1)S(1)}, bf16[64,2048]{1,0:T(8,128)(2,1)S(1)}, u32[]{:S(2)}, u32[]{:S(2)}) collective-permute-start(bf16[64,2048]{1,0:T(8,128)(2,1)S(1)} %final.2), channel_id=1, source_target_pairs={{0,16},{16,0},{1,17},{17,1},{2,18},{18,2},{3,19},{19,3},{4,20},{20... | collective-permute-start | bytes 786440 | tf_op jit(solution)/shard_map/ppermute | solution.py:41
  101.9 1.2 %collective-permute-done.41.refs_2_ = bf16[32,2048]{1,0:T(8,128)(2,1)S(1)} collective-permute-done((bf16[32,2048]{1,0:T(8,128)(2,1)S(1)}, bf16[32,2048]{1,0:T(8,128)(2,1)S(1)}, u32[]{:S(2)}, u32[]{:S(2)}) %collective-permute-start.41) | collective-permute-done | bytes 131104 | tf_op jit(solution)/shard_map/ppermute | solution.py:31
  103.9 1.6 %collective-permute-start.43 = (bf16[64,2048]{1,0:T(8,128)(2,1)S(1)}, bf16[64,2048]{1,0:T(8,128)(2,1)S(1)}, u32[]{:S(2)}, u32[]{:S(2)}) collective-permute-start(bf16[64,2048]{1,0:T(8,128)(2,1)S(1)} %final.3), channel_id=1, source_target_pairs={{0,16},{16,0},{1,17},{17,1},{2,18},{18,2},{3,19},{19,3},{4,20},{20... | collective-permute-start | bytes 786440 | tf_op jit(solution)/shard_map/ppermute | solution.py:41
  105.5 4.1 %collective-permute-done.38 = bf16[64,2048]{1,0:T(8,128)(2,1)S(1)} collective-permute-done((bf16[64,2048]{1,0:T(8,128)(2,1)S(1)}, bf16[64,2048]{1,0:T(8,128)(2,1)S(1)}, u32[]{:S(2)}, u32[]{:S(2)}) %collective-permute-start.38) | collective-permute-done | bytes 262176 | tf_op jit(solution)/shard_map/ppermute | solution.py:41
  109.6 2.8 %collective-permute-done.43 = bf16[64,2048]{1,0:T(8,128)(2,1)S(1)} collective-permute-done((bf16[64,2048]{1,0:T(8,128)(2,1)S(1)}, bf16[64,2048]{1,0:T(8,128)(2,1)S(1)}, u32[]{:S(2)}, u32[]{:S(2)}) %collective-permute-start.43) | collective-permute-done | bytes 262176 | tf_op jit(solution)/shard_map/ppermute | solution.py:41
  (86 shorter events, 23.2 us)
Async XLA Ops:
  2.2 12.8 %collective-permute-start.7 = (bf16[64,2048]{1,0:T(8,128)(2,1)}, bf16[64,2048]{1,0:T(8,128)(2,1)S(1)}, u32[]{:S(2)}, u32[]{:S(2)}) collective-permute-start(bf16[64,2048]{1,0:T(8,128)(2,1)} %get-tuple-element.53.refs_2_), channel_id=1, source_target_pairs={{0,2},{1,3},{4,0},{5,1},{8,4},{9,5},{12,8},{13,9},{14,12},{15,13},... | collective-permute-start | bytes 786440 | tf_op jit(solution)/shard_map/ppermute | solution.py:31
  3.9 12.8 %collective-permute-start.5 = (bf16[64,2048]{1,0:T(8,128)(2,1)}, bf16[64,2048]{1,0:T(8,128)(2,1)S(1)}, u32[]{:S(2)}, u32[]{:S(2)}) collective-permute-start(bf16[64,2048]{1,0:T(8,128)(2,1)} %get-tuple-element.53.refs_2_), channel_id=1, source_target_pairs={{0,4},{1,5},{4,8},{5,9},{8,12},{9,13},{12,14},{13,15},{14,10},{15,... | collective-permute-start | bytes 786440 | tf_op jit(solution)/shard_map/ppermute | solution.py:31
  4.3 12.9 %collective-permute-start.6 = (bf16[64,2176]{1,0:T(8,128)(2,1)}, bf16[64,2176]{1,0:T(8,128)(2,1)S(1)}, u32[]{:S(2)}, u32[]{:S(2)}) collective-permute-start(bf16[64,2176]{1,0:T(8,128)(2,1)} %get-tuple-element.52.refs_1_), channel_id=1, source_target_pairs={{0,2},{1,3},{4,0},{5,1},{8,4},{9,5},{12,8},{13,9},{14,12},{15,13},... | collective-permute-start | bytes 835592 | tf_op jit(solution)/shard_map/ppermute | solution.py:31
  5.9 11.9 %collective-permute-start.2 = (bf16[64,2176]{1,0:T(8,128)(2,1)}, bf16[64,2176]{1,0:T(8,128)(2,1)S(1)}, u32[]{:S(2)}, u32[]{:S(2)}) collective-permute-start(bf16[64,2176]{1,0:T(8,128)(2,1)} %get-tuple-element.52.refs_1_), channel_id=1, source_target_pairs={{0,4},{1,5},{4,8},{5,9},{8,12},{9,13},{12,14},{13,15},{14,10},{15,... | collective-permute-start | bytes 835592 | tf_op jit(solution)/shard_map/ppermute | solution.py:31
  14.0 12.3 %copy-start.1 = (bf16[1,1,2048,768]{3,2,1,0:T(8,128)(2,1)S(1)}, bf16[1,1,2048,768]{3,2,1,0:T(8,128)(2,1)}, u32[]{:S(2)}) copy-start(bf16[1,1,2048,768]{3,2,1,0:T(8,128)(2,1)} %param.11) | copy-start | bytes 9437188
  14.0 12.3 %copy-start.3 = (bf16[1,1,2048,768]{3,2,1,0:T(8,128)(2,1)S(1)}, bf16[1,1,2048,768]{3,2,1,0:T(8,128)(2,1)}, u32[]{:S(2)}) copy-start(bf16[1,1,2048,768]{3,2,1,0:T(8,128)(2,1)} %param.12) | copy-start | bytes 9437188
  14.0 12.3 %copy-start.5 = (bf16[1,1,768,2048]{3,2,1,0:T(8,128)(2,1)S(1)}, bf16[1,1,768,2048]{3,2,1,0:T(8,128)(2,1)}, u32[]{:S(2)}) copy-start(bf16[1,1,768,2048]{3,2,1,0:T(8,128)(2,1)} %param.13) | copy-start | bytes 9437188
  15.0 5.7 %collective-permute-start = (bf16[80,2048]{1,0:T(8,128)(2,1)S(1)}, bf16[80,2048]{1,0:T(8,128)(2,1)S(1)}, u32[]{:S(2)}, u32[]{:S(2)}) collective-permute-start(bf16[80,2048]{1,0:T(8,128)(2,1)S(1)} %get-tuple-element.56), channel_id=1, source_target_pairs={{0,1},{1,0},{2,3},{3,2},{4,5},{5,4},{6,7},{7,6},{8,9},{9,8},{10,11... | collective-permute-start | bytes 983048 | tf_op jit(solution)/shard_map/ppermute | solution.py:36
  15.1 9.2 %collective-permute-start.11 = (bf16[64,2048]{1,0:T(8,128)(2,1)S(1)}, bf16[64,2048]{1,0:T(8,128)(2,1)S(1)}, u32[]{:S(2)}, u32[]{:S(2)}) collective-permute-start(bf16[64,2048]{1,0:T(8,128)(2,1)S(1)} %collective-permute-done.7.refs_4_), channel_id=1, source_target_pairs={{0,2},{1,3},{4,0},{5,1},{8,4},{9,5},{12,8},{13,9},{14,12},{15,13},... | collective-permute-start | bytes 786440 | tf_op jit(solution)/shard_map/ppermute | solution.py:31
  16.7 9.2 %collective-permute-start.9 = (bf16[64,2048]{1,0:T(8,128)(2,1)S(1)}, bf16[64,2048]{1,0:T(8,128)(2,1)S(1)}, u32[]{:S(2)}, u32[]{:S(2)}) collective-permute-start(bf16[64,2048]{1,0:T(8,128)(2,1)S(1)} %collective-permute-done.5.refs_2_), channel_id=1, source_target_pairs={{0,4},{1,5},{4,8},{5,9},{8,12},{9,13},{12,14},{13,15},{14,10},{15,... | collective-permute-start | bytes 786440 | tf_op jit(solution)/shard_map/ppermute | solution.py:31
  19.0 19.0 %collective-permute-start.8 = (bf16[144,2048]{1,0:T(8,128)(2,1)S(1)}, bf16[144,2048]{1,0:T(8,128)(2,1)S(1)}, u32[]{:S(2)}, u32[]{:S(2)}) collective-permute-start(bf16[144,2048]{1,0:T(8,128)(2,1)S(1)} %get-tuple-element.60), channel_id=1, source_target_pairs={{0,1},{1,0},{2,3},{3,2},{4,5},{5,4},{6,7},{7,6},{8,9},{9,8},{10,11... | collective-permute-start | bytes 1769480 | tf_op jit(solution)/shard_map/ppermute | solution.py:36
  19.0 11.2 %collective-permute-start.10 = (bf16[64,2176]{1,0:T(8,128)(2,1)S(1)}, bf16[64,2176]{1,0:T(8,128)(2,1)S(1)}, u32[]{:S(2)}, u32[]{:S(2)}) collective-permute-start(bf16[64,2176]{1,0:T(8,128)(2,1)S(1)} %collective-permute-done.6.refs_3_), channel_id=1, source_target_pairs={{0,2},{1,3},{4,0},{5,1},{8,4},{9,5},{12,8},{13,9},{14,12},{15,13},... | collective-permute-start | bytes 835592 | tf_op jit(solution)/shard_map/ppermute | solution.py:31
  20.7 11.2 %collective-permute-start.3 = (bf16[64,2176]{1,0:T(8,128)(2,1)S(1)}, bf16[64,2176]{1,0:T(8,128)(2,1)S(1)}, u32[]{:S(2)}, u32[]{:S(2)}) collective-permute-start(bf16[64,2176]{1,0:T(8,128)(2,1)S(1)} %collective-permute-done.2.refs_1_), channel_id=1, source_target_pairs={{0,4},{1,5},{4,8},{5,9},{8,12},{9,13},{12,14},{13,15},{14,10},{15,... | collective-permute-start | bytes 835592 | tf_op jit(solution)/shard_map/ppermute | solution.py:31
  24.2 11.6 %collective-permute-start.18 = (bf16[64,2048]{1,0:T(8,128)(2,1)S(1)}, bf16[64,2048]{1,0:T(8,128)(2,1)S(1)}, u32[]{:S(2)}, u32[]{:S(2)}) collective-permute-start(bf16[64,2048]{1,0:T(8,128)(2,1)S(1)} %collective-permute-done.11.refs_4_), channel_id=1, source_target_pairs={{0,2},{1,3},{4,0},{5,1},{8,4},{9,5},{12,8},{13,9},{14,12},{15,13},... | collective-permute-start | bytes 786440 | tf_op jit(solution)/shard_map/ppermute | solution.py:31
  25.9 11.6 %collective-permute-start.16 = (bf16[64,2048]{1,0:T(8,128)(2,1)S(1)}, bf16[64,2048]{1,0:T(8,128)(2,1)S(1)}, u32[]{:S(2)}, u32[]{:S(2)}) collective-permute-start(bf16[64,2048]{1,0:T(8,128)(2,1)S(1)} %collective-permute-done.9.refs_2_), channel_id=1, source_target_pairs={{0,4},{1,5},{4,8},{5,9},{8,12},{9,13},{12,14},{13,15},{14,10},{15,... | collective-permute-start | bytes 786440 | tf_op jit(solution)/shard_map/ppermute | solution.py:31
  30.2 12.0 %collective-permute-start.14 = (bf16[64,2176]{1,0:T(8,128)(2,1)S(1)}, bf16[64,2176]{1,0:T(8,128)(2,1)S(1)}, u32[]{:S(2)}, u32[]{:S(2)}) collective-permute-start(bf16[64,2176]{1,0:T(8,128)(2,1)S(1)} %collective-permute-done.10.refs_3_), channel_id=1, source_target_pairs={{0,2},{1,3},{4,0},{5,1},{8,4},{9,5},{12,8},{13,9},{14,12},{15,13},... | collective-permute-start | bytes 835592 | tf_op jit(solution)/shard_map/ppermute | solution.py:31
  31.8 11.6 %collective-permute-start.4 = (bf16[64,2176]{1,0:T(8,128)(2,1)S(1)}, bf16[64,2176]{1,0:T(8,128)(2,1)S(1)}, u32[]{:S(2)}, u32[]{:S(2)}) collective-permute-start(bf16[64,2176]{1,0:T(8,128)(2,1)S(1)} %collective-permute-done.3.refs_1_), channel_id=1, source_target_pairs={{0,4},{1,5},{4,8},{5,9},{8,12},{9,13},{12,14},{13,15},{14,10},{15,... | collective-permute-start | bytes 835592 | tf_op jit(solution)/shard_map/ppermute | solution.py:31
  35.8 13.9 %collective-permute-start.19 = (bf16[32,2048]{1,0:T(8,128)(2,1)S(1)}, bf16[32,2048]{1,0:T(8,128)(2,1)S(1)}, u32[]{:S(2)}, u32[]{:S(2)}) collective-permute-start(bf16[32,2048]{1,0:T(8,128)(2,1)S(1)} %slice.17), channel_id=1, source_target_pairs={{0,2},{1,3},{4,0},{5,1},{8,4},{9,5},{12,8},{13,9},{14,12},{15,13},... | collective-permute-start | bytes 393224 | tf_op jit(solution)/shard_map/ppermute | solution.py:31
  37.5 12.8 %collective-permute-start.17 = (bf16[32,2048]{1,0:T(8,128)(2,1)S(1)}, bf16[32,2048]{1,0:T(8,128)(2,1)S(1)}, u32[]{:S(2)}, u32[]{:S(2)}) collective-permute-start(bf16[32,2048]{1,0:T(8,128)(2,1)S(1)} %slice.16), channel_id=1, source_target_pairs={{0,4},{1,5},{4,8},{5,9},{8,12},{9,13},{12,14},{13,15},{14,10},{15,... | collective-permute-start | bytes 393224 | tf_op jit(solution)/shard_map/ppermute | solution.py:31
  39.2 3.1 %collective-permute-start.12 = (bf16[144,2048]{1,0:T(8,128)(2,1)S(1)}, bf16[144,2048]{1,0:T(8,128)(2,1)S(1)}, u32[]{:S(2)}, u32[]{:S(2)}) collective-permute-start(bf16[144,2048]{1,0:T(8,128)(2,1)S(1)} %get-tuple-element.62), channel_id=1, source_target_pairs={{0,1},{1,0},{2,3},{3,2},{4,5},{5,4},{6,7},{7,6},{8,9},{9,8},{10,11... | collective-permute-start | bytes 1769480 | tf_op jit(solution)/shard_map/ppermute | solution.py:36
  43.5 6.8 %collective-permute-start.15 = (bf16[32,2176]{1,0:T(8,128)(2,1)S(1)}, bf16[32,2176]{1,0:T(8,128)(2,1)S(1)}, u32[]{:S(2)}, u32[]{:S(2)}) collective-permute-start(bf16[32,2176]{1,0:T(8,128)(2,1)S(1)} %slice.13), channel_id=1, source_target_pairs={{0,2},{1,3},{4,0},{5,1},{8,4},{9,5},{12,8},{13,9},{14,12},{15,13},... | collective-permute-start | bytes 417800 | tf_op jit(solution)/shard_map/ppermute | solution.py:31
  45.1 5.2 %collective-permute-start.13 = (bf16[32,2176]{1,0:T(8,128)(2,1)S(1)}, bf16[32,2176]{1,0:T(8,128)(2,1)S(1)}, u32[]{:S(2)}, u32[]{:S(2)}) collective-permute-start(bf16[32,2176]{1,0:T(8,128)(2,1)S(1)} %slice.12), channel_id=1, source_target_pairs={{0,4},{1,5},{4,8},{5,9},{8,12},{9,13},{12,14},{13,15},{14,10},{15,... | collective-permute-start | bytes 417800 | tf_op jit(solution)/shard_map/ppermute | solution.py:31
  46.7 4.7 %collective-permute-start.21 = (bf16[144,2048]{1,0:T(8,128)(2,1)S(1)}, bf16[144,2048]{1,0:T(8,128)(2,1)S(1)}, u32[]{:S(2)}, u32[]{:S(2)}) collective-permute-start(bf16[144,2048]{1,0:T(8,128)(2,1)S(1)} %get-tuple-element.71), channel_id=1, source_target_pairs={{0,1},{1,0},{2,3},{3,2},{4,5},{5,4},{6,7},{7,6},{8,9},{9,8},{10,11... | collective-permute-start | bytes 1769480 | tf_op jit(solution)/shard_map/ppermute | solution.py:36
  49.8 13.4 %collective-permute-start.24 = (bf16[144,2048]{1,0:T(8,128)(2,1)S(1)}, bf16[144,2048]{1,0:T(8,128)(2,1)S(1)}, u32[]{:S(2)}, u32[]{:S(2)}) collective-permute-start(bf16[144,2048]{1,0:T(8,128)(2,1)S(1)} %get-tuple-element.81), channel_id=1, source_target_pairs={{0,1},{1,0},{2,3},{3,2},{4,5},{5,4},{6,7},{7,6},{8,9},{9,8},{10,11... | collective-permute-start | bytes 1769480 | tf_op jit(solution)/shard_map/ppermute | solution.py:36
  51.3 3.6 %collective-permute-start.20 = (bf16[80,2048]{1,0:T(8,128)(2,1)S(1)}, bf16[80,2048]{1,0:T(8,128)(2,1)S(1)}, u32[]{:S(2)}, u32[]{:S(2)}) collective-permute-start(bf16[80,2048]{1,0:T(8,128)(2,1)S(1)} %get-tuple-element.69), channel_id=1, source_target_pairs={{0,1},{1,0},{2,3},{3,2},{4,5},{5,4},{6,7},{7,6},{8,9},{9,8},{10,11... | collective-permute-start | bytes 983048 | tf_op jit(solution)/shard_map/ppermute | solution.py:36
  54.4 4.0 %collective-permute-start.23 = (bf16[144,2048]{1,0:T(8,128)(2,1)S(1)}, bf16[144,2048]{1,0:T(8,128)(2,1)S(1)}, u32[]{:S(2)}, u32[]{:S(2)}) collective-permute-start(bf16[144,2048]{1,0:T(8,128)(2,1)S(1)} %get-tuple-element.76), channel_id=1, source_target_pairs={{0,1},{1,0},{2,3},{3,2},{4,5},{5,4},{6,7},{7,6},{8,9},{9,8},{10,11... | collective-permute-start | bytes 1769480 | tf_op jit(solution)/shard_map/ppermute | solution.py:36
  56.7 6.9 %copy-start.6 = (bf16[1,128,2048]{2,1,0:T(8,128)(2,1)S(1)}, bf16[1,128,2048]{2,1,0:T(8,128)(2,1)}, u32[]{:S(2)}) copy-start(bf16[1,128,2048]{2,1,0:T(8,128)(2,1)} %param.7) | copy-start | bytes 1572868
  56.7 1.7 %collective-permute-start.22 = (bf16[80,2048]{1,0:T(8,128)(2,1)S(1)}, bf16[80,2048]{1,0:T(8,128)(2,1)S(1)}, u32[]{:S(2)}, u32[]{:S(2)}) collective-permute-start(bf16[80,2048]{1,0:T(8,128)(2,1)S(1)} %get-tuple-element.74), channel_id=1, source_target_pairs={{0,1},{1,0},{2,3},{3,2},{4,5},{5,4},{6,7},{7,6},{8,9},{9,8},{10,11... | collective-permute-start | bytes 983048 | tf_op jit(solution)/shard_map/ppermute | solution.py:36
  56.8 4.7 %collective-permute-start.1 = (bf16[80,2048]{1,0:T(8,128)(2,1)S(1)}, bf16[80,2048]{1,0:T(8,128)(2,1)S(1)}, u32[]{:S(2)}, u32[]{:S(2)}) collective-permute-start(bf16[80,2048]{1,0:T(8,128)(2,1)S(1)} %get-tuple-element.58), channel_id=1, source_target_pairs={{0,1},{1,0},{2,3},{3,2},{4,5},{5,4},{6,7},{7,6},{8,9},{9,8},{10,11... | collective-permute-start | bytes 983048 | tf_op jit(solution)/shard_map/ppermute | solution.py:36
  57.3 20.7 %collective-permute-start.25 = (bf16[144,2048]{1,0:T(8,128)(2,1)S(1)}, bf16[144,2048]{1,0:T(8,128)(2,1)S(1)}, u32[]{:S(2)}, u32[]{:S(2)}) collective-permute-start(bf16[144,2048]{1,0:T(8,128)(2,1)S(1)} %get-tuple-element.83), channel_id=1, source_target_pairs={{0,1},{1,0},{2,3},{3,2},{4,5},{5,4},{6,7},{7,6},{8,9},{9,8},{10,11... | collective-permute-start | bytes 1769480 | tf_op jit(solution)/shard_map/ppermute | solution.py:36
  58.9 9.2 %collective-permute-start.27 = (bf16[64,2048]{1,0:T(8,128)(2,1)S(1)}, bf16[64,2048]{1,0:T(8,128)(2,1)S(1)}, u32[]{:S(2)}, u32[]{:S(2)}) collective-permute-start(bf16[64,2048]{1,0:T(8,128)(2,1)S(1)} %get-tuple-element.84), channel_id=1, source_target_pairs={{0,2},{1,3},{4,0},{5,1},{8,4},{9,5},{12,8},{13,9},{14,12},{15,13},... | collective-permute-start | bytes 786440 | tf_op jit(solution)/shard_map/ppermute | solution.py:31
  60.5 9.2 %collective-permute-start.26 = (bf16[64,2048]{1,0:T(8,128)(2,1)S(1)}, bf16[64,2048]{1,0:T(8,128)(2,1)S(1)}, u32[]{:S(2)}, u32[]{:S(2)}) collective-permute-start(bf16[64,2048]{1,0:T(8,128)(2,1)S(1)} %get-tuple-element.77.refs_6_), channel_id=1, source_target_pairs={{0,4},{1,5},{4,8},{5,9},{8,12},{9,13},{12,14},{13,15},{14,10},{15,... | collective-permute-start | bytes 786440 | tf_op jit(solution)/shard_map/ppermute | solution.py:31
  61.5 12.2 %collective-permute-start.31 = (bf16[64,2048]{1,0:T(8,128)(2,1)S(1)}, bf16[64,2048]{1,0:T(8,128)(2,1)S(1)}, u32[]{:S(2)}, u32[]{:S(2)}) collective-permute-start(bf16[64,2048]{1,0:T(8,128)(2,1)S(1)} %get-tuple-element.87), channel_id=1, source_target_pairs={{0,2},{1,3},{4,0},{5,1},{8,4},{9,5},{12,8},{13,9},{14,12},{15,13},... | collective-permute-start | bytes 786440 | tf_op jit(solution)/shard_map/ppermute | solution.py:31
  63.1 12.2 %collective-permute-start.30 = (bf16[64,2048]{1,0:T(8,128)(2,1)S(1)}, bf16[64,2048]{1,0:T(8,128)(2,1)S(1)}, u32[]{:S(2)}, u32[]{:S(2)}) collective-permute-start(bf16[64,2048]{1,0:T(8,128)(2,1)S(1)} %get-tuple-element.78.refs_4_), channel_id=1, source_target_pairs={{0,4},{1,5},{4,8},{5,9},{8,12},{9,13},{12,14},{13,15},{14,10},{15,... | collective-permute-start | bytes 786440 | tf_op jit(solution)/shard_map/ppermute | solution.py:31
  70.2 9.3 %collective-permute-start.29 = (bf16[64,2048]{1,0:T(8,128)(2,1)S(1)}, bf16[64,2048]{1,0:T(8,128)(2,1)S(1)}, u32[]{:S(2)}, u32[]{:S(2)}) collective-permute-start(bf16[64,2048]{1,0:T(8,128)(2,1)S(1)} %get-tuple-element.86), channel_id=1, source_target_pairs={{0,2},{1,3},{4,0},{5,1},{8,4},{9,5},{12,8},{13,9},{14,12},{15,13},... | collective-permute-start | bytes 786440 | tf_op jit(solution)/shard_map/ppermute | solution.py:31
  70.8 10.1 %collective-permute-start.28 = (bf16[64,2048]{1,0:T(8,128)(2,1)S(1)}, bf16[64,2048]{1,0:T(8,128)(2,1)S(1)}, u32[]{:S(2)}, u32[]{:S(2)}) collective-permute-start(bf16[64,2048]{1,0:T(8,128)(2,1)S(1)} %get-tuple-element.85.refs_8_), channel_id=1, source_target_pairs={{0,4},{1,5},{4,8},{5,9},{8,12},{9,13},{12,14},{13,15},{14,10},{15,... | collective-permute-start | bytes 786440 | tf_op jit(solution)/shard_map/ppermute | solution.py:31
  75.9 9.3 %collective-permute-start.35 = (bf16[64,2048]{1,0:T(8,128)(2,1)S(1)}, bf16[64,2048]{1,0:T(8,128)(2,1)S(1)}, u32[]{:S(2)}, u32[]{:S(2)}) collective-permute-start(bf16[64,2048]{1,0:T(8,128)(2,1)S(1)} %get-tuple-element.91), channel_id=1, source_target_pairs={{0,2},{1,3},{4,0},{5,1},{8,4},{9,5},{12,8},{13,9},{14,12},{15,13},... | collective-permute-start | bytes 786440 | tf_op jit(solution)/shard_map/ppermute | solution.py:31
  76.4 10.1 %collective-permute-start.34 = (bf16[64,2048]{1,0:T(8,128)(2,1)S(1)}, bf16[64,2048]{1,0:T(8,128)(2,1)S(1)}, u32[]{:S(2)}, u32[]{:S(2)}) collective-permute-start(bf16[64,2048]{1,0:T(8,128)(2,1)S(1)} %get-tuple-element.88.refs_8_), channel_id=1, source_target_pairs={{0,4},{1,5},{4,8},{5,9},{8,12},{9,13},{12,14},{13,15},{14,10},{15,... | collective-permute-start | bytes 786440 | tf_op jit(solution)/shard_map/ppermute | solution.py:31
  81.5 9.3 %collective-permute-start.33 = (bf16[64,2048]{1,0:T(8,128)(2,1)S(1)}, bf16[64,2048]{1,0:T(8,128)(2,1)S(1)}, u32[]{:S(2)}, u32[]{:S(2)}) collective-permute-start(bf16[64,2048]{1,0:T(8,128)(2,1)S(1)} %get-tuple-element.90), channel_id=1, source_target_pairs={{0,2},{1,3},{4,0},{5,1},{8,4},{9,5},{12,8},{13,9},{14,12},{15,13},... | collective-permute-start | bytes 786440 | tf_op jit(solution)/shard_map/ppermute | solution.py:31
  82.1 10.1 %collective-permute-start.32 = (bf16[64,2048]{1,0:T(8,128)(2,1)S(1)}, bf16[64,2048]{1,0:T(8,128)(2,1)S(1)}, u32[]{:S(2)}, u32[]{:S(2)}) collective-permute-start(bf16[64,2048]{1,0:T(8,128)(2,1)S(1)} %get-tuple-element.89.refs_8_), channel_id=1, source_target_pairs={{0,4},{1,5},{4,8},{5,9},{8,12},{9,13},{12,14},{13,15},{14,10},{15,... | collective-permute-start | bytes 786440 | tf_op jit(solution)/shard_map/ppermute | solution.py:31
  87.1 9.3 %collective-permute-start.40 = (bf16[64,2048]{1,0:T(8,128)(2,1)S(1)}, bf16[64,2048]{1,0:T(8,128)(2,1)S(1)}, u32[]{:S(2)}, u32[]{:S(2)}) collective-permute-start(bf16[64,2048]{1,0:T(8,128)(2,1)S(1)} %get-tuple-element.96), channel_id=1, source_target_pairs={{0,2},{1,3},{4,0},{5,1},{8,4},{9,5},{12,8},{13,9},{14,12},{15,13},... | collective-permute-start | bytes 786440 | tf_op jit(solution)/shard_map/ppermute | solution.py:31
  87.7 10.1 %collective-permute-start.39 = (bf16[64,2048]{1,0:T(8,128)(2,1)S(1)}, bf16[64,2048]{1,0:T(8,128)(2,1)S(1)}, u32[]{:S(2)}, u32[]{:S(2)}) collective-permute-start(bf16[64,2048]{1,0:T(8,128)(2,1)S(1)} %get-tuple-element.92.refs_5_), channel_id=1, source_target_pairs={{0,4},{1,5},{4,8},{5,9},{8,12},{9,13},{12,14},{13,15},{14,10},{15,... | collective-permute-start | bytes 786440 | tf_op jit(solution)/shard_map/ppermute | solution.py:31
  92.6 7.7 %collective-permute-start.37 = (bf16[32,2048]{1,0:T(8,128)(2,1)S(1)}, bf16[32,2048]{1,0:T(8,128)(2,1)S(1)}, u32[]{:S(2)}, u32[]{:S(2)}) collective-permute-start(bf16[32,2048]{1,0:T(8,128)(2,1)S(1)} %get-tuple-element.94), channel_id=1, source_target_pairs={{0,2},{1,3},{4,0},{5,1},{8,4},{9,5},{12,8},{13,9},{14,12},{15,13},... | collective-permute-start | bytes 393224 | tf_op jit(solution)/shard_map/ppermute | solution.py:31
  93.1 7.1 %collective-permute-start.36 = (bf16[32,2048]{1,0:T(8,128)(2,1)S(1)}, bf16[32,2048]{1,0:T(8,128)(2,1)S(1)}, u32[]{:S(2)}, u32[]{:S(2)}) collective-permute-start(bf16[32,2048]{1,0:T(8,128)(2,1)S(1)} %get-tuple-element.93.refs_5_), channel_id=1, source_target_pairs={{0,4},{1,5},{4,8},{5,9},{8,12},{9,13},{12,14},{13,15},{14,10},{15,... | collective-permute-start | bytes 393224 | tf_op jit(solution)/shard_map/ppermute | solution.py:31
  98.2 5.0 %collective-permute-start.41 = (bf16[32,2048]{1,0:T(8,128)(2,1)S(1)}, bf16[32,2048]{1,0:T(8,128)(2,1)S(1)}, u32[]{:S(2)}, u32[]{:S(2)}) collective-permute-start(bf16[32,2048]{1,0:T(8,128)(2,1)S(1)} %get-tuple-element.97), channel_id=1, source_target_pairs={{0,4},{1,5},{4,8},{5,9},{8,12},{9,13},{12,14},{13,15},{14,10},{15,... | collective-permute-start | bytes 393224 | tf_op jit(solution)/shard_map/ppermute | solution.py:31
  98.8 5.0 %collective-permute-start.42 = (bf16[32,2048]{1,0:T(8,128)(2,1)S(1)}, bf16[32,2048]{1,0:T(8,128)(2,1)S(1)}, u32[]{:S(2)}, u32[]{:S(2)}) collective-permute-start(bf16[32,2048]{1,0:T(8,128)(2,1)S(1)} %get-tuple-element.98), channel_id=1, source_target_pairs={{0,2},{1,3},{4,0},{5,1},{8,4},{9,5},{12,8},{13,9},{14,12},{15,13},... | collective-permute-start | bytes 393224 | tf_op jit(solution)/shard_map/ppermute | solution.py:31
  100.3 9.3 %collective-permute-start.38 = (bf16[64,2048]{1,0:T(8,128)(2,1)S(1)}, bf16[64,2048]{1,0:T(8,128)(2,1)S(1)}, u32[]{:S(2)}, u32[]{:S(2)}) collective-permute-start(bf16[64,2048]{1,0:T(8,128)(2,1)S(1)} %final.2), channel_id=1, source_target_pairs={{0,16},{16,0},{1,17},{17,1},{2,18},{18,2},{3,19},{19,3},{4,20},{20... | collective-permute-start | bytes 786440 | tf_op jit(solution)/shard_map/ppermute | solution.py:41
  103.9 8.5 %collective-permute-start.43 = (bf16[64,2048]{1,0:T(8,128)(2,1)S(1)}, bf16[64,2048]{1,0:T(8,128)(2,1)S(1)}, u32[]{:S(2)}, u32[]{:S(2)}) collective-permute-start(bf16[64,2048]{1,0:T(8,128)(2,1)S(1)} %final.3), channel_id=1, source_target_pairs={{0,16},{16,0},{1,17},{17,1},{2,18},{18,2},{3,19},{19,3},{4,20},{20... | collective-permute-start | bytes 786440 | tf_op jit(solution)/shard_map/ppermute | solution.py:41
  (5 other events, 7.6 us)
